TPU v7x, 1024 devices: a whole 4x8x16 slice. The times are simulated.
1024 devices in a mesh: expert: 8 (over y_hi, core), tp: 128 (over y_lo, z, x).
Axes of the slice: x: 4, y: 8 (y_hi: 4, y_lo: 2; y = y_hi * 2 + y_lo), z: 16, core: 2. Of those that a mesh axis runs over, the one named last changes fastest.
Arguments:
- tokens: bfloat16 [512, 6144], P('expert', 'tp'), may hold values from -6 to 6
- routes: int32 [512, 2], P('expert'), may hold values from 0 to 7, all different within a row; in each aligned block of 64 rows (0 to 63, 64 to 127, ...) at most 32 rows name the same one
- w_gate: bfloat16 [8, 128, 1536, 4, 128], P('expert', 'tp'), may hold values from -0.078125 to 0.078125
- w_up: bfloat16 [8, 128, 1536, 4, 128], P('expert', 'tp'), may hold values from -0.078125 to 0.078125
- hidden_grad: bfloat16 [8, 256, 16384], P('expert', None, 'tp'), may hold values from -6 to 6
Outputs:
- token_grad: bfloat16 [512, 6144], P('expert', 'tp')
Inputs may be any that keep to these rules, and one draw needn't show every extreme that they name: `routes`: the two experts of a token differ; among the 64 tokens of one expert-axis index no expert is named more than 32 times, and some expert exactly that often.
All inputs are finite; a program needn't handle non-finite values.
Results may differ from a plain program's by a relative error of at most 0.0059.
Values may be sent and summed in bfloat16 or wider, within the bound.
No kernel may reach another device: no remote copies, remote signals or barrier semaphores. Data moves between devices by JAX's collectives and lax.ppermute only.
A program may use at most 32 MiB of HBM per device.

v0:
```python
import jax
import jax.numpy as jnp
from jax import lax
from jax.sharding import PartitionSpec as P

DG = 4


def swapped(shard, axis, stride):
    return lax.ppermute(shard, axis, [(i, i ^ 1 << stride) for i in range(lax.axis_size(axis))])


def pick_bit(position, bit):
    return jnp.bitwise_and(jnp.right_shift(position, bit), 1) == 0


def body(tokens, routes, w_gate, w_up, hidden_grad):
    n_groups = lax.axis_size("expert")
    tp_count = lax.axis_size("tp")
    position = lax.axis_index("tp")
    blocks_hidden = tp_count // DG
    low_bits = blocks_hidden.bit_length() - 1
    capacity = hidden_grad.shape[1] // n_groups
    slot_total = n_groups * capacity
    local_tokens = tokens.shape[0]
    features = tokens.shape[1]
    flat_routes = routes.reshape(local_tokens * 2)
    expert_iota = jnp.arange(n_groups, dtype=jnp.int32)
    one_hot = (flat_routes[:, None] == expert_iota[None, :]).astype(jnp.int32)
    before = jnp.cumsum(one_hot, axis=0) - one_hot
    slot_pos = jnp.sum(before * one_hot, axis=1)
    slot_index = flat_routes * capacity + slot_pos
    placing = (jnp.arange(slot_total, dtype=jnp.int32)[:, None] == slot_index[None, :]).astype(
        jnp.bfloat16
    )
    copies = jnp.repeat(tokens, 2, axis=0)
    outgoing = jnp.dot(placing, copies, preferred_element_type=jnp.float32).astype(jnp.bfloat16)
    outgoing = outgoing.reshape(n_groups, capacity, features)
    arrived = lax.all_to_all(outgoing, "expert", split_axis=0, concat_axis=0, tiled=True)
    rows = arrived.reshape(slot_total, features)
    block_rows = w_gate.shape[2]
    gate_weight = w_gate[0, 0].reshape(block_rows, -1)
    up_weight = w_up[0, 0].reshape(block_rows, -1)
    block = rows
    for bit in range(low_bits):
        partner = swapped(block, "tp", bit)
        first = pick_bit(position, bit)
        lower = jnp.where(first, block, partner)
        upper = jnp.where(first, partner, block)
        block = jnp.concatenate([lower, upper], axis=1)
    gate_pre = jnp.dot(block, gate_weight, preferred_element_type=jnp.float32)
    up_pre = jnp.dot(block, up_weight, preferred_element_type=jnp.float32)
    for step in range(2):
        bit = low_bits + 1 - step
        half = gate_pre.shape[1] // 2
        first = pick_bit(position, bit)
        keep_gate = jnp.where(first, gate_pre[:, :half], gate_pre[:, half:])
        keep_up = jnp.where(first, up_pre[:, :half], up_pre[:, half:])
        send_gate = jnp.where(first, gate_pre[:, half:], gate_pre[:, :half])
        send_up = jnp.where(first, up_pre[:, half:], up_pre[:, :half])
        got_gate, got_up = swapped((send_gate, send_up), "tp", bit)
        gate_pre = keep_gate + got_gate
        up_pre = keep_up + got_up
    sigmoid_gate = jax.nn.sigmoid(gate_pre)
    upstream = hidden_grad[0].astype(jnp.float32)
    gate_grad = (upstream * up_pre * sigmoid_gate * (1.0 + gate_pre * (1.0 - sigmoid_gate))).astype(
        jnp.bfloat16
    )
    up_grad = (upstream * gate_pre * sigmoid_gate).astype(jnp.bfloat16)
    for step in range(2):
        bit = low_bits + step
        other_gate, other_up = swapped((gate_grad, up_grad), "tp", bit)
        first = pick_bit(position, bit)
        gate_grad = jnp.concatenate(
            [jnp.where(first, gate_grad, other_gate), jnp.where(first, other_gate, gate_grad)],
            axis=1,
        )
        up_grad = jnp.concatenate(
            [jnp.where(first, up_grad, other_up), jnp.where(first, other_up, up_grad)], axis=1
        )
    dims = (((1,), (1,)), ((), ()))
    partial_sum = lax.dot_general(gate_grad, gate_weight, dims, preferred_element_type=jnp.float32)
    partial_sum = partial_sum + lax.dot_general(
        up_grad, up_weight, dims, preferred_element_type=jnp.float32
    )
    for step in range(low_bits):
        bit = low_bits - 1 - step
        half = partial_sum.shape[1] // 2
        first = pick_bit(position, bit)
        keep_part = jnp.where(first, partial_sum[:, :half], partial_sum[:, half:])
        send_part = jnp.where(first, partial_sum[:, half:], partial_sum[:, :half])
        partial_sum = keep_part + swapped(send_part, "tp", bit)
    slot_grad = partial_sum.astype(jnp.bfloat16).reshape(n_groups, capacity, features)
    returned = lax.all_to_all(slot_grad, "expert", split_axis=0, concat_axis=0, tiled=True).reshape(
        slot_total, features
    )
    per_pair = jnp.dot(placing.T, returned, preferred_element_type=jnp.float32)
    return jnp.sum(per_pair.reshape(local_tokens, 2, features), axis=1).astype(jnp.bfloat16)


def solution(mesh):
    placed = (
        P("expert", "tp"),
        P("expert", None),
        P("expert", "tp", None, None, None),
        P("expert", "tp", None, None, None),
        P("expert", None, "tp"),
    )
    return jax.shard_map(
        body, mesh=mesh, in_specs=placed, out_specs=P("expert", "tp"), check_vma=False
    )
```

profile of v0, /device:TPU:1, one launch (start us, length us, event | category | flops | bytes accessed | tf_op | source)
XLA Modules:
  0.0 285.8 jit_solution(15766345886235012842)
XLA Ops:
  0.0 0.8 copy.15
  1.0 0.2 reduce_window_sum.11
  1.2 0.2 select_reduce_fusion
  1.4 0.8 copy.16
  2.2 0.2 convolution_convert_fusion
  2.7 23.6 %all_to_all.10 = bf16[8,2,768]{2,1,0:T(2,128)(2,1)S(1)} all-to-all(bf16[8,2,768]{2,1,0:T(2,128)(2,1)S(1)} %reshape.63), channel_id=1, replica_groups=mesh['expert'=8,'tp'=128] {'expert'}, dimensions={0} | all-to-all | bytes 49152 | tf_op jit(solution)/shard_map/all_to_all | solution.py:39
  26.4 1.9 collective-permute-start
  28.3 3.1 %collective-permute-done = bf16[256,48]{1,0:T(8,128)(2,1)S(1)} collective-permute-done((bf16[256,48]{1,0:T(8,128)(2,1)S(1)}, bf16[256,48]{1,0:T(8,128)(2,1)S(1)}, u32[]{:S(2)}, u32[]{:S(2)}) %collective-permute-start) | collective-permute-done | bytes 24608 | tf_op jit(solution)/shard_map/ppermute | solution.py:10
  31.5 1.9 collective-permute-start.1
  33.4 4.6 %collective-permute-done.1 = bf16[256,96]{1,0:T(8,128)(2,1)S(1)} collective-permute-done((bf16[256,96]{1,0:T(8,128)(2,1)S(1)}, bf16[256,96]{1,0:T(8,128)(2,1)S(1)}, u32[]{:S(2)}, u32[]{:S(2)}) %collective-permute-start.1) | collective-permute-done | bytes 49184 | tf_op jit(solution)/shard_map/ppermute | solution.py:10
  38.2 1.9 collective-permute-start.2
  40.2 3.8 %collective-permute-done.2 = bf16[256,192]{1,0:T(8,128)(2,1)S(1)} collective-permute-done((bf16[256,192]{1,0:T(8,128)(2,1)S(1)}, bf16[256,192]{1,0:T(8,128)(2,1)S(1)}, u32[]{:S(2)}, u32[]{:S(2)}) %collective-permute-start.2) | collective-permute-done | bytes 98336 | tf_op jit(solution)/shard_map/ppermute | solution.py:10
  44.2 1.9 collective-permute-start.3
  46.2 7.2 %collective-permute-done.3 = bf16[256,384]{1,0:T(8,128)(2,1)S(1)} collective-permute-done((bf16[256,384]{1,0:T(8,128)(2,1)S(1)}, bf16[256,384]{1,0:T(8,128)(2,1)S(1)}, u32[]{:S(2)}, u32[]{:S(2)}) %collective-permute-start.3) | collective-permute-done | bytes 196640 | tf_op jit(solution)/shard_map/ppermute | solution.py:10
  53.6 5.3 %collective-permute-start.4 = (bf16[256,768]{1,0:T(8,128)(2,1)S(1)}, bf16[256,768]{1,0:T(8,128)(2,1)S(1)}, u32[]{:S(2)}, u32[]{:S(2)}) collective-permute-start(bf16[256,768]{1,0:T(8,128)(2,1)S(1)} %pad_maximum_fusion.3), channel_id=1, source_target_pairs={{0,16},{1,17},{2,18},{3,19},{4,20},{5,21},{6,22},{7,23},{8,24},{9,... | collective-permute-start | bytes 1179656 | tf_op jit(solution)/shard_map/ppermute | solution.py:10
  58.9 35.4 %collective-permute-done.4 = bf16[256,768]{1,0:T(8,128)(2,1)S(1)} collective-permute-done((bf16[256,768]{1,0:T(8,128)(2,1)S(1)}, bf16[256,768]{1,0:T(8,128)(2,1)S(1)}, u32[]{:S(2)}, u32[]{:S(2)}) %collective-permute-start.4) | collective-permute-done | bytes 393248 | tf_op jit(solution)/shard_map/ppermute | solution.py:10
  94.4 0.6 fusion.1
  95.1 1.9 collective-permute-start.7
  97.0 0.6 fusion.5
  97.6 3.5 %collective-permute-start.5 = (f32[256,256]{1,0:T(8,128)S(1)}, f32[256,256]{1,0:T(8,128)S(1)}, u32[]{:S(2)}, u32[]{:S(2)}) collective-permute-start(f32[256,256]{1,0:T(8,128)S(1)} %slice_select_fusion.4), channel_id=1, source_target_pairs={{0,64},{1,65},{2,66},{3,67},{4,68},{5,69},{6,70},{7,71},{8,72},{9,... | collective-permute-start | bytes 786440 | tf_op jit(solution)/shard_map/ppermute | solution.py:10
  101.1 3.2 %collective-permute-done.7 = f32[256,256]{1,0:T(8,128)S(1)} collective-permute-done((f32[256,256]{1,0:T(8,128)S(1)}, f32[256,256]{1,0:T(8,128)S(1)}, u32[]{:S(2)}, u32[]{:S(2)}) %collective-permute-start.7) | collective-permute-done | bytes 262176 | tf_op jit(solution)/shard_map/ppermute | solution.py:10
  104.4 12.5 %collective-permute-start.8 = (f32[256,128]{1,0:T(8,128)S(1)}, f32[256,128]{1,0:T(8,128)S(1)}, u32[]{:S(2)}, u32[]{:S(2)}) collective-permute-start(f32[256,128]{1,0:T(8,128)S(1)} %slice_select_fusion.7), channel_id=1, source_target_pairs={{0,32},{1,33},{2,34},{3,35},{4,36},{5,37},{6,38},{7,39},{8,40},{9,... | collective-permute-start | bytes 393224 | tf_op jit(solution)/shard_map/ppermute | solution.py:10
  117.0 5.5 %collective-permute-start.6 = (f32[256,128]{1,0:T(8,128)S(1)}, f32[256,128]{1,0:T(8,128)S(1)}, u32[]{:S(2)}, u32[]{:S(2)}) collective-permute-start(f32[256,128]{1,0:T(8,128)S(1)} %slice_select_fusion.8), channel_id=1, source_target_pairs={{0,32},{1,33},{2,34},{3,35},{4,36},{5,37},{6,38},{7,39},{8,40},{9,... | collective-permute-start | bytes 393224 | tf_op jit(solution)/shard_map/ppermute | solution.py:10
  122.6 10.6 %collective-permute-done.8 = f32[256,128]{1,0:T(8,128)S(1)} collective-permute-done((f32[256,128]{1,0:T(8,128)S(1)}, f32[256,128]{1,0:T(8,128)S(1)}, u32[]{:S(2)}, u32[]{:S(2)}) %collective-permute-start.8) | collective-permute-done | bytes 131104 | tf_op jit(solution)/shard_map/ppermute | solution.py:10
  133.1 4.3 %collective-permute-done.6 = f32[256,128]{1,0:T(8,128)S(1)} collective-permute-done((f32[256,128]{1,0:T(8,128)S(1)}, f32[256,128]{1,0:T(8,128)S(1)}, u32[]{:S(2)}, u32[]{:S(2)}) %collective-permute-start.6) | collective-permute-done | bytes 131104 | tf_op jit(solution)/shard_map/ppermute | solution.py:10
  137.5 3.4 %collective-permute-start.11 = (bf16[256,128]{1,0:T(8,128)(2,1)S(1)}, bf16[256,128]{1,0:T(8,128)(2,1)S(1)}, u32[]{:S(2)}, u32[]{:S(2)}) collective-permute-start(bf16[256,128]{1,0:T(8,128)(2,1)S(1)} %get-tuple-element.8), channel_id=1, source_target_pairs={{0,32},{1,33},{2,34},{3,35},{4,36},{5,37},{6,38},{7,39},{8,40},{9,... | collective-permute-start | bytes 196616 | tf_op jit(solution)/shard_map/ppermute | solution.py:10
  141.0 10.6 %collective-permute-start.9 = (bf16[256,128]{1,0:T(8,128)(2,1)S(1)}, bf16[256,128]{1,0:T(8,128)(2,1)S(1)}, u32[]{:S(2)}, u32[]{:S(2)}) collective-permute-start(bf16[256,128]{1,0:T(8,128)(2,1)S(1)} %get-tuple-element.7), channel_id=1, source_target_pairs={{0,32},{1,33},{2,34},{3,35},{4,36},{5,37},{6,38},{7,39},{8,40},{9,... | collective-permute-start | bytes 196616 | tf_op jit(solution)/shard_map/ppermute | solution.py:10
  151.5 2.2 collective-permute-done.11
  153.8 2.5 collective-permute-start.12
  156.4 2.7 collective-permute-start.10
  159.2 1.1 collective-permute-done.12
  160.4 0.6 fusion.3
  161.0 1.4 collective-permute-done.10
  162.4 0.6 convolution_add_fusion
  163.2 1.9 collective-permute-start.13
  165.1 64.0 %collective-permute-done.13 = f32[256,768]{1,0:T(8,128)S(1)} collective-permute-done((f32[256,768]{1,0:T(8,128)S(1)}, f32[256,768]{1,0:T(8,128)S(1)}, u32[]{:S(2)}, u32[]{:S(2)}) %collective-permute-start.13) | collective-permute-done | bytes 786464 | tf_op jit(solution)/shard_map/ppermute | solution.py:10
  229.3 1.9 collective-permute-start.14
  231.2 16.0 %collective-permute-done.14 = f32[256,384]{1,0:T(8,128)S(1)} collective-permute-done((f32[256,384]{1,0:T(8,128)S(1)}, f32[256,384]{1,0:T(8,128)S(1)}, u32[]{:S(2)}, u32[]{:S(2)}) %collective-permute-start.14) | collective-permute-done | bytes 393248 | tf_op jit(solution)/shard_map/ppermute | solution.py:10
  247.4 1.9 collective-permute-start.15
  249.3 7.4 %collective-permute-done.15 = f32[256,192]{1,0:T(8,128)S(1)} collective-permute-done((f32[256,192]{1,0:T(8,128)S(1)}, f32[256,192]{1,0:T(8,128)S(1)}, u32[]{:S(2)}, u32[]{:S(2)}) %collective-permute-start.15) | collective-permute-done | bytes 196640 | tf_op jit(solution)/shard_map/ppermute | solution.py:10
  256.9 4.7 %collective-permute-start.16 = (f32[256,96]{1,0:T(8,128)S(1)}, f32[256,96]{1,0:T(8,128)S(1)}, u32[]{:S(2)}, u32[]{:S(2)}) collective-permute-start(f32[256,96]{1,0:T(8,128)S(1)} %slice_select_fusion.6), channel_id=1, source_target_pairs={{0,2},{1,3},{2,0},{3,1},{4,6},{5,7},{6,4},{7,5},{8,10},{9,11},{10,... | collective-permute-start | bytes 294920 | tf_op jit(solution)/shard_map/ppermute | solution.py:10
  261.6 2.5 collective-permute-done.16
  264.4 3.1 %collective-permute-start.17 = (f32[256,48]{1,0:T(8,128)S(1)}, f32[256,48]{1,0:T(8,128)S(1)}, u32[]{:S(2)}, u32[]{:S(2)}) collective-permute-start(f32[256,48]{1,0:T(8,128)S(1)} %slice_select_fusion.5), channel_id=1, source_target_pairs={{0,1},{1,0},{2,3},{3,2},{4,5},{5,4},{6,7},{7,6},{8,9},{9,8},{10,11... | collective-permute-start | bytes 147464 | tf_op jit(solution)/shard_map/ppermute | solution.py:10
  267.5 2.6 collective-permute-done.17
  270.2 0.8 reshape.65
  270.9 6.9 %all-to-all-start.1 = ((bf16[8,2,768]{2,1,0:T(2,128)(2,1)}), bf16[8,2,768]{2,1,0:T(2,128)(2,1)S(1)}, u32[]{:S(2)}, u32[]{:S(2)}) async-start(bf16[8,2,768]{2,1,0:T(2,128)(2,1)} %reshape.65), calls=%async_computation.1 | async-start | bytes 49152 | tf_op jit(solution)/shard_map/all_to_all | solution.py:94
  277.9 7.0 %all-to-all-done.1 = bf16[8,2,768]{2,1,0:T(2,128)(2,1)S(1)} async-done(((bf16[8,2,768]{2,1,0:T(2,128)(2,1)}), bf16[8,2,768]{2,1,0:T(2,128)(2,1)S(1)}, u32[]{:S(2)}, u32[]{:S(2)}) %all-to-all-start.1) | async-done | bytes 24608 | tf_op jit(solution)/shard_map/all_to_all | solution.py:94
  285.0 0.8 convolution_reduce_fusion
  (50 shorter events, 3.3 us)
Async XLA Ops:
  26.4 5.0 %collective-permute-start = (bf16[256,48]{1,0:T(8,128)(2,1)S(1)}, bf16[256,48]{1,0:T(8,128)(2,1)S(1)}, u32[]{:S(2)}, u32[]{:S(2)}) collective-permute-start(bf16[256,48]{1,0:T(8,128)(2,1)S(1)} %bitcast.35), channel_id=1, source_target_pairs={{0,1},{1,0},{2,3},{3,2},{4,5},{5,4},{6,7},{7,6},{8,9},{9,8},{10,11... | collective-permute-start | bytes 73736 | tf_op jit(solution)/shard_map/ppermute | solution.py:10
  31.5 6.5 %collective-permute-start.1 = (bf16[256,96]{1,0:T(8,128)(2,1)S(1)}, bf16[256,96]{1,0:T(8,128)(2,1)S(1)}, u32[]{:S(2)}, u32[]{:S(2)}) collective-permute-start(bf16[256,96]{1,0:T(8,128)(2,1)S(1)} %pad_maximum_fusion.8), channel_id=1, source_target_pairs={{0,2},{1,3},{2,0},{3,1},{4,6},{5,7},{6,4},{7,5},{8,10},{9,11},{10,... | collective-permute-start | bytes 147464 | tf_op jit(solution)/shard_map/ppermute | solution.py:10
  38.2 5.7 %collective-permute-start.2 = (bf16[256,192]{1,0:T(8,128)(2,1)S(1)}, bf16[256,192]{1,0:T(8,128)(2,1)S(1)}, u32[]{:S(2)}, u32[]{:S(2)}) collective-permute-start(bf16[256,192]{1,0:T(8,128)(2,1)S(1)} %pad_maximum_fusion.5), channel_id=1, source_target_pairs={{0,4},{1,5},{2,6},{3,7},{4,0},{5,1},{6,2},{7,3},{8,12},{9,13},{10,... | collective-permute-start | bytes 294920 | tf_op jit(solution)/shard_map/ppermute | solution.py:10
  44.2 9.1 %collective-permute-start.3 = (bf16[256,384]{1,0:T(8,128)(2,1)S(1)}, bf16[256,384]{1,0:T(8,128)(2,1)S(1)}, u32[]{:S(2)}, u32[]{:S(2)}) collective-permute-start(bf16[256,384]{1,0:T(8,128)(2,1)S(1)} %pad_maximum_fusion.4), channel_id=1, source_target_pairs={{0,8},{1,9},{2,10},{3,11},{4,12},{5,13},{6,14},{7,15},{8,0},{9,1},... | collective-permute-start | bytes 589832 | tf_op jit(solution)/shard_map/ppermute | solution.py:10
  46.2 48.3 %copy-start = (bf16[1,1,1536,4,128]{4,3,2,1,0:T(4,128)(2,1)S(1)}, bf16[1,1,1536,4,128]{4,3,2,1,0:T(4,128)(2,1)}, u32[]{:S(2)}) copy-start(bf16[1,1,1536,4,128]{4,3,2,1,0:T(4,128)(2,1)} %param.7) | copy-start | bytes 4718596
  53.6 40.7 %collective-permute-start.4 = (bf16[256,768]{1,0:T(8,128)(2,1)S(1)}, bf16[256,768]{1,0:T(8,128)(2,1)S(1)}, u32[]{:S(2)}, u32[]{:S(2)}) collective-permute-start(bf16[256,768]{1,0:T(8,128)(2,1)S(1)} %pad_maximum_fusion.3), channel_id=1, source_target_pairs={{0,16},{1,17},{2,18},{3,19},{4,20},{5,21},{6,22},{7,23},{8,24},{9,... | collective-permute-start | bytes 1179656 | tf_op jit(solution)/shard_map/ppermute | solution.py:10
  94.4 2.6 copy-start.1
  95.1 9.3 %collective-permute-start.7 = (f32[256,256]{1,0:T(8,128)S(1)}, f32[256,256]{1,0:T(8,128)S(1)}, u32[]{:S(2)}, u32[]{:S(2)}) collective-permute-start(f32[256,256]{1,0:T(8,128)S(1)} %slice_select_fusion.3), channel_id=1, source_target_pairs={{0,64},{1,65},{2,66},{3,67},{4,68},{5,69},{6,70},{7,71},{8,72},{9,... | collective-permute-start | bytes 786440 | tf_op jit(solution)/shard_map/ppermute | solution.py:10
  97.6 39.8 %copy-start.2 = (bf16[1,256,128]{2,1,0:T(8,128)(2,1)S(1)}, bf16[1,256,128]{2,1,0:T(8,128)(2,1)}, u32[]{:S(2)}) copy-start(bf16[1,256,128]{2,1,0:T(8,128)(2,1)} %param.9) | copy-start | bytes 196612
  97.6 19.3 %collective-permute-start.5 = (f32[256,256]{1,0:T(8,128)S(1)}, f32[256,256]{1,0:T(8,128)S(1)}, u32[]{:S(2)}, u32[]{:S(2)}) collective-permute-start(f32[256,256]{1,0:T(8,128)S(1)} %slice_select_fusion.4), channel_id=1, source_target_pairs={{0,64},{1,65},{2,66},{3,67},{4,68},{5,69},{6,70},{7,71},{8,72},{9,... | collective-permute-start | bytes 786440 | tf_op jit(solution)/shard_map/ppermute | solution.py:10
  104.4 28.7 %collective-permute-start.8 = (f32[256,128]{1,0:T(8,128)S(1)}, f32[256,128]{1,0:T(8,128)S(1)}, u32[]{:S(2)}, u32[]{:S(2)}) collective-permute-start(f32[256,128]{1,0:T(8,128)S(1)} %slice_select_fusion.7), channel_id=1, source_target_pairs={{0,32},{1,33},{2,34},{3,35},{4,36},{5,37},{6,38},{7,39},{8,40},{9,... | collective-permute-start | bytes 393224 | tf_op jit(solution)/shard_map/ppermute | solution.py:10
  117.0 20.4 %collective-permute-start.6 = (f32[256,128]{1,0:T(8,128)S(1)}, f32[256,128]{1,0:T(8,128)S(1)}, u32[]{:S(2)}, u32[]{:S(2)}) collective-permute-start(f32[256,128]{1,0:T(8,128)S(1)} %slice_select_fusion.8), channel_id=1, source_target_pairs={{0,32},{1,33},{2,34},{3,35},{4,36},{5,37},{6,38},{7,39},{8,40},{9,... | collective-permute-start | bytes 393224 | tf_op jit(solution)/shard_map/ppermute | solution.py:10
  137.5 16.3 %collective-permute-start.11 = (bf16[256,128]{1,0:T(8,128)(2,1)S(1)}, bf16[256,128]{1,0:T(8,128)(2,1)S(1)}, u32[]{:S(2)}, u32[]{:S(2)}) collective-permute-start(bf16[256,128]{1,0:T(8,128)(2,1)S(1)} %get-tuple-element.8), channel_id=1, source_target_pairs={{0,32},{1,33},{2,34},{3,35},{4,36},{5,37},{6,38},{7,39},{8,40},{9,... | collective-permute-start | bytes 196616 | tf_op jit(solution)/shard_map/ppermute | solution.py:10
  141.0 15.4 %collective-permute-start.9 = (bf16[256,128]{1,0:T(8,128)(2,1)S(1)}, bf16[256,128]{1,0:T(8,128)(2,1)S(1)}, u32[]{:S(2)}, u32[]{:S(2)}) collective-permute-start(bf16[256,128]{1,0:T(8,128)(2,1)S(1)} %get-tuple-element.7), channel_id=1, source_target_pairs={{0,32},{1,33},{2,34},{3,35},{4,36},{5,37},{6,38},{7,39},{8,40},{9,... | collective-permute-start | bytes 196616 | tf_op jit(solution)/shard_map/ppermute | solution.py:10
  153.8 6.5 %collective-permute-start.12 = (bf16[256,256]{1,0:T(8,128)(2,1)S(1)}, bf16[256,256]{1,0:T(8,128)(2,1)S(1)}, u32[]{:S(2)}, u32[]{:S(2)}) collective-permute-start(bf16[256,256]{1,0:T(8,128)(2,1)S(1)} %pad_maximum_fusion.7), channel_id=1, source_target_pairs={{0,64},{1,65},{2,66},{3,67},{4,68},{5,69},{6,70},{7,71},{8,72},{9,... | collective-permute-start | bytes 393224 | tf_op jit(solution)/shard_map/ppermute | solution.py:10
  156.4 5.9 %collective-permute-start.10 = (bf16[256,256]{1,0:T(8,128)(2,1)S(1)}, bf16[256,256]{1,0:T(8,128)(2,1)S(1)}, u32[]{:S(2)}, u32[]{:S(2)}) collective-permute-start(bf16[256,256]{1,0:T(8,128)(2,1)S(1)} %pad_maximum_fusion.6), channel_id=1, source_target_pairs={{0,64},{1,65},{2,66},{3,67},{4,68},{5,69},{6,70},{7,71},{8,72},{9,... | collective-permute-start | bytes 393224 | tf_op jit(solution)/shard_map/ppermute | solution.py:10
  163.2 65.9 %collective-permute-start.13 = (f32[256,768]{1,0:T(8,128)S(1)}, f32[256,768]{1,0:T(8,128)S(1)}, u32[]{:S(2)}, u32[]{:S(2)}) collective-permute-start(f32[256,768]{1,0:T(8,128)S(1)} %slice_select_fusion), channel_id=1, source_target_pairs={{0,16},{1,17},{2,18},{3,19},{4,20},{5,21},{6,22},{7,23},{8,24},{9,... | collective-permute-start | bytes 2359304 | tf_op jit(solution)/shard_map/ppermute | solution.py:10
  229.3 17.9 %collective-permute-start.14 = (f32[256,384]{1,0:T(8,128)S(1)}, f32[256,384]{1,0:T(8,128)S(1)}, u32[]{:S(2)}, u32[]{:S(2)}) collective-permute-start(f32[256,384]{1,0:T(8,128)S(1)} %slice_select_fusion.1), channel_id=1, source_target_pairs={{0,8},{1,9},{2,10},{3,11},{4,12},{5,13},{6,14},{7,15},{8,0},{9,1},... | collective-permute-start | bytes 1179656 | tf_op jit(solution)/shard_map/ppermute | solution.py:10
  247.4 9.3 %collective-permute-start.15 = (f32[256,192]{1,0:T(8,128)S(1)}, f32[256,192]{1,0:T(8,128)S(1)}, u32[]{:S(2)}, u32[]{:S(2)}) collective-permute-start(f32[256,192]{1,0:T(8,128)S(1)} %slice_select_fusion.2), channel_id=1, source_target_pairs={{0,4},{1,5},{2,6},{3,7},{4,0},{5,1},{6,2},{7,3},{8,12},{9,13},{10,... | collective-permute-start | bytes 589832 | tf_op jit(solution)/shard_map/ppermute | solution.py:10
  256.9 7.2 %collective-permute-start.16 = (f32[256,96]{1,0:T(8,128)S(1)}, f32[256,96]{1,0:T(8,128)S(1)}, u32[]{:S(2)}, u32[]{:S(2)}) collective-permute-start(f32[256,96]{1,0:T(8,128)S(1)} %slice_select_fusion.6), channel_id=1, source_target_pairs={{0,2},{1,3},{2,0},{3,1},{4,6},{5,7},{6,4},{7,5},{8,10},{9,11},{10,... | collective-permute-start | bytes 294920 | tf_op jit(solution)/shard_map/ppermute | solution.py:10
  264.4 5.7 %collective-permute-start.17 = (f32[256,48]{1,0:T(8,128)S(1)}, f32[256,48]{1,0:T(8,128)S(1)}, u32[]{:S(2)}, u32[]{:S(2)}) collective-permute-start(f32[256,48]{1,0:T(8,128)S(1)} %slice_select_fusion.5), channel_id=1, source_target_pairs={{0,1},{1,0},{2,3},{3,2},{4,5},{5,4},{6,7},{7,6},{8,9},{9,8},{10,11... | collective-permute-start | bytes 147464 | tf_op jit(solution)/shard_map/ppermute | solution.py:10
  270.9 14.0 %all-to-all-start.1 = ((bf16[8,2,768]{2,1,0:T(2,128)(2,1)}), bf16[8,2,768]{2,1,0:T(2,128)(2,1)S(1)}, u32[]{:S(2)}, u32[]{:S(2)}) async-start(bf16[8,2,768]{2,1,0:T(2,128)(2,1)} %reshape.65), calls=%async_computation.1 | async-start | bytes 49152 | tf_op jit(solution)/shard_map/all_to_all | solution.py:94
where the time goes:
time: 287 us; the launch traced here: 286 us
  waiting for transfers between devices  176 us (61%)
  starting transfers between devices  76.2 us (27%)
  blocking collectives  23.6 us (8%)
  matrix products  3.38 us (1%)
  local copies, waits for them, and re-layouts  3.02 us (1%)
  other arithmetic  2.91 us (1%)
    ppermute x18, waiting for transfers between devices, swapped(): lax.ppermute(shard, axis, [(i, i ^ 1 << stride) for i in range(lax.axis_s...  169 us
    ppermute x18, starting transfers between devices, swapped(): lax.ppermute(shard, axis, [(i, i ^ 1 << stride) for i in range(lax.axis_s...  69.3 us
    all_to_all x1, blocking collectives, body(): lax.all_to_all(outgoing, 'expert', split_axis=0, concat_axis=0, tiled=True)  23.6 us
    all_to_all x1, waiting for transfers between devices, body(): lax.all_to_all(slot_grad, 'expert', split_axis=0, concat_axis=0, tiled=True)  6.98 us
    all_to_all x1, starting transfers between devices, body(): lax.all_to_all(slot_grad, 'expert', split_axis=0, concat_axis=0, tiled=True)  6.86 us
  transfers between devices with their start and end apart: 19, of which 17 were waited for; matrix products, arithmetic and copies ran while one was open for 1% of the time, Pallas kernels for 0%

commit v1 on v0

v1 whole, which is shorter than its diff:
```python
import jax
import jax.numpy as jnp
from jax import lax
from jax.sharding import PartitionSpec as P

NX, NZL = 4, 8
X_GROUPS = [[b * NX + x for x in range(NX)] for b in range(32)]
ZL_GROUPS = [
    [hi * 32 + zl * NX + x for zl in range(NZL)] for hi in range(4) for x in range(NX)
]
Y_BIT, ZH_BIT = 64, 32


def swapped(shard, bit):
    return lax.ppermute(shard, "tp", [(i, i ^ bit) for i in range(lax.axis_size("tp"))])


def body(tokens, routes, w_gate, w_up, hidden_grad):
    f32, bf16 = jnp.float32, jnp.bfloat16
    position = lax.axis_index("tp")
    is_y0 = jnp.bitwise_and(position, Y_BIT) == 0
    is_zh0 = jnp.bitwise_and(position, ZH_BIT) == 0
    n_groups = lax.axis_size("expert")
    slot_total = hidden_grad.shape[1]
    capacity = slot_total // n_groups
    n_tok, feat = tokens.shape
    block_rows = w_gate.shape[2]
    hid = w_gate.shape[4]
    wide = NZL * feat

    turned = tokens.T
    packed = jnp.concatenate([turned[: feat // 2], turned[feat // 2 :]], axis=1)
    raw = lax.all_to_all(
        jnp.broadcast_to(packed[None], (NZL,) + packed.shape),
        "tp",
        split_axis=0,
        concat_axis=0,
        axis_index_groups=ZL_GROUPS,
        tiled=True,
    )
    raw = jnp.concatenate([raw[:, :, :n_tok], raw[:, :, n_tok:]], axis=1).reshape(wide, n_tok)

    flat_routes = routes.reshape(n_tok * 2)
    one_hot = (flat_routes[:, None] == jnp.arange(n_groups, dtype=jnp.int32)[None, :]).astype(jnp.int32)
    before = jnp.cumsum(one_hot, axis=0) - one_hot
    slot_index = (flat_routes * capacity + jnp.sum(before * one_hot, axis=1)).reshape(n_tok, 2)
    slots = jnp.arange(slot_total, dtype=jnp.int32)[:, None]
    placing = ((slots == slot_index[None, :, 0]) | (slots == slot_index[None, :, 1])).astype(bf16)

    outgoing = lax.dot_general(
        placing, raw, (((1,), (1,)), ((), ())), preferred_element_type=f32
    ).astype(bf16)
    arrived = lax.all_to_all(outgoing, "expert", split_axis=0, concat_axis=0, tiled=True)
    rows = lax.all_gather(arrived, "tp", axis_index_groups=X_GROUPS, axis=0, tiled=False)
    rows = rows.transpose(1, 0, 2).reshape(slot_total, block_rows)

    both = jnp.stack([w_gate[0, 0], w_up[0, 0]])
    both = both.reshape(2, NZL, NX, feat, 2, 2, hid)
    both = both.transpose(2, 1, 3, 4, 0, 5, 6).reshape(block_rows, 8 * hid)

    pre = jnp.dot(rows, both, preferred_element_type=f32)
    half = 4 * hid
    keep = jnp.where(is_y0, pre[:, :half], pre[:, half:])
    send = jnp.where(is_y0, pre[:, half:], pre[:, :half]).astype(bf16)
    hidden, send = lax.optimization_barrier((hidden_grad[0], send))
    got = swapped(send, Y_BIT)
    hidden_other = swapped(hidden, ZH_BIT)
    keep = keep + got.astype(f32)
    keep = keep + swapped(keep.astype(bf16), ZH_BIT).astype(f32)

    upstream = jnp.concatenate(
        [jnp.where(is_zh0, hidden, hidden_other), jnp.where(is_zh0, hidden_other, hidden)], axis=1
    ).astype(f32)
    gate_pre, up_pre = keep[:, : 2 * hid], keep[:, 2 * hid :]
    sigmoid_gate = jax.nn.sigmoid(gate_pre)
    gate_grad = upstream * up_pre * sigmoid_gate * (1.0 + gate_pre * (1.0 - sigmoid_gate))
    up_grad = upstream * gate_pre * sigmoid_gate
    grads = jnp.concatenate([gate_grad.astype(bf16), up_grad.astype(bf16)], axis=1)
    other = swapped(grads, Y_BIT)
    grads = jnp.concatenate([jnp.where(is_y0, grads, other), jnp.where(is_y0, other, grads)], axis=1)

    partial_sum = lax.dot_general(
        grads, both, (((1,), (1,)), ((), ())), preferred_element_type=f32
    ).astype(bf16)
    pieces = partial_sum.reshape(slot_total, NX, wide).transpose(1, 0, 2)
    pieces = lax.all_to_all(
        pieces, "tp", split_axis=0, concat_axis=0, axis_index_groups=X_GROUPS, tiled=True
    )
    summed = jnp.sum(pieces.astype(f32), axis=0).astype(bf16)
    returned = lax.all_to_all(summed, "expert", split_axis=0, concat_axis=0, tiled=True)

    token_part = lax.dot_general(
        returned, placing, (((0,), (0,)), ((), ())), preferred_element_type=f32
    ).reshape(NZL, feat, n_tok)
    token_part = jnp.concatenate([token_part[:, : feat // 2], token_part[:, feat // 2 :]], axis=2)
    token_part = lax.all_to_all(
        token_part, "tp", split_axis=0, concat_axis=0, axis_index_groups=ZL_GROUPS, tiled=True
    )
    total = jnp.sum(token_part, axis=0)
    total = jnp.concatenate([total[:, :n_tok], total[:, n_tok:]], axis=0)
    return total.T.astype(bf16)


def solution(mesh):
    placed = (
        P("expert", "tp"),
        P("expert", None),
        P("expert", "tp", None, None, None),
        P("expert", "tp", None, None, None),
        P("expert", None, "tp"),
    )
    return jax.shard_map(
        body, mesh=mesh, in_specs=placed, out_specs=P("expert", "tp"), check_vma=False
    )
```

time: 287 us -> 168 us (0.59)
  waiting for transfers between devices: 176 us -> 38.6 us
  blocking collectives: 23.6 us -> 58.8 us
  starting transfers between devices: 76.2 us -> 47.6 us
  other arithmetic: 2.91 us -> 8.9 us
  local copies, waits for them, and re-layouts: 3.02 us -> 7.04 us
    ppermute x18 -> x4, waiting for transfers between devices: 169 us -> 31.2 us  [swapped(): lax.ppermute(shard, 'tp', [(i, i ^ bit) for i in range(lax.axis_size('tp'...]
    ppermute x18 -> x4, starting transfers between devices: 69.3 us -> 22.2 us  [swapped(): lax.ppermute(shard, 'tp', [(i, i ^ bit) for i in range(lax.axis_size('tp'...]
    all_to_all x1 -> x3, blocking collectives: 23.6 us -> 46.8 us  [the longest x1 22.2 us: body(): lax.all_to_all(summed, 'expert', split_axis=0, concat_axis=0, tiled=True)]
    all_to_all x1 -> x2, starting transfers between devices: 6.86 us -> 25.4 us  [the longest x1 16.3 us: body(): lax.all_to_all(jnp.broadcast_to(packed[None], (NZL,) + packed.shape), 'tp...]
    all_gather x0 -> x1, blocking collectives: none -> 12 us  [body(): lax.all_gather(arrived, 'tp', axis_index_groups=X_GROUPS, axis=0, tiled=F...]
    transpose x0 -> x1, other arithmetic: none -> 6.21 us  [body(): both = both.transpose(2, 1, 3, 4, 0, 5, 6).reshape(block_rows, 8 * hid)]
    reshape x2, local copies, waits for them, and re-layouts: 0.25 us -> 3.97 us  [the longest x1 3.89 us: body(): both = both.transpose(2, 1, 3, 4, 0, 5, 6).reshape(block_rows, 8 * hid)]
    all_to_all x1 -> x2, waiting for transfers between devices: 6.98 us -> 7.37 us  [the longest x1 7.37 us: body(): lax.all_to_all(jnp.broadcast_to(packed[None], (NZL,) + packed.shape), 'tp...]
  transfers between devices with their start and end apart: 19 -> 6, of which waited for: 17 -> 3; matrix products, arithmetic and copies ran while one was open for 1% -> 8% of each run, Pallas kernels for 0% -> 0%
where the time goes in v1:
time: 168 us; the launch traced here: 166 us
  blocking collectives  58.8 us (35%)
  starting transfers between devices  47.6 us (28%)
  waiting for transfers between devices  38.6 us (23%)
  other arithmetic  8.9 us (5%)
  local copies, waits for them, and re-layouts  7.04 us (4%)
  matrix products  5.2 us (3%)
    ppermute x4, waiting for transfers between devices, swapped(): lax.ppermute(shard, 'tp', [(i, i ^ bit) for i in range(lax.axis_size('tp'...  31.2 us
    all_to_all x1, blocking collectives, body(): lax.all_to_all(summed, 'expert', split_axis=0, concat_axis=0, tiled=True)  22.2 us
    ppermute x4, starting transfers between devices, swapped(): lax.ppermute(shard, 'tp', [(i, i ^ bit) for i in range(lax.axis_size('tp'...  22.2 us
    all_to_all x1, starting transfers between devices, body(): lax.all_to_all(jnp.broadcast_to(packed[None], (NZL,) + packed.shape), 'tp...  16.3 us
    all_to_all x1, blocking collectives, body(): lax.all_to_all(token_part, 'tp', split_axis=0, concat_axis=0, axis_index_...  13.7 us
    all_gather x1, blocking collectives, body(): lax.all_gather(arrived, 'tp', axis_index_groups=X_GROUPS, axis=0, tiled=F...  12 us
    all_to_all x1, blocking collectives, body(): lax.all_to_all(pieces, 'tp', split_axis=0, concat_axis=0, axis_index_grou...  10.9 us
    all_to_all x1, starting transfers between devices, body(): lax.all_to_all(outgoing, 'expert', split_axis=0, concat_axis=0, tiled=True)  9.17 us
  transfers between devices with their start and end apart: 6, of which 3 were waited for; matrix products, arithmetic and copies ran while one was open for 8% of the time, Pallas kernels for 0%

profile of v1, /device:TPU:1, one launch (start us, length us, event | category | flops | bytes accessed | tf_op | source)
XLA Modules:
  0.0 166.4 jit_solution(8110671653805305873)
XLA Ops:
  0.0 0.7 fusion.23
  0.7 0.1 pad_maximum_fusion.5
  0.8 0.6 broadcast_in_dim.2
  1.4 16.3 %all-to-all-start = ((bf16[8,24,128]{2,1,0:T(8,128)(2,1)}), bf16[8,24,128]{2,1,0:T(8,128)(2,1)S(1)}, u32[]{:S(2)}, u32[]{:S(2)}) async-start(bf16[8,24,128]{2,1,0:T(8,128)(2,1)} %broadcast_in_dim.2), calls=%async_computation | async-start | bytes 98304 | tf_op jit(solution)/shard_map/all_to_all | solution.py:33
  17.7 0.8 copy.31
  18.4 0.1 eq.54
  18.6 0.1 fusion.8
  18.7 0.2 reduce_window_sum.11
  18.8 0.2 select_reduce_fusion
  19.0 0.1 reduce_sum.33
  19.2 0.1 copy.32
  19.2 0.7 multiply_add_fusion
  20.0 7.4 %all-to-all-done = bf16[8,24,128]{2,1,0:T(8,128)(2,1)S(1)} async-done(((bf16[8,24,128]{2,1,0:T(8,128)(2,1)}), bf16[8,24,128]{2,1,0:T(8,128)(2,1)S(1)}, u32[]{:S(2)}, u32[]{:S(2)}) %all-to-all-start) | async-done | bytes 49184 | tf_op jit(solution)/shard_map/all_to_all | solution.py:33
  27.3 0.1 fusion.22
  27.4 1.0 convolution_convert_fusion.1
  28.4 9.2 %all-to-all-start.1 = ((bf16[8,32,384]{2,1,0:T(8,128)(2,1)}), bf16[8,32,384]{2,1,0:T(8,128)(2,1)S(1)}, u32[]{:S(2)}, u32[]{:S(2)}) async-start(bf16[8,32,384]{2,1,0:T(8,128)(2,1)} %bitcast.5), calls=%async_computation.1 | async-start | bytes 393216 | tf_op jit(solution)/shard_map/all_to_all | solution.py:53
  37.6 6.2 %copy_bitcast_fusion = bf16[4,8,48,2,2,2,128]{6,5,4,3,2,1,0:T(2,128)(2,1)S(1)} fusion(bf16[1,8,4,48,2,2,128]{6,5,4,3,2,1,0:T(2,128)(2,1)} %bitcast.39, bf16[1,8,4,48,2,2,128]{6,5,4,3,2,1,0:T(2,128)(2,1)} %bitcast.40), kind=kLoop, calls=%fused_computation.1 | loop fusion | flops 1572864 | bytes 6291456 | tf_op jit(solution)/shard_map/transpose | solution.py:59
  43.8 3.9 %reshape.33 = bf16[1536,1024]{1,0:T(8,128)(2,1)} reshape(bf16[4,8,48,2,2,2,128]{6,5,4,3,2,1,0:T(2,128)(2,1)S(1)} %copy_bitcast_fusion) | data formatting | bytes 6291456 | tf_op jit(solution)/shard_map/reshape | solution.py:59
  47.7 0.0 all-to-all-done.1
  47.7 12.0 %all_gather.7 = bf16[4,256,384]{2,1,0:T(8,128)(2,1)S(1)} all-gather(bf16[1,256,384]{2,1,0:T(8,128)(2,1)S(1)} %bitcast.46), channel_id=1, replica_groups={{0,1,2,3},{4,5,6,7},{8,9,10,11},{12,13,14,15},{16,17,18,19},{20,21,22,2..., dimensions={0}, use_global_device_ids=true | all-gather | bytes 983040 | tf_op jit(solution)/shard_map/all_gather | solution.py:54
  59.7 0.3 copy.33
  60.0 0.0 copy-start.1
  60.0 2.9 %fusion.25 = f32[256,1024]{1,0:T(8,128)S(1)} fusion(bf16[256,1536]{0,1:T(8,128)(2,1)S(1)} %bitcast.43, bf16[1536,1024]{1,0:T(8,128)(2,1)} %reshape.33), kind=kOutput, calls=%fused_computation.51 | convolution fusion | flops 805306368 | bytes 4980736 | tf_op jit(solution)/shard_map/dot_general | solution.py:61
  63.0 0.1 select_convert_fusion
  63.0 2.8 %collective-permute-start.1 = (bf16[256,512]{1,0:T(8,128)(2,1)S(1)}, bf16[256,512]{1,0:T(8,128)(2,1)S(1)}, u32[]{:S(2)}, u32[]{:S(2)}) collective-permute-start(bf16[256,512]{1,0:T(8,128)(2,1)S(1)} %select_convert_fusion), channel_id=1, source_target_pairs={{0,64},{1,65},{2,66},{3,67},{4,68},{5,69},{6,70},{7,71},{8,72},{9,... | collective-permute-start | bytes 786440 | tf_op jit(solution)/shard_map/ppermute | solution.py:15
  65.8 0.0 copy-done.1
  65.8 11.6 %collective-permute-start = (bf16[256,128]{1,0:T(8,128)(2,1)S(1)}, bf16[256,128]{1,0:T(8,128)(2,1)S(1)}, u32[]{:S(2)}, u32[]{:S(2)}) collective-permute-start(bf16[256,128]{1,0:T(8,128)(2,1)S(1)} %bitcast.48), channel_id=1, source_target_pairs={{0,32},{1,33},{2,34},{3,35},{4,36},{5,37},{6,38},{7,39},{8,40},{9,... | collective-permute-start | bytes 196616 | tf_op jit(solution)/shard_map/ppermute | solution.py:15
  77.4 0.0 collective-permute-done.1
  77.4 0.1 fusion.19
  77.6 4.6 %collective-permute-start.2 = (bf16[256,512]{1,0:T(8,128)(2,1)S(1)}, bf16[256,512]{1,0:T(8,128)(2,1)S(1)}, u32[]{:S(2)}, u32[]{:S(2)}) collective-permute-start(bf16[256,512]{1,0:T(8,128)(2,1)S(1)} %fusion.19), channel_id=1, source_target_pairs={{0,32},{1,33},{2,34},{3,35},{4,36},{5,37},{6,38},{7,39},{8,40},{9,... | collective-permute-start | bytes 786440 | tf_op jit(solution)/shard_map/ppermute | solution.py:15
  82.2 0.0 collective-permute-done
  82.2 27.3 %collective-permute-done.2 = bf16[256,512]{1,0:T(8,128)(2,1)S(1)} collective-permute-done((bf16[256,512]{1,0:T(8,128)(2,1)S(1)}, bf16[256,512]{1,0:T(8,128)(2,1)S(1)}, u32[]{:S(2)}, u32[]{:S(2)}) %collective-permute-start.2) | collective-permute-done | bytes 262176 | tf_op jit(solution)/shard_map/ppermute | solution.py:15
  109.5 0.1 convert_add_fusion
  109.7 0.1 fusion.5
  109.9 3.2 %collective-permute-start.3 = (bf16[256,512]{1,0:T(8,128)(2,1)S(1)}, bf16[256,512]{1,0:T(8,128)(2,1)S(1)}, u32[]{:S(2)}, u32[]{:S(2)}) collective-permute-start(bf16[256,512]{1,0:T(8,128)(2,1)S(1)} %pad_maximum_fusion.1), channel_id=1, source_target_pairs={{0,64},{1,65},{2,66},{3,67},{4,68},{5,69},{6,70},{7,71},{8,72},{9,... | collective-permute-start | bytes 786440 | tf_op jit(solution)/shard_map/ppermute | solution.py:15
  113.1 3.9 %collective-permute-done.3 = bf16[256,512]{1,0:T(8,128)(2,1)S(1)} collective-permute-done((bf16[256,512]{1,0:T(8,128)(2,1)S(1)}, bf16[256,512]{1,0:T(8,128)(2,1)S(1)}, u32[]{:S(2)}, u32[]{:S(2)}) %collective-permute-start.3) | collective-permute-done | bytes 262176 | tf_op jit(solution)/shard_map/ppermute | solution.py:15
  117.0 0.1 broadcast_select_fusion.1
  117.1 1.0 convolution_convert_fusion
  118.1 0.1 copy.42
  118.2 10.9 %all_to_all.36 = bf16[4,256,384]{2,1,0:T(8,128)(2,1)S(1)} all-to-all(bf16[4,256,384]{2,1,0:T(8,128)(2,1)S(1)} %bitcast.38), channel_id=1, replica_groups={{0,1,2,3},{4,5,6,7},{8,9,10,11},{12,13,14,15},{16,17,18,19},{20,21,22,2..., dimensions={0} | all-to-all | bytes 1572864 | tf_op jit(solution)/shard_map/all_to_all | solution.py:86
  129.1 0.2 reduce_sum.34
  129.2 22.2 %all_to_all.37 = bf16[8,32,384]{2,1,0:T(8,128)(2,1)S(1)} all-to-all(bf16[8,32,384]{2,1,0:T(8,128)(2,1)S(1)} %bitcast.41), channel_id=1, replica_groups=mesh['expert'=8,'tp'=128] {'expert'}, dimensions={0} | all-to-all | bytes 393216 | tf_op jit(solution)/shard_map/all_to_all | solution.py:90
  151.4 0.1 copy.37
  151.6 0.3 fusion.10
  151.9 0.1 pad_maximum_fusion.4
  152.0 13.7 %all_to_all.38 = f32[8,24,128]{2,1,0:T(8,128)S(1)} all-to-all(f32[8,24,128]{2,1,0:T(8,128)S(1)} %pad_maximum_fusion.4), channel_id=1, replica_groups={{0,4,8,12,16,20,24,28},{1,5,9,13,17,21,25,29},{2,6,10,14,18,22,26,30},{..., dimensions={0} | all-to-all | bytes 196608 | tf_op jit(solution)/shard_map/all_to_all | solution.py:96
  165.7 0.1 fusion.24
  165.8 0.6 maximum_bitcast_fusion
  (8 shorter events, 0.1 us)
Async XLA Ops:
  1.4 25.9 %all-to-all-start = ((bf16[8,24,128]{2,1,0:T(8,128)(2,1)}), bf16[8,24,128]{2,1,0:T(8,128)(2,1)S(1)}, u32[]{:S(2)}, u32[]{:S(2)}) async-start(bf16[8,24,128]{2,1,0:T(8,128)(2,1)} %broadcast_in_dim.2), calls=%async_computation | async-start | bytes 98304 | tf_op jit(solution)/shard_map/all_to_all | solution.py:33
  28.4 19.3 %all-to-all-start.1 = ((bf16[8,32,384]{2,1,0:T(8,128)(2,1)}), bf16[8,32,384]{2,1,0:T(8,128)(2,1)S(1)}, u32[]{:S(2)}, u32[]{:S(2)}) async-start(bf16[8,32,384]{2,1,0:T(8,128)(2,1)} %bitcast.5), calls=%async_computation.1 | async-start | bytes 393216 | tf_op jit(solution)/shard_map/all_to_all | solution.py:53
  60.0 5.8 %copy-start.1 = (bf16[1,256,128]{2,1,0:T(8,128)(2,1)S(1)}, bf16[1,256,128]{2,1,0:T(8,128)(2,1)}, u32[]{:S(2)}) copy-start(bf16[1,256,128]{2,1,0:T(8,128)(2,1)} %param.9) | copy-start | bytes 196612
  63.0 14.4 %collective-permute-start.1 = (bf16[256,512]{1,0:T(8,128)(2,1)S(1)}, bf16[256,512]{1,0:T(8,128)(2,1)S(1)}, u32[]{:S(2)}, u32[]{:S(2)}) collective-permute-start(bf16[256,512]{1,0:T(8,128)(2,1)S(1)} %select_convert_fusion), channel_id=1, source_target_pairs={{0,64},{1,65},{2,66},{3,67},{4,68},{5,69},{6,70},{7,71},{8,72},{9,... | collective-permute-start | bytes 786440 | tf_op jit(solution)/shard_map/ppermute | solution.py:15
  65.8 16.4 %collective-permute-start = (bf16[256,128]{1,0:T(8,128)(2,1)S(1)}, bf16[256,128]{1,0:T(8,128)(2,1)S(1)}, u32[]{:S(2)}, u32[]{:S(2)}) collective-permute-start(bf16[256,128]{1,0:T(8,128)(2,1)S(1)} %bitcast.48), channel_id=1, source_target_pairs={{0,32},{1,33},{2,34},{3,35},{4,36},{5,37},{6,38},{7,39},{8,40},{9,... | collective-permute-start | bytes 196616 | tf_op jit(solution)/shard_map/ppermute | solution.py:15
  77.6 32.0 %collective-permute-start.2 = (bf16[256,512]{1,0:T(8,128)(2,1)S(1)}, bf16[256,512]{1,0:T(8,128)(2,1)S(1)}, u32[]{:S(2)}, u32[]{:S(2)}) collective-permute-start(bf16[256,512]{1,0:T(8,128)(2,1)S(1)} %fusion.19), channel_id=1, source_target_pairs={{0,32},{1,33},{2,34},{3,35},{4,36},{5,37},{6,38},{7,39},{8,40},{9,... | collective-permute-start | bytes 786440 | tf_op jit(solution)/shard_map/ppermute | solution.py:15
  82.2 34.9 %copy-start = (bf16[1536,1024]{1,0:T(8,128)(2,1)S(1)}, bf16[1536,1024]{1,0:T(8,128)(2,1)}, u32[]{:S(2)}) copy-start(bf16[1536,1024]{1,0:T(8,128)(2,1)} %reshape.33) | copy-start | bytes 9437188
  109.9 7.1 %collective-permute-start.3 = (bf16[256,512]{1,0:T(8,128)(2,1)S(1)}, bf16[256,512]{1,0:T(8,128)(2,1)S(1)}, u32[]{:S(2)}, u32[]{:S(2)}) collective-permute-start(bf16[256,512]{1,0:T(8,128)(2,1)S(1)} %pad_maximum_fusion.1), channel_id=1, source_target_pairs={{0,64},{1,65},{2,66},{3,67},{4,68},{5,69},{6,70},{7,71},{8,72},{9,... | collective-permute-start | bytes 786440 | tf_op jit(solution)/shard_map/ppermute | solution.py:15

commit v2 on v1

v2 whole, which is shorter than its diff:
```python
import jax
import jax.numpy as jnp
from jax import lax
from jax.experimental import pallas as pl
from jax.experimental.pallas import tpu as pltpu
from jax.sharding import PartitionSpec as P

NX, NZL = 4, 8
X_GROUPS = [[b * NX + x for x in range(NX)] for b in range(32)]
ZL_GROUPS = [
    [hi * 32 + zl * NX + x for zl in range(NZL)] for hi in range(4) for x in range(NX)
]
Y_BIT, ZH_BIT = 64, 32
F32, BF16 = jnp.float32, jnp.bfloat16
NT = (((1,), (1,)), ((), ()))
TN = (((0,), (0,)), ((), ()))
VMEM = pl.BlockSpec(memory_space=pltpu.VMEM)
SMEM = pl.BlockSpec(memory_space=pltpu.SMEM)


def call(kernel, out_shape, n_scalar, n_array, flops=0, moved=0, mib=6):
    several = isinstance(out_shape, (tuple, list))
    return pl.pallas_call(
        kernel,
        out_shape=out_shape,
        in_specs=[SMEM] * n_scalar + [VMEM] * n_array,
        out_specs=[VMEM] * len(out_shape) if several else VMEM,
        compiler_params=pltpu.CompilerParams(vmem_limit_bytes=mib * 1024 * 1024),
        cost_estimate=pl.CostEstimate(flops=flops, bytes_accessed=moved, transcendentals=0),
    )


def swapped(shard, bit):
    return lax.ppermute(shard, "tp", [(i, i ^ bit) for i in range(lax.axis_size("tp"))])


def over(axis, shard, groups=None):
    return lax.all_to_all(
        shard, axis, split_axis=0, concat_axis=0, axis_index_groups=groups, tiled=True
    )


def dot(a, b, dims=(((1,), (0,)), ((), ()))):
    return lax.dot_general(a, b, dims, preferred_element_type=F32)


def pack_kernel(tok_ref, out_ref):
    turned = tok_ref[...]
    third = turned.shape[0] // 3
    packed = jnp.concatenate([turned[j * third : (j + 1) * third] for j in range(3)], axis=1)
    for z in range(out_ref.shape[0]):
        out_ref[z] = packed


def one_hot(slot_ref, slot_total):
    n_tok = slot_ref.shape[1]
    slots = lax.broadcasted_iota(jnp.int32, (slot_total, n_tok), 0)
    hit = (slots == slot_ref[0:1, :]) | (slots == slot_ref[1:2, :])
    return jnp.where(hit, 1.0, 0.0).astype(BF16)


def dispatch_kernel(slot_ref, raw_ref, out_ref):
    n_tok = slot_ref.shape[1]
    pieces = [
        raw_ref[z, :, j * n_tok : (j + 1) * n_tok] for z in range(raw_ref.shape[0]) for j in range(3)
    ]
    raw = jnp.concatenate(pieces, axis=0)
    out_ref[...] = dot(one_hot(slot_ref, out_ref.shape[0]), raw, NT).astype(BF16)


def halves(y_ref, width):
    own = pl.multiple_of(y_ref[0] * width, width)
    other = pl.multiple_of((1 - y_ref[0]) * width, width)
    return pl.ds(own, width), pl.ds(other, width)


def forward_kernel(y_ref, rows_ref, gate_ref, up_ref, keep_ref, send_ref):
    width = gate_ref.shape[1] // 2
    own, other = halves(y_ref, width)
    rows = jnp.concatenate([rows_ref[x] for x in range(rows_ref.shape[0])], axis=1)
    for m, w_ref in enumerate((gate_ref, up_ref)):
        at = slice(m * width, (m + 1) * width)
        send_ref[:, at] = dot(rows, w_ref[:, other]).astype(BF16)
        keep_ref[:, at] = dot(rows, w_ref[:, own])


def grad_kernel(zh_ref, keep_ref, near_ref, got_ref, hid_ref, far_ref, out_ref):
    hid = hid_ref.shape[1]
    total = keep_ref[...] + near_ref[...].astype(F32) + got_ref[...].astype(F32)
    for j in range(2):
        mine = zh_ref[0] == j
        upstream = jnp.where(mine, hid_ref[...].astype(F32), far_ref[...].astype(F32))
        gate_pre = total[:, j * hid : (j + 1) * hid]
        up_pre = total[:, (2 + j) * hid : (3 + j) * hid]
        sig = jax.nn.sigmoid(gate_pre)
        gate_grad = upstream * up_pre * sig * (1.0 + gate_pre * (1.0 - sig))
        out_ref[:, j * hid : (j + 1) * hid] = gate_grad.astype(BF16)
        out_ref[:, (2 + j) * hid : (3 + j) * hid] = (upstream * gate_pre * sig).astype(BF16)


def backward_kernel(y_ref, own_ref, other_ref, gate_ref, up_ref, out_ref):
    width = gate_ref.shape[1] // 2
    own, other = halves(y_ref, width)
    wide = out_ref.shape[2]
    for x in range(out_ref.shape[0]):
        at = slice(x * wide, (x + 1) * wide)
        total = dot(own_ref[:, :width], gate_ref[at, own], NT)
        total = total + dot(own_ref[:, width:], up_ref[at, own], NT)
        total = total + dot(other_ref[:, :width], gate_ref[at, other], NT)
        total = total + dot(other_ref[:, width:], up_ref[at, other], NT)
        out_ref[x] = total.astype(BF16)


def sum_kernel(pieces_ref, out_ref):
    total = pieces_ref[0].astype(F32)
    for x in range(1, pieces_ref.shape[0]):
        total = total + pieces_ref[x].astype(F32)
    out_ref[...] = total.astype(BF16)


def combine_kernel(slot_ref, back_ref, out_ref):
    placing = one_hot(slot_ref, back_ref.shape[0])
    part = dot(back_ref[...], placing, TN)
    half = out_ref.shape[1]
    for z in range(out_ref.shape[0]):
        low = part[2 * z * half : (2 * z + 1) * half]
        out_ref[z] = jnp.concatenate([low, part[(2 * z + 1) * half : (2 * z + 2) * half]], axis=1)


def finish_kernel(part_ref, out_ref):
    total = part_ref[0]
    for z in range(1, part_ref.shape[0]):
        total = total + part_ref[z]
    n_tok = out_ref.shape[1]
    out_ref[...] = jnp.concatenate([total[:, :n_tok], total[:, n_tok:]], axis=0).astype(BF16)


def body(tokens, routes, w_gate, w_up, hidden_grad):
    position = lax.axis_index("tp")
    y_at = jnp.bitwise_and(jnp.right_shift(position, 6), 1).reshape(1)
    zh_at = jnp.bitwise_and(jnp.right_shift(position, 5), 1).reshape(1)
    n_groups = lax.axis_size("expert")
    slot_total = hidden_grad.shape[1]
    capacity = slot_total // n_groups
    n_tok, feat = tokens.shape
    block_rows = w_gate.shape[2]
    hid = w_gate.shape[4]
    wide = NZL * feat
    shape = jax.ShapeDtypeStruct

    packed = call(pack_kernel, shape((NZL, feat // 3, 3 * n_tok), BF16), 0, 1)(tokens.T)
    raw = over("tp", packed, ZL_GROUPS)
    hidden = hidden_grad[0]
    raw, hidden_send = lax.optimization_barrier((raw, hidden))

    flat_routes = routes.reshape(n_tok * 2)
    named = (flat_routes[:, None] == jnp.arange(n_groups, dtype=jnp.int32)[None, :]).astype(jnp.int32)
    before = jnp.cumsum(named, axis=0) - named
    slot_index = flat_routes * capacity + jnp.sum(before * named, axis=1)
    slot_index = slot_index.reshape(n_tok, 2).T

    outgoing = call(dispatch_kernel, shape((slot_total, wide), BF16), 0, 2)(slot_index, raw)
    arrived = over("expert", outgoing)
    rows = over("tp", jnp.broadcast_to(arrived[None], (NX, slot_total, wide)), X_GROUPS)
    hidden_far = swapped(hidden_send, ZH_BIT)
    rows, hidden_far = lax.optimization_barrier((rows, hidden_far))

    def arranged(w):
        w = w[0, 0].reshape(NZL, NX, feat, 4, hid).transpose(1, 0, 2, 3, 4)
        return w.reshape(block_rows, 4 * hid)

    gate, up = arranged(w_gate), arranged(w_up)

    half = 4 * hid
    n_flops = 2 * slot_total * block_rows * 2 * half
    n_bytes = 4 * block_rows * half
    keep, send = call(
        forward_kernel,
        [shape((slot_total, half), F32), shape((slot_total, half), BF16)],
        1,
        3,
        n_flops,
        n_bytes,
        16,
    )(y_at, rows, gate, up)
    near = swapped(send, Y_BIT)
    got = swapped((keep + near.astype(F32)).astype(BF16), ZH_BIT)

    grads = call(grad_kernel, shape((slot_total, half), BF16), 1, 5)(
        zh_at, keep, near, got, hidden, hidden_far
    )
    other = swapped(grads, Y_BIT)
    pieces = call(
        backward_kernel, shape((NX, slot_total, wide), BF16), 1, 4, n_flops, n_bytes, 16
    )(y_at, grads, other, gate, up)
    pieces = over("tp", pieces, X_GROUPS)
    summed = call(sum_kernel, shape((slot_total, wide), BF16), 0, 1)(pieces)
    returned = over("expert", summed)

    part = call(combine_kernel, shape((NZL, feat // 2, 2 * n_tok), F32), 0, 2)(slot_index, returned)
    part = over("tp", part, ZL_GROUPS)
    total = call(finish_kernel, shape((feat, n_tok), BF16), 0, 1)(part)
    return total.T


def solution(mesh):
    placed = (
        P("expert", "tp"),
        P("expert", None),
        P("expert", "tp", None, None, None),
        P("expert", "tp", None, None, None),
        P("expert", None, "tp"),
    )
    return jax.shard_map(
        body, mesh=mesh, in_specs=placed, out_specs=P("expert", "tp"), check_vma=False
    )
```

time: 168 us -> 177 us (1.054)
  waiting for transfers between devices: 38.6 us -> 50.1 us
  Pallas kernels: 0 us -> 7.3 us
  other arithmetic: 8.9 us -> 1.9 us
  matrix products: 5.2 us -> 0 us
  local copies, waits for them, and re-layouts: 7.04 us -> 12.2 us
  blocking collectives: 58.8 us -> 55.3 us
    all_gather x1 -> x0, blocking collectives: 12 us -> none  [body(): lax.all_gather(arrived, 'tp', axis_index_groups=X_GROUPS, axis=0, tiled=F...]
    all_to_all x2 -> x3, waiting for transfers between devices: 7.37 us -> 17.1 us  [over(): lax.all_to_all(shard, axis, split_axis=0, concat_axis=0, axis_index_group...]
    all_to_all x3, blocking collectives: 46.8 us -> 55.3 us  [over(): lax.all_to_all(shard, axis, split_axis=0, concat_axis=0, axis_index_group...]
    pallas_call x0 -> x8, Pallas kernels: none -> 7.3 us  [the longest x1 2.12 us: body(): call(forward_kernel, [shape((slot_total, half), F32), shape((slot_total,...]
    transpose x1, other arithmetic: 6.21 us -> 0.7 us  [body(): slot_index = slot_index.reshape(n_tok, 2).T]
    dot_general x4 -> x0, matrix products: 5.2 us -> none  [the longest x1 2.93 us: body(): pre = jnp.dot(rows, both, preferred_element_type=f32)]
    another operation x0 -> x2, local copies, waits for them, and re-layouts: none -> 5.18 us  [arranged(): w = w[0, 0].reshape(NZL, NX, feat, 4, hid).transpose(1, 0, 2, 3, 4)]
    all_to_all x2 -> x3, starting transfers between devices: 25.4 us -> 29.6 us  [over(): lax.all_to_all(shard, axis, split_axis=0, concat_axis=0, axis_index_group...]
  transfers between devices with their start and end apart: 6 -> 7, of which waited for: 3 -> 5; matrix products, arithmetic and copies ran while one was open for 8% -> 6% of each run, Pallas kernels for 0% -> 0%
where the time goes in v2:
time: 177 us; the launch traced here: 175 us
  blocking collectives  55.3 us (31%)
  waiting for transfers between devices  50.1 us (28%)
  starting transfers between devices  47.8 us (27%)
  local copies, waits for them, and re-layouts  12.2 us (7%)
  Pallas kernels  7.3 us (4%)
  other arithmetic  1.9 us (1%)
    all_to_all x3, blocking collectives, over(): lax.all_to_all(shard, axis, split_axis=0, concat_axis=0, axis_index_group...  55.3 us
    ppermute x4, waiting for transfers between devices, swapped(): lax.ppermute(shard, 'tp', [(i, i ^ bit) for i in range(lax.axis_size('tp'...  33 us
    all_to_all x3, starting transfers between devices, over(): lax.all_to_all(shard, axis, split_axis=0, concat_axis=0, axis_index_group...  29.6 us
    ppermute x4, starting transfers between devices, swapped(): lax.ppermute(shard, 'tp', [(i, i ^ bit) for i in range(lax.axis_size('tp'...  18.1 us
    all_to_all x3, waiting for transfers between devices, over(): lax.all_to_all(shard, axis, split_axis=0, concat_axis=0, axis_index_group...  17.1 us
    another operation x2, local copies, waits for them, and re-layouts, arranged(): w = w[0, 0].reshape(NZL, NX, feat, 4, hid).transpose(1, 0, 2, 3, 4)  5.18 us
  transfers between devices with their start and end apart: 7, of which 5 were waited for; matrix products, arithmetic and copies ran while one was open for 6% of the time, Pallas kernels for 0%

profile of v2, /device:TPU:1, one launch (start us, length us, event | category | flops | bytes accessed | tf_op | source)
XLA Modules:
  0.0 174.8 jit_solution(15298453516334716927)
XLA Ops:
  0.0 0.0 copy-start.3
  0.0 0.7 copy-done.3
  0.7 0.7 shard_map.55
  1.4 16.3 %all-to-all-start = ((bf16[8,16,192]{2,1,0:T(8,128)(2,1)}), bf16[8,16,192]{2,1,0:T(8,128)(2,1)S(1)}, u32[]{:S(2)}, u32[]{:S(2)}) async-start(bf16[8,16,192]{2,1,0:T(8,128)(2,1)} %shard_map.55), calls=%async_computation | async-start | bytes 131072 | tf_op jit(solution)/shard_map/all_to_all | solution.py:38
  17.7 0.8 copy.10
  18.4 0.1 eq.15
  18.6 0.1 fusion
  18.7 0.2 reduce_window_sum.11
  18.8 0.2 select_reduce_fusion
  19.0 0.1 reduce_sum.12
  19.2 0.1 copy.11
  19.2 0.7 add_bitcast_fusion.slot_ref
  19.9 7.5 %all-to-all-done.raw_ref = bf16[8,16,192]{2,1,0:T(8,128)(2,1)S(1)} async-done(((bf16[8,16,192]{2,1,0:T(8,128)(2,1)}), bf16[8,16,192]{2,1,0:T(8,128)(2,1)S(1)}, u32[]{:S(2)}, u32[]{:S(2)}) %all-to-all-start) | async-done | bytes 49184 | tf_op jit(solution)/shard_map/all_to_all | solution.py:38
  27.4 1.0 shard_map.56
  28.4 9.2 %all-to-all-start.1 = ((bf16[8,32,384]{2,1,0:T(8,128)(2,1)}), bf16[8,32,384]{2,1,0:T(8,128)(2,1)S(1)}, u32[]{:S(2)}, u32[]{:S(2)}) async-start(bf16[8,32,384]{2,1,0:T(8,128)(2,1)} %bitcast.5), calls=%async_computation.1 | async-start | bytes 393216 | tf_op jit(solution)/shard_map/all_to_all | solution.py:38
  37.6 0.0 copy-start.4
  37.6 3.4 %copy.12 = bf16[8,4,48,4,128]{4,3,2,0,1:T(4,128)(2,1)} copy(bf16[8,4,48,4,128]{4,3,2,1,0:T(4,128)(2,1)} %bitcast.30) | data formatting | bytes 3145728 | tf_op jit(solution)/shard_map/reshape;squeeze | solution.py:169
  41.0 0.0 copy-done.4
  41.0 0.0 copy-start.2
  41.0 1.8 %copy.13 = bf16[8,4,48,4,128]{4,3,2,0,1:T(4,128)(2,1)} copy(bf16[8,4,48,4,128]{4,3,2,1,0:T(4,128)(2,1)S(1)} %bitcast.31) | data formatting | bytes 3145728 | tf_op jit(solution)/shard_map/reshape;squeeze | solution.py:169
  42.8 0.0 copy-done.2
  42.8 11.6 %collective-permute-start = (bf16[256,128]{1,0:T(8,128)(2,1)S(1)}, bf16[256,128]{1,0:T(8,128)(2,1)S(1)}, u32[]{:S(2)}, u32[]{:S(2)}) collective-permute-start(bf16[256,128]{1,0:T(8,128)(2,1)S(1)} %bitcast.25), channel_id=1, source_target_pairs={{0,32},{1,33},{2,34},{3,35},{4,36},{5,37},{6,38},{7,39},{8,40},{9,... | collective-permute-start | bytes 196616 | tf_op jit(solution)/shard_map/ppermute | solution.py:34
  54.3 0.0 all-to-all-done.1
  54.4 1.0 broadcast_in_dim.10
  55.3 4.2 %all-to-all-start.2 = ((bf16[4,256,384]{2,1,0:T(8,128)(2,1)}), bf16[4,256,384]{2,1,0:T(8,128)(2,1)}, u32[]{:S(2)}, u32[]{:S(2)}) async-start(bf16[4,256,384]{2,1,0:T(8,128)(2,1)} %broadcast_in_dim.10), calls=%async_computation.2 | async-start | bytes 1572864 | tf_op jit(solution)/shard_map/all_to_all | solution.py:38
  59.5 2.4 %copy_bitcast_fusion = (bf16[1536,512]{1,0:T(8,128)(2,1)S(1)}, bf16[1536,512]{1,0:T(8,128)(2,1)S(1)}) fusion(bf16[192,8,4,128]{3,2,1,0:T(4,128)(2,1)} %bitcast.29, bf16[192,8,4,128]{3,2,1,0:T(4,128)(2,1)} %bitcast.28), kind=kLoop, calls=%fused_computation | loop fusion | bytes 6291456 | tf_op jit(solution)/shard_map/reshape | solution.py:170
  61.9 0.0 collective-permute-done.far_ref
  61.9 9.6 %all-to-all-done.2.rows_ref = bf16[4,256,384]{2,1,0:T(8,128)(2,1)} async-done(((bf16[4,256,384]{2,1,0:T(8,128)(2,1)}), bf16[4,256,384]{2,1,0:T(8,128)(2,1)}, u32[]{:S(2)}, u32[]{:S(2)}) %all-to-all-start.2) | async-done | bytes 786464 | tf_op jit(solution)/shard_map/all_to_all | solution.py:38
  71.5 2.1 %shard_map.57 = (f32[256,512]{1,0:T(8,128)S(1)}, bf16[256,512]{1,0:T(8,128)(2,1)S(1)}) custom-call(s32[1]{0:T(128)} %bitcast.1.y_ref, bf16[4,256,384]{2,1,0:T(8,128)(2,1)} %all-to-all-done.2.rows_ref, bf16[1536,512]{1,0:T(8,128)(2,1)S(1)} %get-tuple-element.18.gate_ref, bf16[1536,512]{1,0:T(8,128)(2,1)S(1)} %get-tuple-element.17.up_ref), custom_call_target="tpu_custom_call" | custom-call | flops 805306368 | bytes 3145728 | tf_op jit(solution)/shard_map/pallas_call | solution.py:177
  73.7 2.3 %collective-permute-start.1 = (bf16[256,512]{1,0:T(8,128)(2,1)S(1)}, bf16[256,512]{1,0:T(8,128)(2,1)S(1)}, u32[]{:S(2)}, u32[]{:S(2)}) collective-permute-start(bf16[256,512]{1,0:T(8,128)(2,1)S(1)} %get-tuple-element.15), channel_id=1, source_target_pairs={{0,64},{1,65},{2,66},{3,67},{4,68},{5,69},{6,70},{7,71},{8,72},{9,... | collective-permute-start | bytes 786440 | tf_op jit(solution)/shard_map/ppermute | solution.py:34
  76.0 6.1 %collective-permute-done.1.near_ref = bf16[256,512]{1,0:T(8,128)(2,1)S(1)} collective-permute-done((bf16[256,512]{1,0:T(8,128)(2,1)S(1)}, bf16[256,512]{1,0:T(8,128)(2,1)S(1)}, u32[]{:S(2)}, u32[]{:S(2)}) %collective-permute-start.1) | collective-permute-done | bytes 262176 | tf_op jit(solution)/shard_map/ppermute | solution.py:34
  82.1 0.8 add_convert_fusion
  82.9 0.0 copy-start
  82.9 0.8 copy-done
  83.6 1.9 %collective-permute-start.2 = (bf16[256,512]{1,0:T(8,128)(2,1)}, bf16[256,512]{1,0:T(8,128)(2,1)}, u32[]{:S(2)}, u32[]{:S(2)}) collective-permute-start(bf16[256,512]{1,0:T(8,128)(2,1)} %add_convert_fusion), channel_id=1, source_target_pairs={{0,32},{1,33},{2,34},{3,35},{4,36},{5,37},{6,38},{7,39},{8,40},{9,... | collective-permute-start | bytes 786440 | tf_op jit(solution)/shard_map/ppermute | solution.py:34
  85.6 22.1 %collective-permute-done.2.got_ref = bf16[256,512]{1,0:T(8,128)(2,1)} collective-permute-done((bf16[256,512]{1,0:T(8,128)(2,1)}, bf16[256,512]{1,0:T(8,128)(2,1)}, u32[]{:S(2)}, u32[]{:S(2)}) %collective-permute-start.2) | collective-permute-done | bytes 262176 | tf_op jit(solution)/shard_map/ppermute | solution.py:34
  107.7 0.0 copy-start.1
  107.7 1.0 copy-done.1
  108.8 1.2 shard_map.58.own_ref
  109.9 2.3 %collective-permute-start.3 = (bf16[256,512]{1,0:T(8,128)(2,1)S(1)}, bf16[256,512]{1,0:T(8,128)(2,1)S(1)}, u32[]{:S(2)}, u32[]{:S(2)}) collective-permute-start(bf16[256,512]{1,0:T(8,128)(2,1)S(1)} %shard_map.58.own_ref), channel_id=1, source_target_pairs={{0,64},{1,65},{2,66},{3,67},{4,68},{5,69},{6,70},{7,71},{8,72},{9,... | collective-permute-start | bytes 786440 | tf_op jit(solution)/shard_map/ppermute | solution.py:34
  112.3 4.8 %collective-permute-done.3.other_ref = bf16[256,512]{1,0:T(8,128)(2,1)S(1)} collective-permute-done((bf16[256,512]{1,0:T(8,128)(2,1)S(1)}, bf16[256,512]{1,0:T(8,128)(2,1)S(1)}, u32[]{:S(2)}, u32[]{:S(2)}) %collective-permute-start.3) | collective-permute-done | bytes 262176 | tf_op jit(solution)/shard_map/ppermute | solution.py:34
  117.0 1.3 shard_map.59
  118.3 10.7 %all_to_all.40.pieces_ref = bf16[4,256,384]{2,1,0:T(8,128)(2,1)S(1)} all-to-all(bf16[4,256,384]{2,1,0:T(8,128)(2,1)S(1)} %shard_map.59), channel_id=1, replica_groups={{0,1,2,3},{4,5,6,7},{8,9,10,11},{12,13,14,15},{16,17,18,19},{20,21,22,2..., dimensions={0} | all-to-all | bytes 1572864 | tf_op jit(solution)/shard_map/all_to_all | solution.py:38
  129.1 0.1 shard_map.60
  129.2 21.6 %all_to_all.41 = bf16[8,32,384]{2,1,0:T(8,128)(2,1)S(1)} all-to-all(bf16[8,32,384]{2,1,0:T(8,128)(2,1)S(1)} %bitcast.24), channel_id=1, replica_groups=mesh['expert'=8,'tp'=128] {'expert'}, dimensions={0} | all-to-all | bytes 393216 | tf_op jit(solution)/shard_map/all_to_all | solution.py:38
  150.7 0.3 shard_map.61
  151.1 23.0 %all_to_all.42.part_ref = f32[8,24,128]{2,1,0:T(8,128)S(1)} all-to-all(f32[8,24,128]{2,1,0:T(8,128)S(1)} %shard_map.61), channel_id=1, replica_groups={{0,4,8,12,16,20,24,28},{1,5,9,13,17,21,25,29},{2,6,10,14,18,22,26,30},{..., dimensions={0} | all-to-all | bytes 196608 | tf_op jit(solution)/shard_map/all_to_all | solution.py:38
  174.1 0.7 shard_map.62
Async XLA Ops:
  0.0 0.7 copy-start.3
  1.4 26.0 %all-to-all-start = ((bf16[8,16,192]{2,1,0:T(8,128)(2,1)}), bf16[8,16,192]{2,1,0:T(8,128)(2,1)S(1)}, u32[]{:S(2)}, u32[]{:S(2)}) async-start(bf16[8,16,192]{2,1,0:T(8,128)(2,1)} %shard_map.55), calls=%async_computation | async-start | bytes 131072 | tf_op jit(solution)/shard_map/all_to_all | solution.py:38
  28.4 26.0 %all-to-all-start.1 = ((bf16[8,32,384]{2,1,0:T(8,128)(2,1)}), bf16[8,32,384]{2,1,0:T(8,128)(2,1)S(1)}, u32[]{:S(2)}, u32[]{:S(2)}) async-start(bf16[8,32,384]{2,1,0:T(8,128)(2,1)} %bitcast.5), calls=%async_computation.1 | async-start | bytes 393216 | tf_op jit(solution)/shard_map/all_to_all | solution.py:38
  37.6 3.4 %copy-start.4 = (bf16[1,1,1536,4,128]{4,3,2,1,0:T(4,128)(2,1)S(1)}, bf16[1,1,1536,4,128]{4,3,2,1,0:T(4,128)(2,1)}, u32[]{:S(2)}) copy-start(bf16[1,1,1536,4,128]{4,3,2,1,0:T(4,128)(2,1)} %param.8) | copy-start | bytes 4718596
  41.0 1.8 %copy-start.2 = (bf16[1,256,128]{2,1,0:T(8,128)(2,1)S(1)}, bf16[1,256,128]{2,1,0:T(8,128)(2,1)}, u32[]{:S(2)}) copy-start(bf16[1,256,128]{2,1,0:T(8,128)(2,1)} %param.9) | copy-start | bytes 196612
  42.8 19.2 %collective-permute-start = (bf16[256,128]{1,0:T(8,128)(2,1)S(1)}, bf16[256,128]{1,0:T(8,128)(2,1)S(1)}, u32[]{:S(2)}, u32[]{:S(2)}) collective-permute-start(bf16[256,128]{1,0:T(8,128)(2,1)S(1)} %bitcast.25), channel_id=1, source_target_pairs={{0,32},{1,33},{2,34},{3,35},{4,36},{5,37},{6,38},{7,39},{8,40},{9,... | collective-permute-start | bytes 196616 | tf_op jit(solution)/shard_map/ppermute | solution.py:34
  55.3 16.2 %all-to-all-start.2 = ((bf16[4,256,384]{2,1,0:T(8,128)(2,1)}), bf16[4,256,384]{2,1,0:T(8,128)(2,1)}, u32[]{:S(2)}, u32[]{:S(2)}) async-start(bf16[4,256,384]{2,1,0:T(8,128)(2,1)} %broadcast_in_dim.10), calls=%async_computation.2 | async-start | bytes 1572864 | tf_op jit(solution)/shard_map/all_to_all | solution.py:38
  73.7 8.4 %collective-permute-start.1 = (bf16[256,512]{1,0:T(8,128)(2,1)S(1)}, bf16[256,512]{1,0:T(8,128)(2,1)S(1)}, u32[]{:S(2)}, u32[]{:S(2)}) collective-permute-start(bf16[256,512]{1,0:T(8,128)(2,1)S(1)} %get-tuple-element.15), channel_id=1, source_target_pairs={{0,64},{1,65},{2,66},{3,67},{4,68},{5,69},{6,70},{7,71},{8,72},{9,... | collective-permute-start | bytes 786440 | tf_op jit(solution)/shard_map/ppermute | solution.py:34
  82.9 0.8 copy-start
  83.6 24.1 %collective-permute-start.2 = (bf16[256,512]{1,0:T(8,128)(2,1)}, bf16[256,512]{1,0:T(8,128)(2,1)}, u32[]{:S(2)}, u32[]{:S(2)}) collective-permute-start(bf16[256,512]{1,0:T(8,128)(2,1)} %add_convert_fusion), channel_id=1, source_target_pairs={{0,32},{1,33},{2,34},{3,35},{4,36},{5,37},{6,38},{7,39},{8,40},{9,... | collective-permute-start | bytes 786440 | tf_op jit(solution)/shard_map/ppermute | solution.py:34
  107.7 1.0 copy-start.1
  109.9 7.1 %collective-permute-start.3 = (bf16[256,512]{1,0:T(8,128)(2,1)S(1)}, bf16[256,512]{1,0:T(8,128)(2,1)S(1)}, u32[]{:S(2)}, u32[]{:S(2)}) collective-permute-start(bf16[256,512]{1,0:T(8,128)(2,1)S(1)} %shard_map.58.own_ref), channel_id=1, source_target_pairs={{0,64},{1,65},{2,66},{3,67},{4,68},{5,69},{6,70},{7,71},{8,72},{9,... | collective-permute-start | bytes 786440 | tf_op jit(solution)/shard_map/ppermute | solution.py:34

commit v3 on v2

v3 whole, which is shorter than its diff:
```python
import functools

import jax
import jax.numpy as jnp
from jax import lax
from jax.experimental import pallas as pl
from jax.experimental.pallas import tpu as pltpu
from jax.sharding import PartitionSpec as P

NX, NZL = 4, 8
X_GROUPS = [[b * NX + x for x in range(NX)] for b in range(32)]
ZH_GROUPS = [
    [y * 64 + zh * 32 + f for zh in range(2)] for y in range(2) for f in range(32)
]
ZL_GROUPS = [
    [hi * 32 + zl * NX + x for zl in range(NZL)] for hi in range(4) for x in range(NX)
]
Y_BIT = 64
F32, BF16 = jnp.float32, jnp.bfloat16
NT = (((1,), (1,)), ((), ()))
TN = (((0,), (0,)), ((), ()))
VMEM = pl.BlockSpec(memory_space=pltpu.VMEM)
SMEM = pl.BlockSpec(memory_space=pltpu.SMEM)


def call(kernel, outs, scalars, arrays, flops=0, mib=6):
    several = isinstance(outs, (tuple, list))
    moved = sum(v.size * v.dtype.itemsize for v in [*arrays, *(outs if several else [outs])])
    return pl.pallas_call(
        kernel,
        out_shape=outs,
        in_specs=[SMEM] * len(scalars) + [VMEM] * len(arrays),
        out_specs=[VMEM] * len(outs) if several else VMEM,
        compiler_params=pltpu.CompilerParams(vmem_limit_bytes=mib * 1024 * 1024),
        cost_estimate=pl.CostEstimate(flops=flops, bytes_accessed=moved, transcendentals=0),
    )(*scalars, *arrays)


def swapped(shard, bit):
    return lax.ppermute(shard, "tp", [(i, i ^ bit) for i in range(lax.axis_size("tp"))])


def over(axis, shard, groups=None):
    return lax.all_to_all(
        shard, axis, split_axis=0, concat_axis=0, axis_index_groups=groups, tiled=True
    )


def dot(a, b, dims=(((1,), (0,)), ((), ()))):
    return lax.dot_general(a, b, dims, preferred_element_type=F32)


def pack_kernel(tok_ref, out_ref):
    turned = tok_ref[...]
    third = turned.shape[0] // 3
    packed = jnp.concatenate([turned[j * third : (j + 1) * third] for j in range(3)], axis=1)
    for z in range(out_ref.shape[0]):
        out_ref[z] = packed


def arrange_kernel(gate_ref, up_ref, gate_out_ref, up_out_ref):
    feat = gate_ref.shape[0] // (NX * NZL)
    for x in range(NX):
        for z in range(NZL):
            src, dst = (z * NX + x) * feat, (x * NZL + z) * feat
            gate_out_ref[dst : dst + feat] = gate_ref[src : src + feat]
            up_out_ref[dst : dst + feat] = up_ref[src : src + feat]


def one_hot(slot_ref, slot_total):
    n_tok = slot_ref.shape[1]
    slots = lax.broadcasted_iota(jnp.int32, (slot_total, n_tok), 0)
    hit = (slots == slot_ref[0:1, :]) | (slots == slot_ref[1:2, :])
    return jnp.where(hit, 1.0, 0.0).astype(BF16)


def dispatch_kernel(slot_ref, raw_ref, out_ref):
    n_tok = slot_ref.shape[1]
    pieces = [
        raw_ref[z, :, j * n_tok : (j + 1) * n_tok] for z in range(raw_ref.shape[0]) for j in range(3)
    ]
    raw = jnp.concatenate(pieces, axis=0)
    out_ref[...] = dot(one_hot(slot_ref, out_ref.shape[0]), raw, NT).astype(BF16)


def halves(y_ref, width):
    own = pl.multiple_of(y_ref[0] * width, width)
    other = pl.multiple_of((1 - y_ref[0]) * width, width)
    return pl.ds(own, width), pl.ds(other, width)


def forward_kernel(y_ref, rows_ref, gate_ref, up_ref, out_ref, *, mine):
    width = gate_ref.shape[1] // 2
    at = halves(y_ref, width)[0 if mine else 1]
    rows = jnp.concatenate([rows_ref[x] for x in range(rows_ref.shape[0])], axis=1)
    for m, w_ref in enumerate((gate_ref, up_ref)):
        out_ref[:, m * width : (m + 1) * width] = dot(rows, w_ref[:, at]).astype(out_ref.dtype)


def near_kernel(keep_ref, near_ref, hid_ref, total_ref, send_ref):
    total = keep_ref[...] + near_ref[...].astype(F32)
    width = total.shape[1]
    total_ref[...] = total
    send_ref[:, :width] = total.astype(BF16)
    send_ref[:, width:] = hid_ref[...]


def grad_kernel(zh_ref, total_ref, both_ref, out_ref):
    width = total_ref.shape[1]
    hid = width // 4
    total = total_ref[...] + both_ref[1 - zh_ref[0], :, :width].astype(F32)
    for j in range(2):
        upstream = both_ref[j, :, width:].astype(F32)
        gate_pre = total[:, j * hid : (j + 1) * hid]
        up_pre = total[:, (2 + j) * hid : (3 + j) * hid]
        sig = jax.nn.sigmoid(gate_pre)
        gate_grad = upstream * up_pre * sig * (1.0 + gate_pre * (1.0 - sig))
        out_ref[:, j * hid : (j + 1) * hid] = gate_grad.astype(BF16)
        out_ref[:, (2 + j) * hid : (3 + j) * hid] = (upstream * gate_pre * sig).astype(BF16)


def backward_kernel(y_ref, grad_ref, gate_ref, up_ref, *rest, mine):
    out_ref = rest[-1]
    width = gate_ref.shape[1] // 2
    at = halves(y_ref, width)[0 if mine else 1]
    wide = out_ref.shape[2]
    for x in range(out_ref.shape[0]):
        r = slice(x * wide, (x + 1) * wide)
        total = dot(grad_ref[:, :width], gate_ref[r, at], NT)
        total = total + dot(grad_ref[:, width:], up_ref[r, at], NT)
        if not mine:
            total = total + rest[0][x]
        out_ref[x] = total.astype(out_ref.dtype)


def sum_kernel(pieces_ref, out_ref):
    total = pieces_ref[0].astype(F32)
    for x in range(1, pieces_ref.shape[0]):
        total = total + pieces_ref[x].astype(F32)
    out_ref[...] = total.astype(BF16)


def combine_kernel(slot_ref, back_ref, out_ref):
    placing = one_hot(slot_ref, back_ref.shape[0])
    part = dot(back_ref[...], placing, TN)
    half = out_ref.shape[1]
    for z in range(out_ref.shape[0]):
        low = part[2 * z * half : (2 * z + 1) * half]
        out_ref[z] = jnp.concatenate([low, part[(2 * z + 1) * half : (2 * z + 2) * half]], axis=1)


def finish_kernel(part_ref, out_ref):
    total = part_ref[0]
    for z in range(1, part_ref.shape[0]):
        total = total + part_ref[z]
    n_tok = out_ref.shape[1]
    out_ref[...] = jnp.concatenate([total[:, :n_tok], total[:, n_tok:]], axis=0).astype(BF16)


def body(tokens, routes, w_gate, w_up, hidden_grad):
    position = lax.axis_index("tp")
    y_at = jnp.bitwise_and(jnp.right_shift(position, 6), 1).reshape(1)
    zh_at = jnp.bitwise_and(jnp.right_shift(position, 5), 1).reshape(1)
    n_groups = lax.axis_size("expert")
    slot_total = hidden_grad.shape[1]
    capacity = slot_total // n_groups
    n_tok, feat = tokens.shape
    block_rows = w_gate.shape[2]
    hid = w_gate.shape[4]
    wide = NZL * feat
    shape = jax.ShapeDtypeStruct

    half = 4 * hid
    flat = [w[0, 0].reshape(block_rows, half) for w in (w_gate, w_up)]
    gate, up = call(arrange_kernel, [shape((block_rows, half), BF16)] * 2, [], flat, mib=16)

    packed = call(pack_kernel, shape((NZL, feat // 3, 3 * n_tok), BF16), [], [tokens.T])
    raw = over("tp", packed, ZL_GROUPS)

    flat_routes = routes.reshape(n_tok * 2)
    named = (flat_routes[:, None] == jnp.arange(n_groups, dtype=jnp.int32)[None, :]).astype(jnp.int32)
    before = jnp.cumsum(named, axis=0) - named
    slot_index = flat_routes * capacity + jnp.sum(before * named, axis=1)
    slot_index = slot_index.reshape(n_tok, 2).T

    outgoing = call(dispatch_kernel, shape((slot_total, wide), BF16), [], [slot_index, raw])
    arrived = over("expert", outgoing)
    arrived, gate, up = lax.optimization_barrier((arrived, gate, up))
    rows = lax.all_gather(arrived, "tp", axis_index_groups=X_GROUPS, axis=0, tiled=False)

    n_flops = 2 * slot_total * block_rows * half
    given = [rows, gate, up]
    send = call(
        functools.partial(forward_kernel, mine=False),
        shape((slot_total, half), BF16),
        [y_at],
        given,
        n_flops,
        16,
    )
    keep = call(
        functools.partial(forward_kernel, mine=True),
        shape((slot_total, half), F32),
        [y_at],
        given,
        n_flops,
        16,
    )
    near = swapped(send, Y_BIT)
    total, send = call(
        near_kernel,
        [shape((slot_total, half), F32), shape((slot_total, half + hid), BF16)],
        [],
        [keep, near, hidden_grad[0]],
    )
    both = lax.all_gather(send, "tp", axis_index_groups=ZH_GROUPS, axis=0, tiled=False)

    grads = call(grad_kernel, shape((slot_total, half), BF16), [zh_at], [total, both])
    other = swapped(grads, Y_BIT)
    pieces = (NX, slot_total, wide)
    held = call(
        functools.partial(backward_kernel, mine=True),
        shape(pieces, F32),
        [y_at],
        [grads, gate, up],
        n_flops,
        16,
    )
    pieces = call(
        functools.partial(backward_kernel, mine=False),
        shape(pieces, BF16),
        [y_at],
        [other, gate, up, held],
        n_flops,
        16,
    )
    pieces = over("tp", pieces, X_GROUPS)
    summed = call(sum_kernel, shape((slot_total, wide), BF16), [], [pieces])
    returned = over("expert", summed)

    part = call(combine_kernel, shape((NZL, feat // 2, 2 * n_tok), F32), [], [slot_index, returned])
    part = over("tp", part, ZL_GROUPS)
    total = call(finish_kernel, shape((feat, n_tok), BF16), [], [part])
    return total.T


def solution(mesh):
    placed = (
        P("expert", "tp"),
        P("expert", None),
        P("expert", "tp", None, None, None),
        P("expert", "tp", None, None, None),
        P("expert", None, "tp"),
    )
    return jax.shard_map(
        body, mesh=mesh, in_specs=placed, out_specs=P("expert", "tp"), check_vma=False
    )
```

time: 177 us -> 160 us (0.904)
  blocking collectives: 55.3 us -> 93.2 us
  waiting for transfers between devices: 50.1 us -> 20.8 us
  starting transfers between devices: 47.8 us -> 30.3 us
  local copies, waits for them, and re-layouts: 12.2 us -> 5.66 us
    all_gather x0 -> x2, blocking collectives: none -> 36 us  [the longest x1 24.6 us: body(): lax.all_gather(send, 'tp', axis_index_groups=ZH_GROUPS, axis=0, tiled=False)]
    ppermute x4 -> x2, waiting for transfers between devices: 33 us -> 7.29 us  [swapped(): lax.ppermute(shard, 'tp', [(i, i ^ bit) for i in range(lax.axis_size('tp'...]
    ppermute x4 -> x2, starting transfers between devices: 18.1 us -> 4.87 us  [swapped(): lax.ppermute(shard, 'tp', [(i, i ^ bit) for i in range(lax.axis_size('tp'...]
    all_to_all x3 -> x2, starting transfers between devices: 29.6 us -> 25.4 us  [over(): lax.all_to_all(shard, axis, split_axis=0, concat_axis=0, axis_index_group...]
    all_to_all x3 -> x2, waiting for transfers between devices: 17.1 us -> 13.5 us  [over(): lax.all_to_all(shard, axis, split_axis=0, concat_axis=0, axis_index_group...]
    another operation x2 -> x1, local copies, waits for them, and re-layouts: 5.18 us -> 2.41 us  [body(): flat = [w[0, 0].reshape(block_rows, half) for w in (w_gate, w_up)]]
    reshape x1 -> x0, local copies, waits for them, and re-layouts: 2.41 us -> none  [arranged(): return w.reshape(block_rows, 4 * hid)]
    all_to_all x3, blocking collectives: 55.3 us -> 57.1 us  [over(): lax.all_to_all(shard, axis, split_axis=0, concat_axis=0, axis_index_group...]
  transfers between devices with their start and end apart: 7 -> 4, of which waited for: 5 -> 4; matrix products, arithmetic and copies ran while one was open for 6% -> 3% of each run, Pallas kernels for 0% -> 1%
where the time goes in v3:
time: 160 us; the launch traced here: 158 us
  blocking collectives  93.2 us (58%)
  starting transfers between devices  30.3 us (19%)
  waiting for transfers between devices  20.8 us (13%)
  Pallas kernels  6.77 us (4%)
  local copies, waits for them, and re-layouts  5.66 us (4%)
    all_to_all x3, blocking collectives, over(): lax.all_to_all(shard, axis, split_axis=0, concat_axis=0, axis_index_group...  57.1 us
    all_to_all x2, starting transfers between devices, over(): lax.all_to_all(shard, axis, split_axis=0, concat_axis=0, axis_index_group...  25.4 us
    all_gather x1, blocking collectives, body(): lax.all_gather(send, 'tp', axis_index_groups=ZH_GROUPS, axis=0, tiled=False)  24.6 us
    all_to_all x2, waiting for transfers between devices, over(): lax.all_to_all(shard, axis, split_axis=0, concat_axis=0, axis_index_group...  13.5 us
    all_gather x1, blocking collectives, body(): lax.all_gather(arrived, 'tp', axis_index_groups=X_GROUPS, axis=0, tiled=F...  11.4 us
    ppermute x2, waiting for transfers between devices, swapped(): lax.ppermute(shard, 'tp', [(i, i ^ bit) for i in range(lax.axis_size('tp'...  7.29 us
    pallas_call x12, Pallas kernels, call(): pl.pallas_call(kernel, out_shape=outs, in_specs=[SMEM] * len(scalars) + [...  6.77 us
    ppermute x2, starting transfers between devices, swapped(): lax.ppermute(shard, 'tp', [(i, i ^ bit) for i in range(lax.axis_size('tp'...  4.87 us
  transfers between devices with their start and end apart: 4, of which 4 were waited for; matrix products, arithmetic and copies ran while one was open for 3% of the time, Pallas kernels for 1%

profile of v3, /device:TPU:1, one launch (start us, length us, event | category | flops | bytes accessed | tf_op | source)
XLA Modules:
  0.0 158.0 jit_solution(3949003732667016167)
XLA Ops:
  0.0 0.0 copy-start.3
  0.0 0.7 copy-done.3
  0.7 0.7 shard_map.55
  1.4 16.3 %all-to-all-start = ((bf16[8,16,192]{2,1,0:T(8,128)(2,1)}), bf16[8,16,192]{2,1,0:T(8,128)(2,1)S(1)}, u32[]{:S(2)}, u32[]{:S(2)}) async-start(bf16[8,16,192]{2,1,0:T(8,128)(2,1)} %shard_map.55), calls=%async_computation | async-start | bytes 131072 | tf_op jit(solution)/shard_map/all_to_all | solution.py:44
  17.7 0.8 copy.8
  18.4 0.1 eq.15
  18.6 0.1 fusion
  18.7 0.2 reduce_window_sum.11
  18.8 0.2 select_reduce_fusion
  19.0 0.1 reduce_sum.12
  19.2 0.1 copy.9
  19.2 0.7 add_bitcast_fusion.slot_ref
  19.9 7.5 %all-to-all-done.raw_ref = bf16[8,16,192]{2,1,0:T(8,128)(2,1)S(1)} async-done(((bf16[8,16,192]{2,1,0:T(8,128)(2,1)}), bf16[8,16,192]{2,1,0:T(8,128)(2,1)S(1)}, u32[]{:S(2)}, u32[]{:S(2)}) %all-to-all-start) | async-done | bytes 49184 | tf_op jit(solution)/shard_map/all_to_all | solution.py:44
  27.4 1.0 shard_map.56
  28.4 9.2 %all-to-all-start.1 = ((bf16[8,32,384]{2,1,0:T(8,128)(2,1)}), bf16[8,32,384]{2,1,0:T(8,128)(2,1)S(1)}, u32[]{:S(2)}, u32[]{:S(2)}) async-start(bf16[8,32,384]{2,1,0:T(8,128)(2,1)} %bitcast.4), calls=%async_computation.1 | async-start | bytes 393216 | tf_op jit(solution)/shard_map/all_to_all | solution.py:44
  37.6 2.4 %copy_bitcast_fusion = (bf16[1536,512]{1,0:T(8,128)(2,1)S(1)}, bf16[1536,512]{1,0:T(8,128)(2,1)S(1)}) fusion(bf16[192,8,4,128]{3,2,1,0:T(4,128)(2,1)} %bitcast.28, bf16[192,8,4,128]{3,2,1,0:T(4,128)(2,1)} %bitcast.29), kind=kLoop, calls=%fused_computation | loop fusion | bytes 6291456 | tf_op jit(solution)/shard_map/reshape;squeeze | solution.py:174
  40.0 0.2 shard_map.57
  40.2 6.0 %all-to-all-done.1 = bf16[8,32,384]{2,1,0:T(8,128)(2,1)S(1)} async-done(((bf16[8,32,384]{2,1,0:T(8,128)(2,1)}), bf16[8,32,384]{2,1,0:T(8,128)(2,1)S(1)}, u32[]{:S(2)}, u32[]{:S(2)}) %all-to-all-start.1) | async-done | bytes 196640 | tf_op jit(solution)/shard_map/all_to_all | solution.py:44
  46.2 11.4 %all-gather = bf16[1024,384]{1,0:T(8,128)(2,1)S(1)} all-gather(bf16[256,384]{1,0:T(8,128)(2,1)S(1)} %bitcast.30), channel_id=2, replica_groups={{0,1,2,3},{4,5,6,7},{8,9,10,11},{12,13,14,15},{16,17,18,19},{20,21,22,2..., dimensions={0}, use_global_device_ids=true | all-gather | bytes 983040 | tf_op jit(solution)/shard_map/all_gather | solution.py:189
  57.6 0.0 copy-start
  57.6 0.6 shard_map.59
  58.2 0.3 copy-done
  58.5 2.4 %collective-permute-start = (bf16[256,512]{1,0:T(8,128)(2,1)S(1)}, bf16[256,512]{1,0:T(8,128)(2,1)}, u32[]{:S(2)}, u32[]{:S(2)}) collective-permute-start(bf16[256,512]{1,0:T(8,128)(2,1)S(1)} %shard_map.59), channel_id=1, source_target_pairs={{0,64},{1,65},{2,66},{3,67},{4,68},{5,69},{6,70},{7,71},{8,72},{9,... | collective-permute-start | bytes 786440 | tf_op jit(solution)/shard_map/ppermute | solution.py:40
  60.9 0.0 copy-start.1
  61.0 1.1 copy-done.1
  62.1 0.0 copy-start.2
  62.1 0.6 shard_map.58.keep_ref
  62.7 3.0 %collective-permute-done.near_ref = bf16[256,512]{1,0:T(8,128)(2,1)} collective-permute-done((bf16[256,512]{1,0:T(8,128)(2,1)S(1)}, bf16[256,512]{1,0:T(8,128)(2,1)}, u32[]{:S(2)}, u32[]{:S(2)}) %collective-permute-start) | collective-permute-done | bytes 262176 | tf_op jit(solution)/shard_map/ppermute | solution.py:40
  65.7 0.0 copy-done.2
  65.7 1.0 shard_map.60
  66.7 24.6 %all-gather.1 = bf16[512,640]{1,0:T(8,128)(2,1)S(1)} all-gather(bf16[256,640]{1,0:T(8,128)(2,1)S(1)} %get-tuple-element.18), channel_id=3, replica_groups={{0,32},{1,33},{2,34},{3,35},{4,36},{5,37},{6,38},{7,39},{8,40},{9,41},{..., dimensions={0}, use_global_device_ids=true | all-gather | bytes 983040 | tf_op jit(solution)/shard_map/all_gather | solution.py:216
  91.4 0.2 shard_map.61.grad_ref
  91.6 2.4 %collective-permute-start.1 = (bf16[256,512]{1,0:T(8,128)(2,1)S(1)}, bf16[256,512]{1,0:T(8,128)(2,1)S(1)}, u32[]{:S(2)}, u32[]{:S(2)}) collective-permute-start(bf16[256,512]{1,0:T(8,128)(2,1)S(1)} %shard_map.61.grad_ref), channel_id=1, source_target_pairs={{0,64},{1,65},{2,66},{3,67},{4,68},{5,69},{6,70},{7,71},{8,72},{9,... | collective-permute-start | bytes 786440 | tf_op jit(solution)/shard_map/ppermute | solution.py:40
  94.0 0.7 shard_map.62.rest_0_
  94.7 4.2 %collective-permute-done.1.grad_ref = bf16[256,512]{1,0:T(8,128)(2,1)S(1)} collective-permute-done((bf16[256,512]{1,0:T(8,128)(2,1)S(1)}, bf16[256,512]{1,0:T(8,128)(2,1)S(1)}, u32[]{:S(2)}, u32[]{:S(2)}) %collective-permute-start.1) | collective-permute-done | bytes 262176 | tf_op jit(solution)/shard_map/ppermute | solution.py:40
  99.0 0.7 shard_map.63
  99.7 12.0 %all_to_all.38.pieces_ref = bf16[4,256,384]{2,1,0:T(8,128)(2,1)S(1)} all-to-all(bf16[4,256,384]{2,1,0:T(8,128)(2,1)S(1)} %shard_map.63), channel_id=1, replica_groups={{0,1,2,3},{4,5,6,7},{8,9,10,11},{12,13,14,15},{16,17,18,19},{20,21,22,2..., dimensions={0} | all-to-all | bytes 1572864 | tf_op jit(solution)/shard_map/all_to_all | solution.py:44
  111.7 0.1 shard_map.64
  111.8 25.0 %all_to_all.39 = bf16[8,32,384]{2,1,0:T(8,128)(2,1)S(1)} all-to-all(bf16[8,32,384]{2,1,0:T(8,128)(2,1)S(1)} %bitcast.25), channel_id=1, replica_groups=mesh['expert'=8,'tp'=128] {'expert'}, dimensions={0} | all-to-all | bytes 393216 | tf_op jit(solution)/shard_map/all_to_all | solution.py:44
  136.8 0.3 shard_map.65
  137.1 20.2 %all_to_all.40.part_ref = f32[8,24,128]{2,1,0:T(8,128)S(1)} all-to-all(f32[8,24,128]{2,1,0:T(8,128)S(1)} %shard_map.65), channel_id=1, replica_groups={{0,4,8,12,16,20,24,28},{1,5,9,13,17,21,25,29},{2,6,10,14,18,22,26,30},{..., dimensions={0} | all-to-all | bytes 196608 | tf_op jit(solution)/shard_map/all_to_all | solution.py:44
  157.3 0.7 shard_map.66
Async XLA Ops:
  0.0 0.7 copy-start.3
  1.4 26.0 %all-to-all-start = ((bf16[8,16,192]{2,1,0:T(8,128)(2,1)}), bf16[8,16,192]{2,1,0:T(8,128)(2,1)S(1)}, u32[]{:S(2)}, u32[]{:S(2)}) async-start(bf16[8,16,192]{2,1,0:T(8,128)(2,1)} %shard_map.55), calls=%async_computation | async-start | bytes 131072 | tf_op jit(solution)/shard_map/all_to_all | solution.py:44
  28.4 17.8 %all-to-all-start.1 = ((bf16[8,32,384]{2,1,0:T(8,128)(2,1)}), bf16[8,32,384]{2,1,0:T(8,128)(2,1)S(1)}, u32[]{:S(2)}, u32[]{:S(2)}) async-start(bf16[8,32,384]{2,1,0:T(8,128)(2,1)} %bitcast.4), calls=%async_computation.1 | async-start | bytes 393216 | tf_op jit(solution)/shard_map/all_to_all | solution.py:44
  57.6 0.9 copy-start
  58.5 7.2 %collective-permute-start = (bf16[256,512]{1,0:T(8,128)(2,1)S(1)}, bf16[256,512]{1,0:T(8,128)(2,1)}, u32[]{:S(2)}, u32[]{:S(2)}) collective-permute-start(bf16[256,512]{1,0:T(8,128)(2,1)S(1)} %shard_map.59), channel_id=1, source_target_pairs={{0,64},{1,65},{2,66},{3,67},{4,68},{5,69},{6,70},{7,71},{8,72},{9,... | collective-permute-start | bytes 786440 | tf_op jit(solution)/shard_map/ppermute | solution.py:40
  60.9 1.1 copy-start.1
  62.1 3.6 %copy-start.2 = (bf16[1,256,128]{2,1,0:T(8,128)(2,1)S(1)}, bf16[1,256,128]{2,1,0:T(8,128)(2,1)}, u32[]{:S(2)}) copy-start(bf16[1,256,128]{2,1,0:T(8,128)(2,1)} %param.9) | copy-start | bytes 196612
  91.6 7.4 %collective-permute-start.1 = (bf16[256,512]{1,0:T(8,128)(2,1)S(1)}, bf16[256,512]{1,0:T(8,128)(2,1)S(1)}, u32[]{:S(2)}, u32[]{:S(2)}) collective-permute-start(bf16[256,512]{1,0:T(8,128)(2,1)S(1)} %shard_map.61.grad_ref), channel_id=1, source_target_pairs={{0,64},{1,65},{2,66},{3,67},{4,68},{5,69},{6,70},{7,71},{8,72},{9,... | collective-permute-start | bytes 786440 | tf_op jit(solution)/shard_map/ppermute | solution.py:40

commit v4 on v3

--- a/solution.py
+++ b/solution.py
@@ -9,13 +9,10 @@
 
 NX, NZL = 4, 8
 X_GROUPS = [[b * NX + x for x in range(NX)] for b in range(32)]
-ZH_GROUPS = [
-    [y * 64 + zh * 32 + f for zh in range(2)] for y in range(2) for f in range(32)
-]
 ZL_GROUPS = [
     [hi * 32 + zl * NX + x for zl in range(NZL)] for hi in range(4) for x in range(NX)
 ]
-Y_BIT = 64
+Y_BIT, ZH_BIT = 64, 32
 F32, BF16 = jnp.float32, jnp.bfloat16
 NT = (((1,), (1,)), ((), ()))
 TN = (((0,), (0,)), ((), ()))
@@ -89,28 +86,28 @@
     return pl.ds(own, width), pl.ds(other, width)
 
 
-def forward_kernel(y_ref, rows_ref, gate_ref, up_ref, out_ref, *, mine):
+def forward_kernel(y_ref, rows_ref, gate_ref, up_ref, *out_refs, mine):
     width = gate_ref.shape[1] // 2
     at = halves(y_ref, width)[0 if mine else 1]
+    part = out_refs[0].shape[0]
     rows = jnp.concatenate([rows_ref[x] for x in range(rows_ref.shape[0])], axis=1)
     for m, w_ref in enumerate((gate_ref, up_ref)):
-        out_ref[:, m * width : (m + 1) * width] = dot(rows, w_ref[:, at]).astype(out_ref.dtype)
-
-
-def near_kernel(keep_ref, near_ref, hid_ref, total_ref, send_ref):
-    total = keep_ref[...] + near_ref[...].astype(F32)
-    width = total.shape[1]
-    total_ref[...] = total
-    send_ref[:, :width] = total.astype(BF16)
-    send_ref[:, width:] = hid_ref[...]
-
-
-def grad_kernel(zh_ref, total_ref, both_ref, out_ref):
-    width = total_ref.shape[1]
-    hid = width // 4
-    total = total_ref[...] + both_ref[1 - zh_ref[0], :, :width].astype(F32)
+        out = dot(rows, w_ref[:, at])
+        for c, out_ref in enumerate(out_refs):
+            out_ref[:, m * width : (m + 1) * width] = out[c * part : (c + 1) * part].astype(out_ref.dtype)
+
+
+def near_kernel(keep_ref, near_ref, send_ref):
+    send_ref[...] = (keep_ref[...] + near_ref[...].astype(F32)).astype(BF16)
+
+
+def grad_kernel(zh_ref, keep_ref, near_ref, got_ref, hid_ref, far_ref, out_ref, *, chunk):
+    rows, hid = keep_ref.shape[0], hid_ref.shape[1]
+    total = keep_ref[...] + near_ref[...].astype(F32) + got_ref[...].astype(F32)
+    at = slice(chunk * rows, (chunk + 1) * rows)
+    own, far = hid_ref[at].astype(F32), far_ref[at].astype(F32)
     for j in range(2):
-        upstream = both_ref[j, :, width:].astype(F32)
+        upstream = jnp.where(zh_ref[0] == j, own, far)
         gate_pre = total[:, j * hid : (j + 1) * hid]
         up_pre = total[:, (2 + j) * hid : (3 + j) * hid]
         sig = jax.nn.sigmoid(gate_pre)
@@ -119,18 +116,32 @@
         out_ref[:, (2 + j) * hid : (3 + j) * hid] = (upstream * gate_pre * sig).astype(BF16)
 
 
-def backward_kernel(y_ref, grad_ref, gate_ref, up_ref, *rest, mine):
-    out_ref = rest[-1]
+def backward(y_ref, grad_ref, gate_ref, up_ref, x, wide, mine):
     width = gate_ref.shape[1] // 2
     at = halves(y_ref, width)[0 if mine else 1]
-    wide = out_ref.shape[2]
+    r = slice(x * wide, (x + 1) * wide)
+    return dot(grad_ref[:, :width], gate_ref[r, at], NT) + dot(grad_ref[:, width:], up_ref[r, at], NT)
+
+
+def backward_first_kernel(y_ref, own_ref, other_ref, gate_ref, up_ref, out_ref):
+    weights = gate_ref, up_ref
     for x in range(out_ref.shape[0]):
-        r = slice(x * wide, (x + 1) * wide)
-        total = dot(grad_ref[:, :width], gate_ref[r, at], NT)
-        total = total + dot(grad_ref[:, width:], up_ref[r, at], NT)
-        if not mine:
-            total = total + rest[0][x]
-        out_ref[x] = total.astype(out_ref.dtype)
+        total = backward(y_ref, own_ref, *weights, x, out_ref.shape[2], True)
+        total = total + backward(y_ref, other_ref, *weights, x, out_ref.shape[2], False)
+        out_ref[x] = total.astype(BF16)
+
+
+def backward_own_kernel(y_ref, own_ref, gate_ref, up_ref, out_ref):
+    for x in range(out_ref.shape[0]):
+        out_ref[x] = backward(y_ref, own_ref, gate_ref, up_ref, x, out_ref.shape[2], True)
+
+
+def backward_last_kernel(y_ref, other_ref, gate_ref, up_ref, held_ref, first_ref, out_ref):
+    rows = first_ref.shape[1]
+    for x in range(out_ref.shape[0]):
+        total = held_ref[x] + backward(y_ref, other_ref, gate_ref, up_ref, x, out_ref.shape[2], False)
+        out_ref[x, :rows] = first_ref[x]
+        out_ref[x, rows:] = total.astype(BF16)
 
 
 def sum_kernel(pieces_ref, out_ref):
@@ -185,62 +196,73 @@
 
     outgoing = call(dispatch_kernel, shape((slot_total, wide), BF16), [], [slot_index, raw])
     arrived = over("expert", outgoing)
-    arrived, gate, up = lax.optimization_barrier((arrived, gate, up))
+    hidden = hidden_grad[0]
+    hidden_far = swapped(hidden, ZH_BIT)
+    arrived, gate, up, hidden_far = lax.optimization_barrier((arrived, gate, up, hidden_far))
     rows = lax.all_gather(arrived, "tp", axis_index_groups=X_GROUPS, axis=0, tiled=False)
 
     n_flops = 2 * slot_total * block_rows * half
+    part = slot_total // 2
     given = [rows, gate, up]
     send = call(
         functools.partial(forward_kernel, mine=False),
-        shape((slot_total, half), BF16),
+        [shape((part, half), BF16)] * 2,
         [y_at],
         given,
         n_flops,
         16,
     )
+    near = [swapped(v, Y_BIT) for v in send]
     keep = call(
         functools.partial(forward_kernel, mine=True),
-        shape((slot_total, half), F32),
+        [shape((part, half), F32)] * 2,
         [y_at],
         given,
         n_flops,
         16,
     )
-    near = swapped(send, Y_BIT)
-    total, send = call(
-        near_kernel,
-        [shape((slot_total, half), F32), shape((slot_total, half + hid), BF16)],
-        [],
-        [keep, near, hidden_grad[0]],
-    )
-    both = lax.all_gather(send, "tp", axis_index_groups=ZH_GROUPS, axis=0, tiled=False)
-
-    grads = call(grad_kernel, shape((slot_total, half), BF16), [zh_at], [total, both])
-    other = swapped(grads, Y_BIT)
-    pieces = (NX, slot_total, wide)
+    got = [
+        swapped(call(near_kernel, shape((part, half), BF16), [], [k, n]), ZH_BIT)
+        for k, n in zip(keep, near)
+    ]
+
+    def gradients(c):
+        return call(
+            functools.partial(grad_kernel, chunk=c),
+            shape((part, half), BF16),
+            [zh_at],
+            [keep[c], near[c], got[c], hidden, hidden_far],
+        )
+
+    own = gradients(0)
+    first = call(
+        backward_first_kernel,
+        shape((NX, part, wide), BF16),
+        [y_at],
+        [own, swapped(own, Y_BIT), gate, up],
+        n_flops,
+        16,
+    )
+    own = gradients(1)
+    other = swapped(own, Y_BIT)
     held = call(
-        functools.partial(backward_kernel, mine=True),
-        shape(pieces, F32),
-        [y_at],
-        [grads, gate, up],
-        n_flops,
-        16,
+        backward_own_kernel, shape((NX, part, wide), F32), [y_at], [own, gate, up], n_flops // 2, 16
     )
     pieces = call(
-        functools.partial(backward_kernel, mine=False),
-        shape(pieces, BF16),
-        [y_at],
-        [other, gate, up, held],
-        n_flops,
+        backward_last_kernel,
+        shape((NX, slot_total, wide), BF16),
+        [y_at],
+        [other, gate, up, held, first],
+        n_flops // 2,
         16,
     )
     pieces = over("tp", pieces, X_GROUPS)
     summed = call(sum_kernel, shape((slot_total, wide), BF16), [], [pieces])
     returned = over("expert", summed)
 
-    part = call(combine_kernel, shape((NZL, feat // 2, 2 * n_tok), F32), [], [slot_index, returned])
-    part = over("tp", part, ZL_GROUPS)
-    total = call(finish_kernel, shape((feat, n_tok), BF16), [], [part])
+    shares = call(combine_kernel, shape((NZL, feat // 2, 2 * n_tok), F32), [], [slot_index, returned])
+    shares = over("tp", shares, ZL_GROUPS)
+    total = call(finish_kernel, shape((feat, n_tok), BF16), [], [shares])
     return total.T
 
 

time: 160 us -> 169 us (1.056)
  starting transfers between devices: 30.3 us -> 60.7 us
  blocking collectives: 93.2 us -> 73.6 us
  waiting for transfers between devices: 20.8 us -> 7.13 us
  local copies, waits for them, and re-layouts: 5.66 us -> 13.8 us
  Pallas kernels: 6.77 us -> 9.82 us
    ppermute x2 -> x7, starting transfers between devices: 4.87 us -> 36.1 us  [swapped(): lax.ppermute(shard, 'tp', [(i, i ^ bit) for i in range(lax.axis_size('tp'...]
    all_gather x1 -> x0, blocking collectives: 24.6 us -> none  [body(): lax.all_gather(send, 'tp', axis_index_groups=ZH_GROUPS, axis=0, tiled=False)]
    all_to_all x2, waiting for transfers between devices: 13.5 us -> 1.56 us  [over(): lax.all_to_all(shard, axis, split_axis=0, concat_axis=0, axis_index_group...]
    unnamed x9 -> x23, local copies, waits for them, and re-layouts: 2.91 us -> 9.36 us
    all_to_all x3, blocking collectives: 57.1 us -> 62.3 us  [over(): lax.all_to_all(shard, axis, split_axis=0, concat_axis=0, axis_index_group...]
    pallas_call x12 -> x15, Pallas kernels: 6.77 us -> 9.82 us  [call(): pl.pallas_call(kernel, out_shape=outs, in_specs=[SMEM] * len(scalars) + [...]
    ppermute x2 -> x7, waiting for transfers between devices: 7.29 us -> 5.57 us  [swapped(): lax.ppermute(shard, 'tp', [(i, i ^ bit) for i in range(lax.axis_size('tp'...]
  transfers between devices with their start and end apart: 4 -> 9, of which waited for: 4 -> 3; matrix products, arithmetic and copies ran while one was open for 3% -> 4% of each run, Pallas kernels for 1% -> 4%
where the time goes in v4:
time: 169 us; the launch traced here: 166 us
  blocking collectives  73.6 us (44%)
  starting transfers between devices  60.7 us (36%)
  local copies, waits for them, and re-layouts  13.8 us (8%)
  Pallas kernels  9.82 us (6%)
  waiting for transfers between devices  7.13 us (4%)
    all_to_all x3, blocking collectives, over(): lax.all_to_all(shard, axis, split_axis=0, concat_axis=0, axis_index_group...  62.3 us
    ppermute x7, starting transfers between devices, swapped(): lax.ppermute(shard, 'tp', [(i, i ^ bit) for i in range(lax.axis_size('tp'...  36.1 us
    all_to_all x2, starting transfers between devices, over(): lax.all_to_all(shard, axis, split_axis=0, concat_axis=0, axis_index_group...  24.6 us
    all_gather x1, blocking collectives, body(): lax.all_gather(arrived, 'tp', axis_index_groups=X_GROUPS, axis=0, tiled=F...  11.4 us
    pallas_call x15, Pallas kernels, call(): pl.pallas_call(kernel, out_shape=outs, in_specs=[SMEM] * len(scalars) + [...  9.82 us
    unnamed x23, local copies, waits for them, and re-layouts  9.36 us
    ppermute x7, waiting for transfers between devices, swapped(): lax.ppermute(shard, 'tp', [(i, i ^ bit) for i in range(lax.axis_size('tp'...  5.57 us
    another operation x1, local copies, waits for them, and re-layouts, body(): flat = [w[0, 0].reshape(block_rows, half) for w in (w_gate, w_up)]  4.06 us
  transfers between devices with their start and end apart: 9, of which 3 were waited for; matrix products, arithmetic and copies ran while one was open for 4% of the time, Pallas kernels for 4%

profile of v4, /device:TPU:1, one launch (start us, length us, event | category | flops | bytes accessed | tf_op | source)
XLA Modules:
  0.0 166.4 jit_solution(5720007921839136544)
XLA Ops:
  0.0 0.7 copy-done.10
  0.7 0.7 shard_map.55
  1.4 16.3 %all-to-all-start = ((bf16[8,16,192]{2,1,0:T(8,128)(2,1)}), bf16[8,16,192]{2,1,0:T(8,128)(2,1)S(1)}, u32[]{:S(2)}, u32[]{:S(2)}) async-start(bf16[8,16,192]{2,1,0:T(8,128)(2,1)} %shard_map.55), calls=%async_computation | async-start | bytes 131072 | tf_op jit(solution)/shard_map/all_to_all | solution.py:41
  17.7 11.6 %collective-permute-start = (bf16[256,128]{1,0:T(8,128)(2,1)}, bf16[256,128]{1,0:T(8,128)(2,1)S(1)}, u32[]{:S(2)}, u32[]{:S(2)}) collective-permute-start(bf16[256,128]{1,0:T(8,128)(2,1)} %bitcast.24), channel_id=1, source_target_pairs={{0,32},{1,33},{2,34},{3,35},{4,36},{5,37},{6,38},{7,39},{8,40},{9,... | collective-permute-start | bytes 196616 | tf_op jit(solution)/shard_map/ppermute | solution.py:37
  29.2 0.8 copy.8
  30.0 0.1 eq.15
  30.1 0.1 fusion
  30.2 0.2 reduce_window_sum.11
  30.4 0.2 select_reduce_fusion
  30.6 0.1 reduce_sum.12
  30.8 0.7 add_bitcast_fusion.slot_ref
  31.5 1.0 shard_map.56
  32.5 8.3 %all-to-all-start.1 = ((bf16[8,32,384]{2,1,0:T(8,128)(2,1)}), bf16[8,32,384]{2,1,0:T(8,128)(2,1)S(1)}, u32[]{:S(2)}, u32[]{:S(2)}) async-start(bf16[8,32,384]{2,1,0:T(8,128)(2,1)} %bitcast.4), calls=%async_computation.1 | async-start | bytes 393216 | tf_op jit(solution)/shard_map/all_to_all | solution.py:41
  40.8 4.1 %copy_bitcast_fusion = (bf16[1536,512]{1,0:T(8,128)(2,1)}, bf16[1536,512]{1,0:T(8,128)(2,1)}) fusion(bf16[192,8,4,128]{3,2,1,0:T(4,128)(2,1)} %bitcast.28, bf16[192,8,4,128]{3,2,1,0:T(4,128)(2,1)} %bitcast.29), kind=kLoop, calls=%fused_computation | loop fusion | bytes 6291456 | tf_op jit(solution)/shard_map/reshape;squeeze | solution.py:185
  44.9 1.4 copy-done
  46.3 1.4 copy-done.1
  47.7 0.2 shard_map.57
  47.9 1.6 all-to-all-done.1
  49.5 11.4 %all-gather = bf16[1024,384]{1,0:T(8,128)(2,1)S(1)} all-gather(bf16[256,384]{1,0:T(8,128)(2,1)S(1)} %bitcast.30), channel_id=2, replica_groups={{0,1,2,3},{4,5,6,7},{8,9,10,11},{12,13,14,15},{16,17,18,19},{20,21,22,2..., dimensions={0}, use_global_device_ids=true | all-gather | bytes 983040 | tf_op jit(solution)/shard_map/all_gather | solution.py:202
  60.8 0.6 shard_map.59
  61.4 2.5 %collective-permute-start.4 = (bf16[128,512]{1,0:T(8,128)(2,1)S(1)}, bf16[128,512]{1,0:T(8,128)(2,1)S(1)}, u32[]{:S(2)}, u32[]{:S(2)}) collective-permute-start(bf16[128,512]{1,0:T(8,128)(2,1)S(1)} %get-tuple-element.24), channel_id=1, source_target_pairs={{0,64},{1,65},{2,66},{3,67},{4,68},{5,69},{6,70},{7,71},{8,72},{9,... | collective-permute-start | bytes 393224 | tf_op jit(solution)/shard_map/ppermute | solution.py:37
  63.9 2.8 %collective-permute-start.1 = (bf16[128,512]{1,0:T(8,128)(2,1)S(1)}, bf16[128,512]{1,0:T(8,128)(2,1)S(1)}, u32[]{:S(2)}, u32[]{:S(2)}) collective-permute-start(bf16[128,512]{1,0:T(8,128)(2,1)S(1)} %get-tuple-element.21), channel_id=1, source_target_pairs={{0,64},{1,65},{2,66},{3,67},{4,68},{5,69},{6,70},{7,71},{8,72},{9,... | collective-permute-start | bytes 393224 | tf_op jit(solution)/shard_map/ppermute | solution.py:37
  66.7 0.6 shard_map.58
  67.3 0.7 shard_map.63
  68.0 0.7 copy-done.2
  68.7 8.3 %collective-permute-start.5 = (bf16[128,512]{1,0:T(8,128)(2,1)}, bf16[128,512]{1,0:T(8,128)(2,1)}, u32[]{:S(2)}, u32[]{:S(2)}) collective-permute-start(bf16[128,512]{1,0:T(8,128)(2,1)} %shard_map.63), channel_id=1, source_target_pairs={{0,32},{1,33},{2,34},{3,35},{4,36},{5,37},{6,38},{7,39},{8,40},{9,... | collective-permute-start | bytes 393224 | tf_op jit(solution)/shard_map/ppermute | solution.py:37
  77.1 0.7 shard_map.60
  77.8 5.6 %collective-permute-start.2 = (bf16[128,512]{1,0:T(8,128)(2,1)}, bf16[128,512]{1,0:T(8,128)(2,1)}, u32[]{:S(2)}, u32[]{:S(2)}) collective-permute-start(bf16[128,512]{1,0:T(8,128)(2,1)} %shard_map.60), channel_id=1, source_target_pairs={{0,32},{1,33},{2,34},{3,35},{4,36},{5,37},{6,38},{7,39},{8,40},{9,... | collective-permute-start | bytes 393224 | tf_op jit(solution)/shard_map/ppermute | solution.py:37
  83.4 4.4 %collective-permute-done.5.got_ref = bf16[128,512]{1,0:T(8,128)(2,1)} collective-permute-done((bf16[128,512]{1,0:T(8,128)(2,1)}, bf16[128,512]{1,0:T(8,128)(2,1)}, u32[]{:S(2)}, u32[]{:S(2)}) %collective-permute-start.5) | collective-permute-done | bytes 131104 | tf_op jit(solution)/shard_map/ppermute | solution.py:37
  87.8 0.9 copy-done.3
  88.8 0.9 copy-done.5
  89.7 0.8 copy-done.6
  90.5 0.8 copy-done.8
  91.3 1.0 shard_map.64.own_ref
  92.4 2.5 %collective-permute-start.6 = (bf16[128,512]{1,0:T(8,128)(2,1)S(1)}, bf16[128,512]{1,0:T(8,128)(2,1)S(1)}, u32[]{:S(2)}, u32[]{:S(2)}) collective-permute-start(bf16[128,512]{1,0:T(8,128)(2,1)S(1)} %shard_map.64.own_ref), channel_id=1, source_target_pairs={{0,64},{1,65},{2,66},{3,67},{4,68},{5,69},{6,70},{7,71},{8,72},{9,... | collective-permute-start | bytes 393224 | tf_op jit(solution)/shard_map/ppermute | solution.py:37
  94.8 0.8 copy-done.9
  95.7 1.0 shard_map.61.own_ref
  96.7 2.8 %collective-permute-start.3 = (bf16[128,512]{1,0:T(8,128)(2,1)S(1)}, bf16[128,512]{1,0:T(8,128)(2,1)S(1)}, u32[]{:S(2)}, u32[]{:S(2)}) collective-permute-start(bf16[128,512]{1,0:T(8,128)(2,1)S(1)} %shard_map.61.own_ref), channel_id=1, source_target_pairs={{0,64},{1,65},{2,66},{3,67},{4,68},{5,69},{6,70},{7,71},{8,72},{9,... | collective-permute-start | bytes 393224 | tf_op jit(solution)/shard_map/ppermute | solution.py:37
  99.5 0.6 shard_map.62.held_ref
  100.2 1.1 shard_map.65.first_ref
  101.2 1.2 collective-permute-done.3.other_ref
  102.4 0.6 shard_map.66
  103.0 12.8 %all_to_all.38.pieces_ref = bf16[4,256,384]{2,1,0:T(8,128)(2,1)S(1)} all-to-all(bf16[4,256,384]{2,1,0:T(8,128)(2,1)S(1)} %shard_map.66), channel_id=1, replica_groups={{0,1,2,3},{4,5,6,7},{8,9,10,11},{12,13,14,15},{16,17,18,19},{20,21,22,2..., dimensions={0} | all-to-all | bytes 1572864 | tf_op jit(solution)/shard_map/all_to_all | solution.py:41
  115.9 0.1 shard_map.67
  116.0 21.8 %all_to_all.39 = bf16[8,32,384]{2,1,0:T(8,128)(2,1)S(1)} all-to-all(bf16[8,32,384]{2,1,0:T(8,128)(2,1)S(1)} %bitcast.23), channel_id=1, replica_groups=mesh['expert'=8,'tp'=128] {'expert'}, dimensions={0} | all-to-all | bytes 393216 | tf_op jit(solution)/shard_map/all_to_all | solution.py:41
  137.8 0.3 shard_map.68
  138.1 27.6 %all_to_all.40.part_ref = f32[8,24,128]{2,1,0:T(8,128)S(1)} all-to-all(f32[8,24,128]{2,1,0:T(8,128)S(1)} %shard_map.68), channel_id=1, replica_groups={{0,4,8,12,16,20,24,28},{1,5,9,13,17,21,25,29},{2,6,10,14,18,22,26,30},{..., dimensions={0} | all-to-all | bytes 196608 | tf_op jit(solution)/shard_map/all_to_all | solution.py:41
  165.7 0.7 shard_map.69
  (20 shorter events, 0.1 us)
Async XLA Ops:
  0.0 0.7 copy-start.10
  1.4 30.1 %all-to-all-start = ((bf16[8,16,192]{2,1,0:T(8,128)(2,1)}), bf16[8,16,192]{2,1,0:T(8,128)(2,1)S(1)}, u32[]{:S(2)}, u32[]{:S(2)}) async-start(bf16[8,16,192]{2,1,0:T(8,128)(2,1)} %shard_map.55), calls=%async_computation | async-start | bytes 131072 | tf_op jit(solution)/shard_map/all_to_all | solution.py:41
  17.7 30.2 %collective-permute-start = (bf16[256,128]{1,0:T(8,128)(2,1)}, bf16[256,128]{1,0:T(8,128)(2,1)S(1)}, u32[]{:S(2)}, u32[]{:S(2)}) collective-permute-start(bf16[256,128]{1,0:T(8,128)(2,1)} %bitcast.24), channel_id=1, source_target_pairs={{0,32},{1,33},{2,34},{3,35},{4,36},{5,37},{6,38},{7,39},{8,40},{9,... | collective-permute-start | bytes 196616 | tf_op jit(solution)/shard_map/ppermute | solution.py:37
  32.5 17.0 %all-to-all-start.1 = ((bf16[8,32,384]{2,1,0:T(8,128)(2,1)}), bf16[8,32,384]{2,1,0:T(8,128)(2,1)S(1)}, u32[]{:S(2)}, u32[]{:S(2)}) async-start(bf16[8,32,384]{2,1,0:T(8,128)(2,1)} %bitcast.4), calls=%async_computation.1 | async-start | bytes 393216 | tf_op jit(solution)/shard_map/all_to_all | solution.py:41
  44.9 1.4 copy-start
  46.3 1.4 copy-start.1
  47.9 13.5 %copy-start.7 = (bf16[256,128]{1,0:T(8,128)(2,1)}, bf16[256,128]{1,0:T(8,128)(2,1)S(1)}, u32[]{:S(2)}) copy-start(bf16[256,128]{1,0:T(8,128)(2,1)S(1)} %collective-permute-done.far_ref) | copy-start | bytes 196612
  61.4 5.9 %collective-permute-start.4 = (bf16[128,512]{1,0:T(8,128)(2,1)S(1)}, bf16[128,512]{1,0:T(8,128)(2,1)S(1)}, u32[]{:S(2)}, u32[]{:S(2)}) collective-permute-start(bf16[128,512]{1,0:T(8,128)(2,1)S(1)} %get-tuple-element.24), channel_id=1, source_target_pairs={{0,64},{1,65},{2,66},{3,67},{4,68},{5,69},{6,70},{7,71},{8,72},{9,... | collective-permute-start | bytes 393224 | tf_op jit(solution)/shard_map/ppermute | solution.py:37
  63.9 13.2 %collective-permute-start.1 = (bf16[128,512]{1,0:T(8,128)(2,1)S(1)}, bf16[128,512]{1,0:T(8,128)(2,1)S(1)}, u32[]{:S(2)}, u32[]{:S(2)}) collective-permute-start(bf16[128,512]{1,0:T(8,128)(2,1)S(1)} %get-tuple-element.21), channel_id=1, source_target_pairs={{0,64},{1,65},{2,66},{3,67},{4,68},{5,69},{6,70},{7,71},{8,72},{9,... | collective-permute-start | bytes 393224 | tf_op jit(solution)/shard_map/ppermute | solution.py:37
  67.3 9.8 %copy-start.4 = (bf16[128,512]{1,0:T(8,128)(2,1)}, bf16[128,512]{1,0:T(8,128)(2,1)S(1)}, u32[]{:S(2)}) copy-start(bf16[128,512]{1,0:T(8,128)(2,1)S(1)} %collective-permute-done.4.near_ref) | copy-start | bytes 393220
  68.0 0.7 copy-start.2
  68.7 19.1 %collective-permute-start.5 = (bf16[128,512]{1,0:T(8,128)(2,1)}, bf16[128,512]{1,0:T(8,128)(2,1)}, u32[]{:S(2)}, u32[]{:S(2)}) collective-permute-start(bf16[128,512]{1,0:T(8,128)(2,1)} %shard_map.63), channel_id=1, source_target_pairs={{0,32},{1,33},{2,34},{3,35},{4,36},{5,37},{6,38},{7,39},{8,40},{9,... | collective-permute-start | bytes 393224 | tf_op jit(solution)/shard_map/ppermute | solution.py:37
  77.8 17.1 %collective-permute-start.2 = (bf16[128,512]{1,0:T(8,128)(2,1)}, bf16[128,512]{1,0:T(8,128)(2,1)}, u32[]{:S(2)}, u32[]{:S(2)}) collective-permute-start(bf16[128,512]{1,0:T(8,128)(2,1)} %shard_map.60), channel_id=1, source_target_pairs={{0,32},{1,33},{2,34},{3,35},{4,36},{5,37},{6,38},{7,39},{8,40},{9,... | collective-permute-start | bytes 393224 | tf_op jit(solution)/shard_map/ppermute | solution.py:37
  87.8 1.0 copy-start.3
  88.8 0.9 copy-start.5
  89.7 0.8 copy-start.6
  90.5 0.8 copy-start.8
  92.4 7.8 %collective-permute-start.6 = (bf16[128,512]{1,0:T(8,128)(2,1)S(1)}, bf16[128,512]{1,0:T(8,128)(2,1)S(1)}, u32[]{:S(2)}, u32[]{:S(2)}) collective-permute-start(bf16[128,512]{1,0:T(8,128)(2,1)S(1)} %shard_map.64.own_ref), channel_id=1, source_target_pairs={{0,64},{1,65},{2,66},{3,67},{4,68},{5,69},{6,70},{7,71},{8,72},{9,... | collective-permute-start | bytes 393224 | tf_op jit(solution)/shard_map/ppermute | solution.py:37
  94.8 0.8 copy-start.9
  96.7 5.7 %collective-permute-start.3 = (bf16[128,512]{1,0:T(8,128)(2,1)S(1)}, bf16[128,512]{1,0:T(8,128)(2,1)S(1)}, u32[]{:S(2)}, u32[]{:S(2)}) collective-permute-start(bf16[128,512]{1,0:T(8,128)(2,1)S(1)} %shard_map.61.own_ref), channel_id=1, source_target_pairs={{0,64},{1,65},{2,66},{3,67},{4,68},{5,69},{6,70},{7,71},{8,72},{9,... | collective-permute-start | bytes 393224 | tf_op jit(solution)/shard_map/ppermute | solution.py:37

commit v5 on v3

v5 whole, which is shorter than its diff:
```python
import functools

import jax
import jax.numpy as jnp
from jax import lax
from jax.experimental import pallas as pl
from jax.experimental.pallas import tpu as pltpu
from jax.sharding import PartitionSpec as P

NK, NM = 4, 8
FEW, TILE = 16, 128


def groups(bits, count=128):
    mask = sum(1 << b for b in bits)
    spread = [sum(((k >> i) & 1) << b for i, b in enumerate(bits)) for k in range(1 << len(bits))]
    return [[base | v for v in spread] for base in range(count) if not base & mask]


M_GROUPS, K_GROUPS, ZH_GROUPS = groups((0, 1, 2)), groups((3, 4)), groups((5,))
Y_BIT = 64
F32, BF16 = jnp.float32, jnp.bfloat16
NT = (((1,), (1,)), ((), ()))
TN = (((0,), (0,)), ((), ()))
VMEM = pl.BlockSpec(memory_space=pltpu.VMEM)
SMEM = pl.BlockSpec(memory_space=pltpu.SMEM)


def call(kernel, outs, scalars, arrays, flops=0, mib=6):
    several = isinstance(outs, (tuple, list))
    moved = sum(v.size * v.dtype.itemsize for v in [*arrays, *(outs if several else [outs])])
    return pl.pallas_call(
        kernel,
        out_shape=outs,
        in_specs=[SMEM] * len(scalars) + [VMEM] * len(arrays),
        out_specs=[VMEM] * len(outs) if several else VMEM,
        compiler_params=pltpu.CompilerParams(vmem_limit_bytes=mib * 1024 * 1024),
        cost_estimate=pl.CostEstimate(flops=flops, bytes_accessed=moved, transcendentals=0),
    )(*scalars, *arrays)


def swapped(shard, bit):
    return lax.ppermute(shard, "tp", [(i, i ^ bit) for i in range(lax.axis_size("tp"))])


def over(axis, shard, groups=None):
    return lax.all_to_all(
        shard, axis, split_axis=0, concat_axis=0, axis_index_groups=groups, tiled=True
    )


def dot(a, b, dims=(((1,), (0,)), ((), ()))):
    return lax.dot_general(a, b, dims, preferred_element_type=F32)


def pack_kernel(tok_ref, out_ref):
    turned = tok_ref[...]
    third = turned.shape[0] // 3
    packed = jnp.concatenate([turned[j * third : (j + 1) * third] for j in range(3)], axis=1)
    for z in range(out_ref.shape[0]):
        out_ref[z] = packed


def arrange_kernel(gate_ref, up_ref, gate_out_ref, up_out_ref):
    feat = gate_ref.shape[0] // (NM * NK)
    for m in range(NM):
        for k in range(NK):
            src, dst = (k * NM + m) * feat, (m * NK + k) * feat
            gate_out_ref[dst : dst + feat] = gate_ref[src : src + feat]
            up_out_ref[dst : dst + feat] = up_ref[src : src + feat]


def one_hot(slot_ref, half):
    shape = (TILE, slot_ref.shape[1])
    row = lax.broadcasted_iota(jnp.int32, shape, 0)
    slots = jnp.right_shift(row, 4) * (2 * FEW) + half * FEW + jnp.bitwise_and(row, FEW - 1)
    hit = (slots == slot_ref[0:1, :]) | (slots == slot_ref[1:2, :])
    return jnp.where(hit, 1.0, 0.0).astype(BF16)


def dispatch_kernel(slot_ref, raw_ref, out_ref):
    n_tok = slot_ref.shape[1]
    pieces = [
        raw_ref[k, :, j * n_tok : (j + 1) * n_tok] for k in range(raw_ref.shape[0]) for j in range(3)
    ]
    raw = jnp.concatenate(pieces, axis=0)
    out = [dot(one_hot(slot_ref, h), raw, NT) for h in range(2)]
    out_ref[...] = jnp.concatenate(out, axis=1).astype(BF16)


def copies_kernel(in_ref, out_ref):
    for m in range(out_ref.shape[0]):
        out_ref[m] = in_ref[...]


def halves(y_ref, width):
    own = pl.multiple_of(y_ref[0] * width, width)
    other = pl.multiple_of((1 - y_ref[0]) * width, width)
    return pl.ds(own, width), pl.ds(other, width)


def forward_kernel(y_ref, rows_ref, gate_ref, up_ref, out_ref, *, mine):
    width = gate_ref.shape[1] // 2
    at = halves(y_ref, width)[0 if mine else 1]
    wide = rows_ref.shape[2] // 2
    rows = [
        jnp.concatenate([rows_ref[m, :, h * wide : (h + 1) * wide] for m in range(NM)], axis=1)
        for h in range(2)
    ]
    rows = jnp.concatenate(rows, axis=0)
    for m, w_ref in enumerate((gate_ref, up_ref)):
        out_ref[:, m * width : (m + 1) * width] = dot(rows, w_ref[:, at]).astype(out_ref.dtype)


def near_kernel(keep_ref, near_ref, hid_ref, send_ref):
    width = keep_ref.shape[1]
    send_ref[:, :width] = (keep_ref[...] + near_ref[...].astype(F32)).astype(BF16)
    for h in range(2):
        for source in range(TILE // FEW):
            src, dst = (2 * source + h) * FEW, h * TILE + source * FEW
            send_ref[dst : dst + FEW, width:] = hid_ref[src : src + FEW]


def grad_kernel(zh_ref, keep_ref, near_ref, both_ref, out_ref):
    width = keep_ref.shape[1]
    hid = width // 4
    total = keep_ref[...] + near_ref[...].astype(F32)
    total = total + both_ref[1 - zh_ref[0], :, :width].astype(F32)
    for j in range(2):
        upstream = both_ref[j, :, width:].astype(F32)
        gate_pre = total[:, j * hid : (j + 1) * hid]
        up_pre = total[:, (2 + j) * hid : (3 + j) * hid]
        sig = jax.nn.sigmoid(gate_pre)
        gate_grad = upstream * up_pre * sig * (1.0 + gate_pre * (1.0 - sig))
        out_ref[:, j * hid : (j + 1) * hid] = gate_grad.astype(BF16)
        out_ref[:, (2 + j) * hid : (3 + j) * hid] = (upstream * gate_pre * sig).astype(BF16)


def backward(y_ref, grad_ref, gate_ref, up_ref, pair, mine):
    width = gate_ref.shape[1] // 2
    at = halves(y_ref, width)[0 if mine else 1]
    wide = 2 * (gate_ref.shape[0] // NM)
    r = slice(pair * wide, (pair + 1) * wide)
    return dot(grad_ref[:, :width], gate_ref[r, at], NT) + dot(grad_ref[:, width:], up_ref[r, at], NT)


def backward_own_kernel(y_ref, grad_ref, gate_ref, up_ref, out_ref):
    for pair in range(NM // 2):
        out_ref[pair] = backward(y_ref, grad_ref, gate_ref, up_ref, pair, True)


def backward_other_kernel(y_ref, grad_ref, gate_ref, up_ref, held_ref, out_ref):
    wide = out_ref.shape[2] // 2
    for pair in range(NM // 2):
        total = held_ref[pair] + backward(y_ref, grad_ref, gate_ref, up_ref, pair, False)
        total = total.astype(BF16)
        for j in range(2):
            piece = [total[h * TILE : (h + 1) * TILE, j * wide : (j + 1) * wide] for h in range(2)]
            out_ref[2 * pair + j] = jnp.concatenate(piece, axis=1)


def sum_kernel(pieces_ref, out_ref):
    total = pieces_ref[0].astype(F32)
    for m in range(1, pieces_ref.shape[0]):
        total = total + pieces_ref[m].astype(F32)
    out_ref[...] = total.astype(BF16)


def combine_kernel(slot_ref, back_ref, out_ref):
    wide = back_ref.shape[1] // 2
    back = back_ref[...]
    part = dot(back, one_hot(slot_ref, 0), TN)[:wide] + dot(back, one_hot(slot_ref, 1), TN)[wide:]
    rows = out_ref.shape[1]
    for k in range(out_ref.shape[0]):
        low = part[2 * k * rows : (2 * k + 1) * rows]
        out_ref[k] = jnp.concatenate([low, part[(2 * k + 1) * rows : (2 * k + 2) * rows]], axis=1)


def finish_kernel(part_ref, out_ref):
    total = part_ref[0]
    for z in range(1, part_ref.shape[0]):
        total = total + part_ref[z]
    n_tok = out_ref.shape[1]
    out_ref[...] = jnp.concatenate([total[:, :n_tok], total[:, n_tok:]], axis=0).astype(BF16)


def body(tokens, routes, w_gate, w_up, hidden_grad):
    position = lax.axis_index("tp")
    y_at = jnp.bitwise_and(jnp.right_shift(position, 6), 1).reshape(1)
    zh_at = jnp.bitwise_and(jnp.right_shift(position, 5), 1).reshape(1)
    n_groups = lax.axis_size("expert")
    slot_total = hidden_grad.shape[1]
    capacity = slot_total // n_groups
    n_tok, feat = tokens.shape
    block_rows = w_gate.shape[2]
    hid = w_gate.shape[4]
    wide = NK * feat
    half = 4 * hid
    shape = jax.ShapeDtypeStruct

    flat = [w[0, 0].reshape(block_rows, half) for w in (w_gate, w_up)]
    gate, up = call(arrange_kernel, [shape((block_rows, half), BF16)] * 2, [], flat, mib=16)

    packed = call(pack_kernel, shape((NK, feat // 3, 3 * n_tok), BF16), [], [tokens.T])
    raw = over("tp", packed, K_GROUPS)

    flat_routes = routes.reshape(n_tok * 2)
    named = (flat_routes[:, None] == jnp.arange(n_groups, dtype=jnp.int32)[None, :]).astype(jnp.int32)
    before = jnp.cumsum(named, axis=0) - named
    slot_index = flat_routes * capacity + jnp.sum(before * named, axis=1)
    slot_index = slot_index.reshape(n_tok, 2).T

    outgoing = call(dispatch_kernel, shape((TILE, 2 * wide), BF16), [], [slot_index, raw])
    arrived = over("expert", outgoing)
    copies = call(copies_kernel, shape((NM, TILE, 2 * wide), BF16), [], [arrived])
    rows = over("tp", copies, M_GROUPS)

    n_flops = 2 * slot_total * block_rows * half
    given = [rows, gate, up]
    send = call(
        functools.partial(forward_kernel, mine=False),
        shape((slot_total, half), BF16),
        [y_at],
        given,
        n_flops,
        16,
    )
    keep = call(
        functools.partial(forward_kernel, mine=True),
        shape((slot_total, half), F32),
        [y_at],
        given,
        n_flops,
        16,
    )
    near = swapped(send, Y_BIT)
    send = call(
        near_kernel, shape((slot_total, half + hid), BF16), [], [keep, near, hidden_grad[0]]
    )
    both = lax.all_gather(send, "tp", axis_index_groups=ZH_GROUPS, axis=0, tiled=False)

    grads = call(grad_kernel, shape((slot_total, half), BF16), [zh_at], [keep, near, both])
    other = swapped(grads, Y_BIT)
    held = call(
        backward_own_kernel,
        shape((NM // 2, slot_total, 2 * wide), F32),
        [y_at],
        [grads, gate, up],
        n_flops,
        16,
    )
    pieces = call(
        backward_other_kernel,
        shape((NM, TILE, 2 * wide), BF16),
        [y_at],
        [other, gate, up, held],
        n_flops,
        16,
    )
    pieces = over("tp", pieces, M_GROUPS)
    summed = call(sum_kernel, shape((TILE, 2 * wide), BF16), [], [pieces])
    returned = over("expert", summed)

    part = call(combine_kernel, shape((NK, feat // 2, 2 * n_tok), F32), [], [slot_index, returned])
    part = over("tp", part, K_GROUPS)
    total = call(finish_kernel, shape((feat, n_tok), BF16), [], [part])
    return total.T


def solution(mesh):
    placed = (
        P("expert", "tp"),
        P("expert", None),
        P("expert", "tp", None, None, None),
        P("expert", "tp", None, None, None),
        P("expert", None, "tp"),
    )
    return jax.shard_map(
        body, mesh=mesh, in_specs=placed, out_specs=P("expert", "tp"), check_vma=False
    )
```

time: 160 us -> 163 us (1.019)
  blocking collectives: 93.2 us -> 102 us
  starting transfers between devices: 30.3 us -> 25.3 us
  local copies, waits for them, and re-layouts: 5.66 us -> 2.35 us
  Pallas kernels: 6.77 us -> 9.26 us
    all_to_all x3 -> x4, blocking collectives: 57.1 us -> 78.5 us  [over(): lax.all_to_all(shard, axis, split_axis=0, concat_axis=0, axis_index_group...]
    all_gather x1 -> x0, blocking collectives: 11.4 us -> none  [body(): lax.all_gather(arrived, 'tp', axis_index_groups=X_GROUPS, axis=0, tiled=F...]
    all_to_all x2, starting transfers between devices: 25.4 us -> 20.3 us  [over(): lax.all_to_all(shard, axis, split_axis=0, concat_axis=0, axis_index_group...]
    pallas_call x12 -> x13, Pallas kernels: 6.77 us -> 9.26 us  [call(): pl.pallas_call(kernel, out_shape=outs, in_specs=[SMEM] * len(scalars) + [...]
    another operation x1, local copies, waits for them, and re-layouts: 2.41 us -> 0.52 us  [body(): flat = [w[0, 0].reshape(block_rows, half) for w in (w_gate, w_up)]]
  transfers between devices with their start and end apart: 4 -> 4, of which waited for: 4 -> 4; matrix products, arithmetic and copies ran while one was open for 3% -> 2% of each run, Pallas kernels for 1% -> 2%
where the time goes in v5:
time: 163 us; the launch traced here: 162 us
  blocking collectives  102 us (63%)
  starting transfers between devices  25.3 us (16%)
  waiting for transfers between devices  22 us (13%)
  Pallas kernels  9.26 us (6%)
  local copies, waits for them, and re-layouts  2.35 us (1%)
    all_to_all x4, blocking collectives, over(): lax.all_to_all(shard, axis, split_axis=0, concat_axis=0, axis_index_group...  78.5 us
    all_gather x1, blocking collectives, body(): lax.all_gather(send, 'tp', axis_index_groups=ZH_GROUPS, axis=0, tiled=False)  23.2 us
    all_to_all x2, starting transfers between devices, over(): lax.all_to_all(shard, axis, split_axis=0, concat_axis=0, axis_index_group...  20.3 us
    all_to_all x2, waiting for transfers between devices, over(): lax.all_to_all(shard, axis, split_axis=0, concat_axis=0, axis_index_group...  14.8 us
    pallas_call x13, Pallas kernels, call(): pl.pallas_call(kernel, out_shape=outs, in_specs=[SMEM] * len(scalars) + [...  9.26 us
    ppermute x2, waiting for transfers between devices, swapped(): lax.ppermute(shard, 'tp', [(i, i ^ bit) for i in range(lax.axis_size('tp'...  7.21 us
    ppermute x2, starting transfers between devices, swapped(): lax.ppermute(shard, 'tp', [(i, i ^ bit) for i in range(lax.axis_size('tp'...  4.99 us
  transfers between devices with their start and end apart: 4, of which 4 were waited for; matrix products, arithmetic and copies ran while one was open for 2% of the time, Pallas kernels for 2%

profile of v5, /device:TPU:1, one launch (start us, length us, event | category | flops | bytes accessed | tf_op | source)
XLA Modules:
  0.0 162.0 jit_solution(6652557817755788338)
XLA Ops:
  0.0 0.0 copy-start.1
  0.0 0.7 copy-done.1
  0.7 0.7 shard_map.55
  1.4 14.4 %all-to-all-start = ((bf16[4,16,192]{2,1,0:T(8,128)(2,1)}), bf16[4,16,192]{2,1,0:T(8,128)(2,1)S(1)}, u32[]{:S(2)}, u32[]{:S(2)}) async-start(bf16[4,16,192]{2,1,0:T(8,128)(2,1)} %shard_map.55), calls=%async_computation | async-start | bytes 65536 | tf_op jit(solution)/shard_map/all_to_all | solution.py:47
  15.8 0.8 copy.8
  16.6 0.0 copy-start.3
  16.6 0.1 eq.15
  16.7 0.0 copy-start.2
  16.8 0.1 fusion
  16.8 0.2 reduce_window_sum.11
  17.0 0.2 select_reduce_fusion
  17.2 0.1 reduce_sum.12
  17.3 0.1 copy.9
  17.4 0.8 add_bitcast_fusion.slot_ref
  18.2 6.0 %all-to-all-done.raw_ref = bf16[4,16,192]{2,1,0:T(8,128)(2,1)S(1)} async-done(((bf16[4,16,192]{2,1,0:T(8,128)(2,1)}), bf16[4,16,192]{2,1,0:T(8,128)(2,1)S(1)}, u32[]{:S(2)}, u32[]{:S(2)}) %all-to-all-start) | async-done | bytes 24608 | tf_op jit(solution)/shard_map/all_to_all | solution.py:47
  24.3 0.3 shard_map.56
  24.6 16.7 %all_to_all.42 = bf16[8,16,384]{2,1,0:T(8,128)(2,1)S(1)} all-to-all(bf16[8,16,384]{2,1,0:T(8,128)(2,1)S(1)} %bitcast.22), channel_id=1, replica_groups=mesh['expert'=8,'tp'=128] {'expert'}, dimensions={0} | all-to-all | bytes 196608 | tf_op jit(solution)/shard_map/all_to_all | solution.py:47
  41.3 1.0 shard_map.57
  42.2 5.8 %all-to-all-start.2 = ((bf16[8,128,384]{2,1,0:T(8,128)(2,1)}), bf16[8,128,384]{2,1,0:T(8,128)(2,1)}, u32[]{:S(2)}, u32[]{:S(2)}) async-start(bf16[8,128,384]{2,1,0:T(8,128)(2,1)} %shard_map.57), calls=%async_computation.2 | async-start | bytes 1572864 | tf_op jit(solution)/shard_map/all_to_all | solution.py:47
  48.0 0.0 copy-done.3
  48.0 0.0 copy-done.2
  48.0 0.5 copy_bitcast_fusion
  48.6 0.2 shard_map.58
  48.8 8.8 %all-to-all-done.2.rows_ref = bf16[8,128,384]{2,1,0:T(8,128)(2,1)} async-done(((bf16[8,128,384]{2,1,0:T(8,128)(2,1)}), bf16[8,128,384]{2,1,0:T(8,128)(2,1)}, u32[]{:S(2)}, u32[]{:S(2)}) %all-to-all-start.2) | async-done | bytes 786464 | tf_op jit(solution)/shard_map/all_to_all | solution.py:47
  57.6 2.5 %shard_map.60 = bf16[256,512]{1,0:T(8,128)(2,1)} custom-call(s32[1]{0:T(128)} %bitcast.1.y_ref, bf16[8,128,384]{2,1,0:T(8,128)(2,1)} %all-to-all-done.2.rows_ref, bf16[1536,512]{1,0:T(8,128)(2,1)S(1)} %get-tuple-element.7.gate_ref, bf16[1536,512]{1,0:T(8,128)(2,1)S(1)} %get-tuple-element.8.up_ref), custom_call_target="tpu_custom_call" | custom-call | flops 402653184 | bytes 4194304 | tf_op jit(solution)/shard_map/pallas_call | solution.py:32
  60.0 2.5 %collective-permute-start = (bf16[256,512]{1,0:T(8,128)(2,1)}, bf16[256,512]{1,0:T(8,128)(2,1)S(1)}, u32[]{:S(2)}, u32[]{:S(2)}) collective-permute-start(bf16[256,512]{1,0:T(8,128)(2,1)} %shard_map.60), channel_id=1, source_target_pairs={{0,64},{1,65},{2,66},{3,67},{4,68},{5,69},{6,70},{7,71},{8,72},{9,... | collective-permute-start | bytes 786440 | tf_op jit(solution)/shard_map/ppermute | solution.py:43
  62.6 0.0 copy-start
  62.6 1.8 %shard_map.59.keep_ref = f32[256,512]{1,0:T(8,128)S(1)} custom-call(s32[1]{0:T(128)} %bitcast.1.y_ref, bf16[8,128,384]{2,1,0:T(8,128)(2,1)} %all-to-all-done.2.rows_ref, bf16[1536,512]{1,0:T(8,128)(2,1)S(1)} %get-tuple-element.7.gate_ref, bf16[1536,512]{1,0:T(8,128)(2,1)S(1)} %get-tuple-element.8.up_ref), custom_call_target="tpu_custom_call" | custom-call | flops 402653184 | bytes 4456448 | tf_op jit(solution)/shard_map/pallas_call | solution.py:32
  64.3 3.0 %collective-permute-done.near_ref = bf16[256,512]{1,0:T(8,128)(2,1)S(1)} collective-permute-done((bf16[256,512]{1,0:T(8,128)(2,1)}, bf16[256,512]{1,0:T(8,128)(2,1)S(1)}, u32[]{:S(2)}, u32[]{:S(2)}) %collective-permute-start) | collective-permute-done | bytes 262176 | tf_op jit(solution)/shard_map/ppermute | solution.py:43
  67.4 0.0 copy-done
  67.4 0.1 shard_map.61
  67.4 23.2 %all-gather = bf16[512,640]{1,0:T(8,128)(2,1)S(1)} all-gather(bf16[256,640]{1,0:T(8,128)(2,1)S(1)} %shard_map.61), channel_id=2, replica_groups={{0,32},{1,33},{2,34},{3,35},{4,36},{5,37},{6,38},{7,39},{8,40},{9,41},{..., dimensions={0}, use_global_device_ids=true | all-gather | bytes 983040 | tf_op jit(solution)/shard_map/all_gather | solution.py:240
  90.7 0.2 shard_map.62.grad_ref
  90.9 2.5 %collective-permute-start.1 = (bf16[256,512]{1,0:T(8,128)(2,1)S(1)}, bf16[256,512]{1,0:T(8,128)(2,1)S(1)}, u32[]{:S(2)}, u32[]{:S(2)}) collective-permute-start(bf16[256,512]{1,0:T(8,128)(2,1)S(1)} %shard_map.62.grad_ref), channel_id=1, source_target_pairs={{0,64},{1,65},{2,66},{3,67},{4,68},{5,69},{6,70},{7,71},{8,72},{9,... | collective-permute-start | bytes 786440 | tf_op jit(solution)/shard_map/ppermute | solution.py:43
  93.4 0.7 shard_map.63.held_ref
  94.1 4.2 %collective-permute-done.1.grad_ref = bf16[256,512]{1,0:T(8,128)(2,1)S(1)} collective-permute-done((bf16[256,512]{1,0:T(8,128)(2,1)S(1)}, bf16[256,512]{1,0:T(8,128)(2,1)S(1)}, u32[]{:S(2)}, u32[]{:S(2)}) %collective-permute-start.1) | collective-permute-done | bytes 262176 | tf_op jit(solution)/shard_map/ppermute | solution.py:43
  98.3 0.8 shard_map.64
  99.1 37.1 %all_to_all.43.pieces_ref = bf16[8,128,384]{2,1,0:T(8,128)(2,1)S(1)} all-to-all(bf16[8,128,384]{2,1,0:T(8,128)(2,1)S(1)} %shard_map.64), channel_id=1, replica_groups={{0,1,2,3,4,5,6,7},{8,9,10,11,12,13,14,15},{16,17,18,19,20,21,22,23},{24..., dimensions={0} | all-to-all | bytes 1572864 | tf_op jit(solution)/shard_map/all_to_all | solution.py:47
  136.2 0.1 shard_map.65
  136.3 13.7 %all_to_all.44 = bf16[8,16,384]{2,1,0:T(8,128)(2,1)S(1)} all-to-all(bf16[8,16,384]{2,1,0:T(8,128)(2,1)S(1)} %bitcast.24), channel_id=1, replica_groups=mesh['expert'=8,'tp'=128] {'expert'}, dimensions={0} | all-to-all | bytes 196608 | tf_op jit(solution)/shard_map/all_to_all | solution.py:47
  150.0 0.3 shard_map.66
  150.3 11.0 %all_to_all.45.part_ref = f32[4,24,128]{2,1,0:T(8,128)S(1)} all-to-all(f32[4,24,128]{2,1,0:T(8,128)S(1)} %shard_map.66), channel_id=1, replica_groups={{0,8,16,24},{1,9,17,25},{2,10,18,26},{3,11,19,27},{4,12,20,28},{5,13,21..., dimensions={0} | all-to-all | bytes 98304 | tf_op jit(solution)/shard_map/all_to_all | solution.py:47
  161.3 0.7 shard_map.67
Async XLA Ops:
  0.0 0.7 copy-start.1
  1.4 22.9 %all-to-all-start = ((bf16[4,16,192]{2,1,0:T(8,128)(2,1)}), bf16[4,16,192]{2,1,0:T(8,128)(2,1)S(1)}, u32[]{:S(2)}, u32[]{:S(2)}) async-start(bf16[4,16,192]{2,1,0:T(8,128)(2,1)} %shard_map.55), calls=%async_computation | async-start | bytes 65536 | tf_op jit(solution)/shard_map/all_to_all | solution.py:47
  16.6 31.4 %copy-start.3 = (bf16[1,1,1536,4,128]{4,3,2,1,0:T(4,128)(2,1)S(1)}, bf16[1,1,1536,4,128]{4,3,2,1,0:T(4,128)(2,1)}, u32[]{:S(2)}) copy-start(bf16[1,1,1536,4,128]{4,3,2,1,0:T(4,128)(2,1)} %param.7) | copy-start | bytes 4718596
  16.7 31.3 %copy-start.2 = (bf16[1,1,1536,4,128]{4,3,2,1,0:T(4,128)(2,1)S(1)}, bf16[1,1,1536,4,128]{4,3,2,1,0:T(4,128)(2,1)}, u32[]{:S(2)}) copy-start(bf16[1,1,1536,4,128]{4,3,2,1,0:T(4,128)(2,1)} %param.8) | copy-start | bytes 4718596
  42.2 15.4 %all-to-all-start.2 = ((bf16[8,128,384]{2,1,0:T(8,128)(2,1)}), bf16[8,128,384]{2,1,0:T(8,128)(2,1)}, u32[]{:S(2)}, u32[]{:S(2)}) async-start(bf16[8,128,384]{2,1,0:T(8,128)(2,1)} %shard_map.57), calls=%async_computation.2 | async-start | bytes 1572864 | tf_op jit(solution)/shard_map/all_to_all | solution.py:47
  60.0 7.3 %collective-permute-start = (bf16[256,512]{1,0:T(8,128)(2,1)}, bf16[256,512]{1,0:T(8,128)(2,1)S(1)}, u32[]{:S(2)}, u32[]{:S(2)}) collective-permute-start(bf16[256,512]{1,0:T(8,128)(2,1)} %shard_map.60), channel_id=1, source_target_pairs={{0,64},{1,65},{2,66},{3,67},{4,68},{5,69},{6,70},{7,71},{8,72},{9,... | collective-permute-start | bytes 786440 | tf_op jit(solution)/shard_map/ppermute | solution.py:43
  62.6 4.8 %copy-start = (bf16[1,256,128]{2,1,0:T(8,128)(2,1)S(1)}, bf16[1,256,128]{2,1,0:T(8,128)(2,1)}, u32[]{:S(2)}) copy-start(bf16[1,256,128]{2,1,0:T(8,128)(2,1)} %param.9) | copy-start | bytes 196612
  90.9 7.4 %collective-permute-start.1 = (bf16[256,512]{1,0:T(8,128)(2,1)S(1)}, bf16[256,512]{1,0:T(8,128)(2,1)S(1)}, u32[]{:S(2)}, u32[]{:S(2)}) collective-permute-start(bf16[256,512]{1,0:T(8,128)(2,1)S(1)} %shard_map.62.grad_ref), channel_id=1, source_target_pairs={{0,64},{1,65},{2,66},{3,67},{4,68},{5,69},{6,70},{7,71},{8,72},{9,... | collective-permute-start | bytes 786440 | tf_op jit(solution)/shard_map/ppermute | solution.py:43

commit v6 on v5

--- a/solution.py
+++ b/solution.py
@@ -18,7 +18,7 @@
 
 
 M_GROUPS, K_GROUPS, ZH_GROUPS = groups((0, 1, 2)), groups((3, 4)), groups((5,))
-Y_BIT = 64
+Y_BIT, ZH_BIT = 64, 32
 F32, BF16 = jnp.float32, jnp.bfloat16
 NT = (((1,), (1,)), ((), ()))
 TN = (((0,), (0,)), ((), ()))
@@ -61,13 +61,23 @@
         out_ref[z] = packed
 
 
+def place(m, f, wide):
+    pair, odd = divmod(m, 2)
+    at = odd * TILE + f if f < TILE else 2 * TILE + odd * (wide - TILE) + f - TILE
+    return 2 * pair * wide + at
+
+
 def arrange_kernel(gate_ref, up_ref, gate_out_ref, up_out_ref):
     feat = gate_ref.shape[0] // (NM * NK)
     for m in range(NM):
         for k in range(NK):
-            src, dst = (k * NM + m) * feat, (m * NK + k) * feat
-            gate_out_ref[dst : dst + feat] = gate_ref[src : src + feat]
-            up_out_ref[dst : dst + feat] = up_ref[src : src + feat]
+            src, low = (k * NM + m) * feat, k * feat
+            cut = min(max(TILE - low, 0), feat)
+            for a, b in ((0, cut), (cut, feat)):
+                if a < b:
+                    dst = place(m, low + a, NK * feat)
+                    gate_out_ref[dst : dst + b - a] = gate_ref[src + a : src + b]
+                    up_out_ref[dst : dst + b - a] = up_ref[src + a : src + b]
 
 
 def one_hot(slot_ref, half):
@@ -84,7 +94,8 @@
         raw_ref[k, :, j * n_tok : (j + 1) * n_tok] for k in range(raw_ref.shape[0]) for j in range(3)
     ]
     raw = jnp.concatenate(pieces, axis=0)
-    out = [dot(one_hot(slot_ref, h), raw, NT) for h in range(2)]
+    swap = jnp.concatenate([raw[TILE:], raw[:TILE]], axis=0)
+    out = [dot(one_hot(slot_ref, 0), raw, NT), dot(one_hot(slot_ref, 1), swap, NT)]
     out_ref[...] = jnp.concatenate(out, axis=1).astype(BF16)
 
 
@@ -103,31 +114,34 @@
     width = gate_ref.shape[1] // 2
     at = halves(y_ref, width)[0 if mine else 1]
     wide = rows_ref.shape[2] // 2
-    rows = [
-        jnp.concatenate([rows_ref[m, :, h * wide : (h + 1) * wide] for m in range(NM)], axis=1)
-        for h in range(2)
-    ]
+    rows = []
+    for head, tail in ((slice(0, TILE), slice(TILE, wide)), (slice(2 * wide - TILE, 2 * wide), slice(wide, 2 * wide - TILE))):
+        cols = []
+        for m in range(0, NM, 2):
+            cols += [rows_ref[m, :, head], rows_ref[m + 1, :, head]]
+            cols.append(jnp.concatenate([rows_ref[m, :, tail], rows_ref[m + 1, :, tail]], axis=1))
+        rows.append(jnp.concatenate(cols, axis=1))
     rows = jnp.concatenate(rows, axis=0)
     for m, w_ref in enumerate((gate_ref, up_ref)):
         out_ref[:, m * width : (m + 1) * width] = dot(rows, w_ref[:, at]).astype(out_ref.dtype)
 
 
-def near_kernel(keep_ref, near_ref, hid_ref, send_ref):
-    width = keep_ref.shape[1]
-    send_ref[:, :width] = (keep_ref[...] + near_ref[...].astype(F32)).astype(BF16)
-    for h in range(2):
-        for source in range(TILE // FEW):
-            src, dst = (2 * source + h) * FEW, h * TILE + source * FEW
-            send_ref[dst : dst + FEW, width:] = hid_ref[src : src + FEW]
-
-
-def grad_kernel(zh_ref, keep_ref, near_ref, both_ref, out_ref):
+def near_kernel(keep_ref, near_ref, send_ref):
+    send_ref[...] = (keep_ref[...] + near_ref[...].astype(F32)).astype(BF16)
+
+
+def slot_order(ref):
+    starts = [(2 * source + h) * FEW for h in range(2) for source in range(TILE // FEW)]
+    return jnp.concatenate([ref[v : v + FEW] for v in starts], axis=0).astype(F32)
+
+
+def grad_kernel(zh_ref, keep_ref, near_ref, both_ref, hid_ref, far_ref, out_ref):
     width = keep_ref.shape[1]
     hid = width // 4
-    total = keep_ref[...] + near_ref[...].astype(F32)
-    total = total + both_ref[1 - zh_ref[0], :, :width].astype(F32)
+    total = keep_ref[...] + near_ref[...].astype(F32) + both_ref[1 - zh_ref[0]].astype(F32)
+    own, far = slot_order(hid_ref), slot_order(far_ref)
     for j in range(2):
-        upstream = both_ref[j, :, width:].astype(F32)
+        upstream = jnp.where(zh_ref[0] == j, own, far)
         gate_pre = total[:, j * hid : (j + 1) * hid]
         up_pre = total[:, (2 + j) * hid : (3 + j) * hid]
         sig = jax.nn.sigmoid(gate_pre)
@@ -154,9 +168,13 @@
     for pair in range(NM // 2):
         total = held_ref[pair] + backward(y_ref, grad_ref, gate_ref, up_ref, pair, False)
         total = total.astype(BF16)
+        tail = wide - TILE
         for j in range(2):
-            piece = [total[h * TILE : (h + 1) * TILE, j * wide : (j + 1) * wide] for h in range(2)]
-            out_ref[2 * pair + j] = jnp.concatenate(piece, axis=1)
+            head, at = slice(j * TILE, (j + 1) * TILE), 2 * TILE + j * tail
+            out_ref[2 * pair + j, :, :TILE] = total[:TILE, head]
+            out_ref[2 * pair + j, :, 2 * wide - TILE :] = total[TILE:, head]
+            mixed = [total[:TILE, at : at + tail], total[TILE:, at : at + tail]]
+            out_ref[2 * pair + j, :, TILE : 2 * wide - TILE] = jnp.concatenate(mixed, axis=1)
 
 
 def sum_kernel(pieces_ref, out_ref):
@@ -169,7 +187,9 @@
 def combine_kernel(slot_ref, back_ref, out_ref):
     wide = back_ref.shape[1] // 2
     back = back_ref[...]
-    part = dot(back, one_hot(slot_ref, 0), TN)[:wide] + dot(back, one_hot(slot_ref, 1), TN)[wide:]
+    last = dot(back, one_hot(slot_ref, 1), TN)
+    last = jnp.concatenate([last[2 * wide - TILE :], last[wide : 2 * wide - TILE]], axis=0)
+    part = dot(back, one_hot(slot_ref, 0), TN)[:wide] + last
     rows = out_ref.shape[1]
     for k in range(out_ref.shape[0]):
         low = part[2 * k * rows : (2 * k + 1) * rows]
@@ -214,6 +234,9 @@
     arrived = over("expert", outgoing)
     copies = call(copies_kernel, shape((NM, TILE, 2 * wide), BF16), [], [arrived])
     rows = over("tp", copies, M_GROUPS)
+    hidden = hidden_grad[0]
+    hidden_far = swapped(hidden, ZH_BIT)
+    rows, hidden_far = lax.optimization_barrier((rows, hidden_far))
 
     n_flops = 2 * slot_total * block_rows * half
     given = [rows, gate, up]
@@ -234,12 +257,10 @@
         16,
     )
     near = swapped(send, Y_BIT)
-    send = call(
-        near_kernel, shape((slot_total, half + hid), BF16), [], [keep, near, hidden_grad[0]]
-    )
+    send = call(near_kernel, shape((slot_total, half), BF16), [], [keep, near])
     both = lax.all_gather(send, "tp", axis_index_groups=ZH_GROUPS, axis=0, tiled=False)
 
-    grads = call(grad_kernel, shape((slot_total, half), BF16), [zh_at], [keep, near, both])
+    grads = call(grad_kernel, shape((slot_total, half), BF16), [zh_at], [keep, near, both, hidden, hidden_far])
     other = swapped(grads, Y_BIT)
     held = call(
         backward_own_kernel,

time: 163 us -> 163 us (level)
  blocking collectives: 102 us -> 87.6 us
  starting transfers between devices: 25.3 us -> 37 us
  local copies, waits for them, and re-layouts: 2.35 us -> 6.82 us
    all_to_all x4, blocking collectives: 78.5 us -> 64.1 us  [over(): lax.all_to_all(shard, axis, split_axis=0, concat_axis=0, axis_index_group...]
    ppermute x2 -> x3, starting transfers between devices: 4.99 us -> 16.6 us  [swapped(): lax.ppermute(shard, 'tp', [(i, i ^ bit) for i in range(lax.axis_size('tp'...]
    all_to_all x2, waiting for transfers between devices: 14.8 us -> 6.15 us  [over(): lax.all_to_all(shard, axis, split_axis=0, concat_axis=0, axis_index_group...]
    ppermute x2 -> x3, waiting for transfers between devices: 7.21 us -> 14.7 us  [swapped(): lax.ppermute(shard, 'tp', [(i, i ^ bit) for i in range(lax.axis_size('tp'...]
    unnamed x9 -> x13, local copies, waits for them, and re-layouts: 1.49 us -> 4.3 us
    another operation x1, local copies, waits for them, and re-layouts: 0.52 us -> 2.18 us  [body(): flat = [w[0, 0].reshape(block_rows, half) for w in (w_gate, w_up)]]
  transfers between devices with their start and end apart: 4 -> 5, of which waited for: 4 -> 4; matrix products, arithmetic and copies ran while one was open for 2% -> 3% of each run, Pallas kernels for 2% -> 2%
where the time goes in v6:
time: 163 us
  blocking collectives  87.6 us (54%)
  starting transfers between devices  37 us (23%)
  waiting for transfers between devices  20.9 us (13%)
  Pallas kernels  9.16 us (6%)
  local copies, waits for them, and re-layouts  6.82 us (4%)
    all_to_all x4, blocking collectives, over(): lax.all_to_all(shard, axis, split_axis=0, concat_axis=0, axis_index_group...  64.1 us
    all_gather x1, blocking collectives, body(): lax.all_gather(send, 'tp', axis_index_groups=ZH_GROUPS, axis=0, tiled=False)  23.5 us
    all_to_all x2, starting transfers between devices, over(): lax.all_to_all(shard, axis, split_axis=0, concat_axis=0, axis_index_group...  20.4 us
    ppermute x3, starting transfers between devices, swapped(): lax.ppermute(shard, 'tp', [(i, i ^ bit) for i in range(lax.axis_size('tp'...  16.6 us
    ppermute x3, waiting for transfers between devices, swapped(): lax.ppermute(shard, 'tp', [(i, i ^ bit) for i in range(lax.axis_size('tp'...  14.7 us
    pallas_call x13, Pallas kernels, call(): pl.pallas_call(kernel, out_shape=outs, in_specs=[SMEM] * len(scalars) + [...  9.16 us
    all_to_all x2, waiting for transfers between devices, over(): lax.all_to_all(shard, axis, split_axis=0, concat_axis=0, axis_index_group...  6.15 us
    unnamed x13, local copies, waits for them, and re-layouts  4.3 us
  transfers between devices with their start and end apart: 5, of which 4 were waited for; matrix products, arithmetic and copies ran while one was open for 3% of the time, Pallas kernels for 2%

profile of v6, /device:TPU:1, one launch (start us, length us, event | category | flops | bytes accessed | tf_op | source)
XLA Modules:
  0.0 162.7 jit_solution(6094983641615900011)
XLA Ops:
  0.0 0.0 copy-start.3
  0.0 0.7 copy-done.3
  0.7 0.7 shard_map.55
  1.4 0.0 copy-start.5
  1.4 14.6 %all-to-all-start = ((bf16[4,16,192]{2,1,0:T(8,128)(2,1)}), bf16[4,16,192]{2,1,0:T(8,128)(2,1)S(1)}, u32[]{:S(2)}, u32[]{:S(2)}) async-start(bf16[4,16,192]{2,1,0:T(8,128)(2,1)} %shard_map.55), calls=%async_computation | async-start | bytes 65536 | tf_op jit(solution)/shard_map/all_to_all | solution.py:47
  16.0 0.8 copy.8
  16.7 0.0 copy-start.2
  16.7 0.1 eq.15
  16.9 0.0 copy-start.4
  16.9 0.1 fusion
  17.0 0.2 reduce_window_sum.11
  17.1 0.2 select_reduce_fusion
  17.3 0.1 reduce_sum.12
  17.5 0.1 copy.9
  17.5 0.7 add_bitcast_fusion.slot_ref
  18.2 6.1 %all-to-all-done.raw_ref = bf16[4,16,192]{2,1,0:T(8,128)(2,1)S(1)} async-done(((bf16[4,16,192]{2,1,0:T(8,128)(2,1)}), bf16[4,16,192]{2,1,0:T(8,128)(2,1)S(1)}, u32[]{:S(2)}, u32[]{:S(2)}) %all-to-all-start) | async-done | bytes 24608 | tf_op jit(solution)/shard_map/all_to_all | solution.py:47
  24.4 0.3 shard_map.56
  24.7 16.6 %all_to_all.42 = bf16[8,16,384]{2,1,0:T(8,128)(2,1)S(1)} all-to-all(bf16[8,16,384]{2,1,0:T(8,128)(2,1)S(1)} %bitcast.22), channel_id=1, replica_groups=mesh['expert'=8,'tp'=128] {'expert'}, dimensions={0} | all-to-all | bytes 196608 | tf_op jit(solution)/shard_map/all_to_all | solution.py:47
  41.4 1.0 shard_map.57
  42.3 5.8 %all-to-all-start.2 = ((bf16[8,128,384]{2,1,0:T(8,128)(2,1)}), bf16[8,128,384]{2,1,0:T(8,128)(2,1)}, u32[]{:S(2)}, u32[]{:S(2)}) async-start(bf16[8,128,384]{2,1,0:T(8,128)(2,1)} %shard_map.57), calls=%async_computation.2 | async-start | bytes 1572864 | tf_op jit(solution)/shard_map/all_to_all | solution.py:47
  48.2 0.0 copy-done.2
  48.2 11.6 %collective-permute-start = (bf16[256,128]{1,0:T(8,128)(2,1)S(1)}, bf16[256,128]{1,0:T(8,128)(2,1)S(1)}, u32[]{:S(2)}, u32[]{:S(2)}) collective-permute-start(bf16[256,128]{1,0:T(8,128)(2,1)S(1)} %bitcast.25), channel_id=1, source_target_pairs={{0,32},{1,33},{2,34},{3,35},{4,36},{5,37},{6,38},{7,39},{8,40},{9,... | collective-permute-start | bytes 196616 | tf_op jit(solution)/shard_map/ppermute | solution.py:43
  59.8 0.0 copy-done.5
  59.8 0.0 copy-done.4
  59.8 2.2 %copy_bitcast_fusion = (bf16[1536,512]{1,0:T(8,128)(2,1)}, bf16[1536,512]{1,0:T(8,128)(2,1)}) fusion(bf16[192,8,4,128]{3,2,1,0:T(4,128)(2,1)S(1)} %bitcast.28, bf16[192,8,4,128]{3,2,1,0:T(4,128)(2,1)S(1)} %bitcast.29), kind=kLoop, calls=%fused_computation | loop fusion | bytes 6291456 | tf_op jit(solution)/shard_map/reshape;squeeze | solution.py:221
  61.9 0.0 copy-start
  62.0 1.4 copy-done
  63.4 0.0 copy-start.1
  63.4 1.4 copy-done.1
  64.8 0.2 shard_map.58
  65.0 5.6 %collective-permute-done.far_ref = bf16[256,128]{1,0:T(8,128)(2,1)S(1)} collective-permute-done((bf16[256,128]{1,0:T(8,128)(2,1)S(1)}, bf16[256,128]{1,0:T(8,128)(2,1)S(1)}, u32[]{:S(2)}, u32[]{:S(2)}) %collective-permute-start) | collective-permute-done | bytes 65568 | tf_op jit(solution)/shard_map/ppermute | solution.py:43
  70.6 0.0 all-to-all-done.2.rows_ref
  70.6 2.4 %shard_map.60 = bf16[256,512]{1,0:T(8,128)(2,1)} custom-call(s32[1]{0:T(128)} %bitcast.1.y_ref, bf16[8,128,384]{2,1,0:T(8,128)(2,1)} %all-to-all-done.2.rows_ref, bf16[1536,512]{1,0:T(8,128)(2,1)S(1)} %get-tuple-element.10.gate_ref, bf16[1536,512]{1,0:T(8,128)(2,1)S(1)} %get-tuple-element.11.up_ref), custom_call_target="tpu_custom_call" | custom-call | flops 402653184 | bytes 4194304 | tf_op jit(solution)/shard_map/pallas_call | solution.py:32
  73.0 2.5 %collective-permute-start.1 = (bf16[256,512]{1,0:T(8,128)(2,1)}, bf16[256,512]{1,0:T(8,128)(2,1)S(1)}, u32[]{:S(2)}, u32[]{:S(2)}) collective-permute-start(bf16[256,512]{1,0:T(8,128)(2,1)} %shard_map.60), channel_id=1, source_target_pairs={{0,64},{1,65},{2,66},{3,67},{4,68},{5,69},{6,70},{7,71},{8,72},{9,... | collective-permute-start | bytes 786440 | tf_op jit(solution)/shard_map/ppermute | solution.py:43
  75.6 1.7 %shard_map.59.keep_ref = f32[256,512]{1,0:T(8,128)S(1)} custom-call(s32[1]{0:T(128)} %bitcast.1.y_ref, bf16[8,128,384]{2,1,0:T(8,128)(2,1)} %all-to-all-done.2.rows_ref, bf16[1536,512]{1,0:T(8,128)(2,1)S(1)} %get-tuple-element.10.gate_ref, bf16[1536,512]{1,0:T(8,128)(2,1)S(1)} %get-tuple-element.11.up_ref), custom_call_target="tpu_custom_call" | custom-call | flops 402653184 | bytes 4456448 | tf_op jit(solution)/shard_map/pallas_call | solution.py:32
  77.3 3.1 %collective-permute-done.1.near_ref = bf16[256,512]{1,0:T(8,128)(2,1)S(1)} collective-permute-done((bf16[256,512]{1,0:T(8,128)(2,1)}, bf16[256,512]{1,0:T(8,128)(2,1)S(1)}, u32[]{:S(2)}, u32[]{:S(2)}) %collective-permute-start.1) | collective-permute-done | bytes 262176 | tf_op jit(solution)/shard_map/ppermute | solution.py:43
  80.4 23.5 %all-gather = bf16[512,512]{1,0:T(8,128)(2,1)S(1)} all-gather(bf16[256,512]{1,0:T(8,128)(2,1)S(1)} %shard_map.61), channel_id=2, replica_groups={{0,32},{1,33},{2,34},{3,35},{4,36},{5,37},{6,38},{7,39},{8,40},{9,41},{..., dimensions={0}, use_global_device_ids=true | all-gather | bytes 786432 | tf_op jit(solution)/shard_map/all_gather | solution.py:261
  103.9 0.2 shard_map.62.grad_ref
  104.1 2.5 %collective-permute-start.2 = (bf16[256,512]{1,0:T(8,128)(2,1)S(1)}, bf16[256,512]{1,0:T(8,128)(2,1)S(1)}, u32[]{:S(2)}, u32[]{:S(2)}) collective-permute-start(bf16[256,512]{1,0:T(8,128)(2,1)S(1)} %shard_map.62.grad_ref), channel_id=1, source_target_pairs={{0,64},{1,65},{2,66},{3,67},{4,68},{5,69},{6,70},{7,71},{8,72},{9,... | collective-permute-start | bytes 786440 | tf_op jit(solution)/shard_map/ppermute | solution.py:43
  106.6 0.7 shard_map.63.held_ref
  107.4 6.0 %collective-permute-done.2.grad_ref = bf16[256,512]{1,0:T(8,128)(2,1)S(1)} collective-permute-done((bf16[256,512]{1,0:T(8,128)(2,1)S(1)}, bf16[256,512]{1,0:T(8,128)(2,1)S(1)}, u32[]{:S(2)}, u32[]{:S(2)}) %collective-permute-start.2) | collective-permute-done | bytes 262176 | tf_op jit(solution)/shard_map/ppermute | solution.py:43
  113.3 0.8 shard_map.64
  114.1 22.6 %all_to_all.43.pieces_ref = bf16[8,128,384]{2,1,0:T(8,128)(2,1)S(1)} all-to-all(bf16[8,128,384]{2,1,0:T(8,128)(2,1)S(1)} %shard_map.64), channel_id=1, replica_groups={{0,1,2,3,4,5,6,7},{8,9,10,11,12,13,14,15},{16,17,18,19,20,21,22,23},{24..., dimensions={0} | all-to-all | bytes 1572864 | tf_op jit(solution)/shard_map/all_to_all | solution.py:47
  136.8 0.1 shard_map.65
  136.9 13.8 %all_to_all.44 = bf16[8,16,384]{2,1,0:T(8,128)(2,1)S(1)} all-to-all(bf16[8,16,384]{2,1,0:T(8,128)(2,1)S(1)} %bitcast.24), channel_id=1, replica_groups=mesh['expert'=8,'tp'=128] {'expert'}, dimensions={0} | all-to-all | bytes 196608 | tf_op jit(solution)/shard_map/all_to_all | solution.py:47
  150.7 0.3 shard_map.66
  151.0 11.0 %all_to_all.45.part_ref = f32[4,24,128]{2,1,0:T(8,128)S(1)} all-to-all(f32[4,24,128]{2,1,0:T(8,128)S(1)} %shard_map.66), channel_id=1, replica_groups={{0,8,16,24},{1,9,17,25},{2,10,18,26},{3,11,19,27},{4,12,20,28},{5,13,21..., dimensions={0} | all-to-all | bytes 98304 | tf_op jit(solution)/shard_map/all_to_all | solution.py:47
  162.0 0.7 shard_map.67
  (1 shorter events, 0.0 us)
Async XLA Ops:
  0.0 0.7 copy-start.3
  1.4 58.4 %copy-start.5 = (bf16[1,1,1536,4,128]{4,3,2,1,0:T(4,128)(2,1)S(1)}, bf16[1,1,1536,4,128]{4,3,2,1,0:T(4,128)(2,1)}, u32[]{:S(2)}) copy-start(bf16[1,1,1536,4,128]{4,3,2,1,0:T(4,128)(2,1)} %param.7) | copy-start | bytes 4718596
  1.4 23.0 %all-to-all-start = ((bf16[4,16,192]{2,1,0:T(8,128)(2,1)}), bf16[4,16,192]{2,1,0:T(8,128)(2,1)S(1)}, u32[]{:S(2)}, u32[]{:S(2)}) async-start(bf16[4,16,192]{2,1,0:T(8,128)(2,1)} %shard_map.55), calls=%async_computation | async-start | bytes 65536 | tf_op jit(solution)/shard_map/all_to_all | solution.py:47
  16.7 31.4 %copy-start.2 = (bf16[1,256,128]{2,1,0:T(8,128)(2,1)S(1)}, bf16[1,256,128]{2,1,0:T(8,128)(2,1)}, u32[]{:S(2)}) copy-start(bf16[1,256,128]{2,1,0:T(8,128)(2,1)} %param.9) | copy-start | bytes 196612
  16.9 42.9 %copy-start.4 = (bf16[1,1,1536,4,128]{4,3,2,1,0:T(4,128)(2,1)S(1)}, bf16[1,1,1536,4,128]{4,3,2,1,0:T(4,128)(2,1)}, u32[]{:S(2)}) copy-start(bf16[1,1,1536,4,128]{4,3,2,1,0:T(4,128)(2,1)} %param.8) | copy-start | bytes 4718596
  42.3 28.3 %all-to-all-start.2 = ((bf16[8,128,384]{2,1,0:T(8,128)(2,1)}), bf16[8,128,384]{2,1,0:T(8,128)(2,1)}, u32[]{:S(2)}, u32[]{:S(2)}) async-start(bf16[8,128,384]{2,1,0:T(8,128)(2,1)} %shard_map.57), calls=%async_computation.2 | async-start | bytes 1572864 | tf_op jit(solution)/shard_map/all_to_all | solution.py:47
  48.2 22.4 %collective-permute-start = (bf16[256,128]{1,0:T(8,128)(2,1)S(1)}, bf16[256,128]{1,0:T(8,128)(2,1)S(1)}, u32[]{:S(2)}, u32[]{:S(2)}) collective-permute-start(bf16[256,128]{1,0:T(8,128)(2,1)S(1)} %bitcast.25), channel_id=1, source_target_pairs={{0,32},{1,33},{2,34},{3,35},{4,36},{5,37},{6,38},{7,39},{8,40},{9,... | collective-permute-start | bytes 196616 | tf_op jit(solution)/shard_map/ppermute | solution.py:43
  61.9 1.4 copy-start
  63.4 1.4 copy-start.1
  73.0 7.3 %collective-permute-start.1 = (bf16[256,512]{1,0:T(8,128)(2,1)}, bf16[256,512]{1,0:T(8,128)(2,1)S(1)}, u32[]{:S(2)}, u32[]{:S(2)}) collective-permute-start(bf16[256,512]{1,0:T(8,128)(2,1)} %shard_map.60), channel_id=1, source_target_pairs={{0,64},{1,65},{2,66},{3,67},{4,68},{5,69},{6,70},{7,71},{8,72},{9,... | collective-permute-start | bytes 786440 | tf_op jit(solution)/shard_map/ppermute | solution.py:43
  104.1 9.2 %collective-permute-start.2 = (bf16[256,512]{1,0:T(8,128)(2,1)S(1)}, bf16[256,512]{1,0:T(8,128)(2,1)S(1)}, u32[]{:S(2)}, u32[]{:S(2)}) collective-permute-start(bf16[256,512]{1,0:T(8,128)(2,1)S(1)} %shard_map.62.grad_ref), channel_id=1, source_target_pairs={{0,64},{1,65},{2,66},{3,67},{4,68},{5,69},{6,70},{7,71},{8,72},{9,... | collective-permute-start | bytes 786440 | tf_op jit(solution)/shard_map/ppermute | solution.py:43

commit v7 on v6

v7 whole, which is shorter than its diff:
```python
import functools

import jax
import jax.numpy as jnp
from jax import lax
from jax.experimental import pallas as pl
from jax.experimental.pallas import tpu as pltpu
from jax.sharding import PartitionSpec as P

NX, NZL, NK = 4, 8, 4
ORDER = [2 * k + z0 for z0 in range(2) for k in range(NK)]
FEW, TILE = 16, 128


def groups(bits, count=128):
    mask = sum(1 << b for b in bits)
    spread = [sum(((k >> i) & 1) << b for i, b in enumerate(bits)) for k in range(1 << len(bits))]
    return [[base | v for v in spread] for base in range(count) if not base & mask]


X_GROUPS, ZL_GROUPS, ZH_GROUPS = groups((0, 1)), groups((2, 3, 4)), groups((5,))
M_GROUPS, K_GROUPS = groups((0, 1, 2)), groups((3, 4))
Y_BIT, ZH_BIT = 64, 32
F32, BF16 = jnp.float32, jnp.bfloat16
NT = (((1,), (1,)), ((), ()))
TN = (((0,), (0,)), ((), ()))
VMEM = pl.BlockSpec(memory_space=pltpu.VMEM)
SMEM = pl.BlockSpec(memory_space=pltpu.SMEM)


def call(kernel, outs, scalars, arrays, flops=0, mib=6):
    several = isinstance(outs, (tuple, list))
    moved = sum(v.size * v.dtype.itemsize for v in [*arrays, *(outs if several else [outs])])
    return pl.pallas_call(
        kernel,
        out_shape=outs,
        in_specs=[SMEM] * len(scalars) + [VMEM] * len(arrays),
        out_specs=[VMEM] * len(outs) if several else VMEM,
        compiler_params=pltpu.CompilerParams(vmem_limit_bytes=mib * 1024 * 1024),
        cost_estimate=pl.CostEstimate(flops=flops, bytes_accessed=moved, transcendentals=0),
    )(*scalars, *arrays)


def swapped(shard, bit):
    return lax.ppermute(shard, "tp", [(i, i ^ bit) for i in range(lax.axis_size("tp"))])


def over(axis, shard, groups=None):
    return lax.all_to_all(
        shard, axis, split_axis=0, concat_axis=0, axis_index_groups=groups, tiled=True
    )


def dot(a, b, dims=(((1,), (0,)), ((), ()))):
    return lax.dot_general(a, b, dims, preferred_element_type=F32)


def pack_kernel(tok_ref, out_ref):
    turned = tok_ref[...]
    third = turned.shape[0] // 3
    packed = jnp.concatenate([turned[j * third : (j + 1) * third] for j in range(3)], axis=1)
    for z in range(out_ref.shape[0]):
        out_ref[z] = packed


def arrange_kernel(in_ref, out_ref):
    feat = in_ref.shape[0] // (NX * NZL)
    for x in range(NX):
        for at, z in enumerate(ORDER):
            src, dst = (z * NX + x) * feat, (x * NZL + at) * feat
            out_ref[dst : dst + feat] = in_ref[src : src + feat]


def one_hot(slot_ref, slots):
    hit = (slots == slot_ref[0:1, :]) | (slots == slot_ref[1:2, :])
    return jnp.where(hit, 1.0, 0.0).astype(BF16)


def dispatch_kernel(slot_ref, raw_ref, out_ref):
    n_tok = slot_ref.shape[1]
    pieces = [
        raw_ref[z, :, j * n_tok : (j + 1) * n_tok] for z in ORDER for j in range(3)
    ]
    raw = jnp.concatenate(pieces, axis=0)
    slots = lax.broadcasted_iota(jnp.int32, (out_ref.shape[0], n_tok), 0)
    out_ref[...] = dot(one_hot(slot_ref, slots), raw, NT).astype(BF16)


def halves(y_ref, width):
    own = pl.multiple_of(y_ref[0] * width, width)
    other = pl.multiple_of((1 - y_ref[0]) * width, width)
    return pl.ds(own, width), pl.ds(other, width)


def forward_kernel(y_ref, rows_ref, gate_ref, up_ref, out_ref, *, mine):
    width = gate_ref.shape[1] // 2
    at = halves(y_ref, width)[0 if mine else 1]
    rows = jnp.concatenate([rows_ref[x] for x in range(rows_ref.shape[0])], axis=1)
    for m, w_ref in enumerate((gate_ref, up_ref)):
        out_ref[:, m * width : (m + 1) * width] = dot(rows, w_ref[:, at]).astype(out_ref.dtype)


def near_kernel(keep_ref, near_ref, send_ref):
    send_ref[...] = (keep_ref[...] + near_ref[...].astype(F32)).astype(BF16)


def grad_kernel(zh_ref, keep_ref, near_ref, both_ref, hid_ref, far_ref, out_ref):
    width = keep_ref.shape[1]
    hid = width // 4
    total = keep_ref[...] + near_ref[...].astype(F32) + both_ref[1 - zh_ref[0]].astype(F32)
    own, far = hid_ref[...].astype(F32), far_ref[...].astype(F32)
    for j in range(2):
        upstream = jnp.where(zh_ref[0] == j, own, far)
        gate_pre = total[:, j * hid : (j + 1) * hid]
        up_pre = total[:, (2 + j) * hid : (3 + j) * hid]
        sig = jax.nn.sigmoid(gate_pre)
        gate_grad = upstream * up_pre * sig * (1.0 + gate_pre * (1.0 - sig))
        out_ref[:, j * hid : (j + 1) * hid] = gate_grad.astype(BF16)
        out_ref[:, (2 + j) * hid : (3 + j) * hid] = (upstream * gate_pre * sig).astype(BF16)


def backward(y_ref, grad_ref, gate_ref, up_ref, x, mine):
    width = gate_ref.shape[1] // 2
    at = halves(y_ref, width)[0 if mine else 1]
    wide = gate_ref.shape[0] // NX
    r = slice(x * wide, (x + 1) * wide)
    return dot(grad_ref[:, :width], gate_ref[r, at], NT) + dot(grad_ref[:, width:], up_ref[r, at], NT)


def backward_own_kernel(y_ref, grad_ref, gate_ref, up_ref, out_ref):
    for x in range(NX):
        out_ref[x] = backward(y_ref, grad_ref, gate_ref, up_ref, x, True)


def backward_other_kernel(y_ref, grad_ref, gate_ref, up_ref, held_ref, out_ref):
    wide = out_ref.shape[2] // 2
    for x in range(NX):
        total = held_ref[x] + backward(y_ref, grad_ref, gate_ref, up_ref, x, False)
        total = total.astype(BF16)
        part = []
        for h in range(2):
            starts = [(2 * e + h) * FEW for e in range(TILE // FEW)]
            part.append(jnp.concatenate([total[v : v + FEW] for v in starts], axis=0))
        for z0 in range(2):
            at = slice(z0 * wide, (z0 + 1) * wide)
            out_ref[z0 * NX + x] = jnp.concatenate([part[0][:, at], part[1][:, at]], axis=1)


def sum_kernel(pieces_ref, out_ref):
    total = pieces_ref[0].astype(F32)
    for x in range(1, pieces_ref.shape[0]):
        total = total + pieces_ref[x].astype(F32)
    out_ref[...] = total.astype(BF16)


def returned_rows(slot_ref, half):
    row = lax.broadcasted_iota(jnp.int32, (TILE, slot_ref.shape[1]), 0)
    return jnp.right_shift(row, 4) * (2 * FEW) + half * FEW + jnp.bitwise_and(row, FEW - 1)


def combine_kernel(slot_ref, back_ref, out_ref):
    wide = back_ref.shape[1] // 2
    back = back_ref[...]
    part = [dot(back, one_hot(slot_ref, returned_rows(slot_ref, h)), TN) for h in range(2)]
    part = part[0][:wide] + part[1][wide:]
    rows = out_ref.shape[1]
    for k in range(out_ref.shape[0]):
        low = part[2 * k * rows : (2 * k + 1) * rows]
        out_ref[k] = jnp.concatenate([low, part[(2 * k + 1) * rows : (2 * k + 2) * rows]], axis=1)


def finish_kernel(part_ref, out_ref):
    total = part_ref[0]
    for z in range(1, part_ref.shape[0]):
        total = total + part_ref[z]
    n_tok = out_ref.shape[1]
    out_ref[...] = jnp.concatenate([total[:, :n_tok], total[:, n_tok:]], axis=0).astype(BF16)


def body(tokens, routes, w_gate, w_up, hidden_grad):
    position = lax.axis_index("tp")
    y_at = jnp.bitwise_and(jnp.right_shift(position, 6), 1).reshape(1)
    zh_at = jnp.bitwise_and(jnp.right_shift(position, 5), 1).reshape(1)
    n_groups = lax.axis_size("expert")
    slot_total = hidden_grad.shape[1]
    capacity = slot_total // n_groups
    n_tok, feat = tokens.shape
    block_rows = w_gate.shape[2]
    hid = w_gate.shape[4]
    wide = NZL * feat
    shape = jax.ShapeDtypeStruct

    half = 4 * hid
    gate, up = [
        call(arrange_kernel, shape((block_rows, half), BF16), [], [w[0, 0].reshape(block_rows, half)])
        for w in (w_gate, w_up)
    ]

    packed = call(pack_kernel, shape((NZL, feat // 3, 3 * n_tok), BF16), [], [tokens.T])
    raw = over("tp", packed, ZL_GROUPS)

    flat_routes = routes.reshape(n_tok * 2)
    named = (flat_routes[:, None] == jnp.arange(n_groups, dtype=jnp.int32)[None, :]).astype(jnp.int32)
    before = jnp.cumsum(named, axis=0) - named
    slot_index = flat_routes * capacity + jnp.sum(before * named, axis=1)
    slot_index = slot_index.reshape(n_tok, 2).T

    outgoing = call(dispatch_kernel, shape((slot_total, wide), BF16), [], [slot_index, raw])
    arrived = over("expert", outgoing)
    hidden = hidden_grad[0]
    hidden_far = swapped(hidden, ZH_BIT)
    arrived, gate, up = lax.optimization_barrier((arrived, gate, up))
    rows = lax.all_gather(arrived, "tp", axis_index_groups=X_GROUPS, axis=0, tiled=False)
    rows, hidden_far = lax.optimization_barrier((rows, hidden_far))

    n_flops = 2 * slot_total * block_rows * half
    given = [rows, gate, up]
    send = call(
        functools.partial(forward_kernel, mine=False),
        shape((slot_total, half), BF16),
        [y_at],
        given,
        n_flops,
        16,
    )
    keep = call(
        functools.partial(forward_kernel, mine=True),
        shape((slot_total, half), F32),
        [y_at],
        given,
        n_flops,
        16,
    )
    near = swapped(send, Y_BIT)
    send = call(near_kernel, shape((slot_total, half), BF16), [], [keep, near])
    both = lax.all_gather(send, "tp", axis_index_groups=ZH_GROUPS, axis=0, tiled=False)

    grads = call(
        grad_kernel,
        shape((slot_total, half), BF16),
        [zh_at],
        [keep, near, both, hidden, hidden_far],
    )
    other = swapped(grads, Y_BIT)
    held = call(
        backward_own_kernel,
        shape((NX, slot_total, wide), F32),
        [y_at],
        [grads, gate, up],
        n_flops,
        16,
    )
    pieces = call(
        backward_other_kernel,
        shape((2 * NX, TILE, wide), BF16),
        [y_at],
        [other, gate, up, held],
        n_flops,
        16,
    )
    pieces = over("tp", pieces, M_GROUPS)
    summed = call(sum_kernel, shape((TILE, wide), BF16), [], [pieces])
    returned = over("expert", summed)

    part = call(combine_kernel, shape((NK, feat // 2, 2 * n_tok), F32), [], [slot_index, returned])
    part = over("tp", part, K_GROUPS)
    total = call(finish_kernel, shape((feat, n_tok), BF16), [], [part])
    return total.T


def solution(mesh):
    placed = (
        P("expert", "tp"),
        P("expert", None),
        P("expert", "tp", None, None, None),
        P("expert", "tp", None, None, None),
        P("expert", None, "tp"),
    )
    return jax.shard_map(
        body, mesh=mesh, in_specs=placed, out_specs=P("expert", "tp"), check_vma=False
    )
```

time: 163 us -> 162 us (level)
  starting transfers between devices: 37 us -> 41.2 us
  waiting for transfers between devices: 20.9 us -> 17.5 us
  Pallas kernels: 9.16 us -> 6.57 us
    all_to_all x4 -> x3, blocking collectives: 64.1 us -> 47.6 us  [over(): lax.all_to_all(shard, axis, split_axis=0, concat_axis=0, axis_index_group...]
    all_gather x0 -> x1, blocking collectives: none -> 12 us  [body(): lax.all_gather(arrived, 'tp', axis_index_groups=X_GROUPS, axis=0, tiled=F...]
    all_gather x1, blocking collectives: 23.5 us -> 28.8 us  [body(): lax.all_gather(send, 'tp', axis_index_groups=ZH_GROUPS, axis=0, tiled=False)]
    all_to_all x2, starting transfers between devices: 20.4 us -> 25.4 us  [over(): lax.all_to_all(shard, axis, split_axis=0, concat_axis=0, axis_index_group...]
    ppermute x3, waiting for transfers between devices: 14.7 us -> 10 us  [swapped(): lax.ppermute(shard, 'tp', [(i, i ^ bit) for i in range(lax.axis_size('tp'...]
    pallas_call x13, Pallas kernels: 9.16 us -> 6.57 us  [call(): pl.pallas_call(kernel, out_shape=outs, in_specs=[SMEM] * len(scalars) + [...]
    another operation x1 -> x0, local copies, waits for them, and re-layouts: 2.18 us -> none  [body(): flat = [w[0, 0].reshape(block_rows, half) for w in (w_gate, w_up)]]
  transfers between devices with their start and end apart: 5 -> 5, of which waited for: 4 -> 3; matrix products, arithmetic and copies ran while one was open for 3% -> 3% of each run, Pallas kernels for 2% -> 1%
where the time goes in v7:
time: 162 us; the launch traced here: 161 us
  blocking collectives  88.4 us (55%)
  starting transfers between devices  41.2 us (25%)
  waiting for transfers between devices  17.5 us (11%)
  Pallas kernels  6.57 us (4%)
  local copies, waits for them, and re-layouts  6.2 us (4%)
    all_to_all x3, blocking collectives, over(): lax.all_to_all(shard, axis, split_axis=0, concat_axis=0, axis_index_group...  47.6 us
    all_gather x1, blocking collectives, body(): lax.all_gather(send, 'tp', axis_index_groups=ZH_GROUPS, axis=0, tiled=False)  28.8 us
    all_to_all x2, starting transfers between devices, over(): lax.all_to_all(shard, axis, split_axis=0, concat_axis=0, axis_index_group...  25.4 us
    ppermute x3, starting transfers between devices, swapped(): lax.ppermute(shard, 'tp', [(i, i ^ bit) for i in range(lax.axis_size('tp'...  15.8 us
    all_gather x1, blocking collectives, body(): lax.all_gather(arrived, 'tp', axis_index_groups=X_GROUPS, axis=0, tiled=F...  12 us
    ppermute x3, waiting for transfers between devices, swapped(): lax.ppermute(shard, 'tp', [(i, i ^ bit) for i in range(lax.axis_size('tp'...  10 us
    all_to_all x2, waiting for transfers between devices, over(): lax.all_to_all(shard, axis, split_axis=0, concat_axis=0, axis_index_group...  7.49 us
    pallas_call x13, Pallas kernels, call(): pl.pallas_call(kernel, out_shape=outs, in_specs=[SMEM] * len(scalars) + [...  6.57 us
  transfers between devices with their start and end apart: 5, of which 3 were waited for; matrix products, arithmetic and copies ran while one was open for 3% of the time, Pallas kernels for 1%

profile of v7, /device:TPU:1, one launch (start us, length us, event | category | flops | bytes accessed | tf_op | source)
XLA Modules:
  0.0 161.2 jit_solution(2568502884250922124)
XLA Ops:
  0.0 0.0 copy-start.3
  0.0 0.7 copy-done.3
  0.7 0.7 shard_map.55
  1.4 16.3 %all-to-all-start = ((bf16[8,16,192]{2,1,0:T(8,128)(2,1)}), bf16[8,16,192]{2,1,0:T(8,128)(2,1)S(1)}, u32[]{:S(2)}, u32[]{:S(2)}) async-start(bf16[8,16,192]{2,1,0:T(8,128)(2,1)} %shard_map.55), calls=%async_computation | async-start | bytes 131072 | tf_op jit(solution)/shard_map/all_to_all | solution.py:49
  17.7 0.8 copy.8
  18.4 0.1 eq.15
  18.6 0.1 fusion
  18.7 0.2 reduce_window_sum.11
  18.8 0.2 select_reduce_fusion
  19.0 0.1 reduce_sum.12
  19.2 0.1 copy.9
  19.2 0.7 add_bitcast_fusion.slot_ref
  19.9 7.5 %all-to-all-done.raw_ref = bf16[8,16,192]{2,1,0:T(8,128)(2,1)S(1)} async-done(((bf16[8,16,192]{2,1,0:T(8,128)(2,1)}), bf16[8,16,192]{2,1,0:T(8,128)(2,1)S(1)}, u32[]{:S(2)}, u32[]{:S(2)}) %all-to-all-start) | async-done | bytes 49184 | tf_op jit(solution)/shard_map/all_to_all | solution.py:49
  27.4 1.0 shard_map.56
  28.4 9.2 %all-to-all-start.1 = ((bf16[8,32,384]{2,1,0:T(8,128)(2,1)}), bf16[8,32,384]{2,1,0:T(8,128)(2,1)S(1)}, u32[]{:S(2)}, u32[]{:S(2)}) async-start(bf16[8,32,384]{2,1,0:T(8,128)(2,1)} %bitcast.4), calls=%async_computation.1 | async-start | bytes 393216 | tf_op jit(solution)/shard_map/all_to_all | solution.py:49
  37.6 11.6 %collective-permute-start = (bf16[256,128]{1,0:T(8,128)(2,1)}, bf16[256,128]{1,0:T(8,128)(2,1)S(1)}, u32[]{:S(2)}, u32[]{:S(2)}) collective-permute-start(bf16[256,128]{1,0:T(8,128)(2,1)} %bitcast.30), channel_id=1, source_target_pairs={{0,32},{1,33},{2,34},{3,35},{4,36},{5,37},{6,38},{7,39},{8,40},{9,... | collective-permute-start | bytes 196616 | tf_op jit(solution)/shard_map/ppermute | solution.py:45
  49.2 1.7 %copy.15 = bf16[192,8,4,128]{3,1,2,0:T(8,128)(2,1)S(1)} copy(bf16[192,8,4,128]{3,2,1,0:T(4,128)(2,1)} %bitcast.33) | data formatting | bytes 3145728
  50.8 0.0 copy-start.4
  50.9 0.1 shard_map.57.gate_ref
  51.0 1.3 copy-done.4
  52.3 0.3 copy.14
  52.5 0.1 shard_map.58.up_ref
  52.6 0.0 all-to-all-done.1
  52.7 12.0 %all-gather = bf16[1024,384]{1,0:T(8,128)(2,1)S(1)} all-gather(bf16[256,384]{1,0:T(8,128)(2,1)S(1)} %bitcast.35), channel_id=2, replica_groups={{0,1,2,3},{4,5,6,7},{8,9,10,11},{12,13,14,15},{16,17,18,19},{20,21,22,2..., dimensions={0}, use_global_device_ids=true | all-gather | bytes 983040 | tf_op jit(solution)/shard_map/all_gather | solution.py:213
  64.6 0.0 copy-start
  64.7 0.0 collective-permute-done.far_ref
  64.7 1.3 shard_map.60
  65.9 0.0 copy-done
  65.9 2.3 %collective-permute-start.1 = (bf16[256,512]{1,0:T(8,128)(2,1)}, bf16[256,512]{1,0:T(8,128)(2,1)S(1)}, u32[]{:S(2)}, u32[]{:S(2)}) collective-permute-start(bf16[256,512]{1,0:T(8,128)(2,1)} %shard_map.60), channel_id=1, source_target_pairs={{0,64},{1,65},{2,66},{3,67},{4,68},{5,69},{6,70},{7,71},{8,72},{9,... | collective-permute-start | bytes 786440 | tf_op jit(solution)/shard_map/ppermute | solution.py:45
  68.2 0.0 copy-start.1
  68.3 1.1 copy-done.1
  69.4 0.6 shard_map.59.keep_ref
  70.0 0.0 copy-start.2
  70.0 3.6 %collective-permute-done.1.near_ref = bf16[256,512]{1,0:T(8,128)(2,1)S(1)} collective-permute-done((bf16[256,512]{1,0:T(8,128)(2,1)}, bf16[256,512]{1,0:T(8,128)(2,1)S(1)}, u32[]{:S(2)}, u32[]{:S(2)}) %collective-permute-start.1) | collective-permute-done | bytes 262176 | tf_op jit(solution)/shard_map/ppermute | solution.py:45
  73.6 28.8 %all-gather.1 = bf16[512,512]{1,0:T(8,128)(2,1)S(1)} all-gather(bf16[256,512]{1,0:T(8,128)(2,1)S(1)} %shard_map.61), channel_id=3, replica_groups={{0,32},{1,33},{2,34},{3,35},{4,36},{5,37},{6,38},{7,39},{8,40},{9,41},{..., dimensions={0}, use_global_device_ids=true | all-gather | bytes 786432 | tf_op jit(solution)/shard_map/all_gather | solution.py:236
  102.4 0.0 copy-done.2
  102.4 0.2 shard_map.62.grad_ref
  102.6 1.9 %collective-permute-start.2 = (bf16[256,512]{1,0:T(8,128)(2,1)S(1)}, bf16[256,512]{1,0:T(8,128)(2,1)S(1)}, u32[]{:S(2)}, u32[]{:S(2)}) collective-permute-start(bf16[256,512]{1,0:T(8,128)(2,1)S(1)} %shard_map.62.grad_ref), channel_id=1, source_target_pairs={{0,64},{1,65},{2,66},{3,67},{4,68},{5,69},{6,70},{7,71},{8,72},{9,... | collective-permute-start | bytes 786440 | tf_op jit(solution)/shard_map/ppermute | solution.py:45
  104.6 0.7 shard_map.63.held_ref
  105.3 6.4 %collective-permute-done.2.grad_ref = bf16[256,512]{1,0:T(8,128)(2,1)S(1)} collective-permute-done((bf16[256,512]{1,0:T(8,128)(2,1)S(1)}, bf16[256,512]{1,0:T(8,128)(2,1)S(1)}, u32[]{:S(2)}, u32[]{:S(2)}) %collective-permute-start.2) | collective-permute-done | bytes 262176 | tf_op jit(solution)/shard_map/ppermute | solution.py:45
  111.7 0.8 shard_map.64
  112.5 18.5 %all_to_all.38.pieces_ref = bf16[8,128,384]{2,1,0:T(8,128)(2,1)S(1)} all-to-all(bf16[8,128,384]{2,1,0:T(8,128)(2,1)S(1)} %shard_map.64), channel_id=1, replica_groups={{0,1,2,3,4,5,6,7},{8,9,10,11,12,13,14,15},{16,17,18,19,20,21,22,23},{24..., dimensions={0} | all-to-all | bytes 1572864 | tf_op jit(solution)/shard_map/all_to_all | solution.py:49
  131.0 0.1 shard_map.65
  131.1 18.0 %all_to_all.39 = bf16[8,16,384]{2,1,0:T(8,128)(2,1)S(1)} all-to-all(bf16[8,16,384]{2,1,0:T(8,128)(2,1)S(1)} %bitcast.29), channel_id=1, replica_groups=mesh['expert'=8,'tp'=128] {'expert'}, dimensions={0} | all-to-all | bytes 196608 | tf_op jit(solution)/shard_map/all_to_all | solution.py:49
  149.2 0.3 shard_map.66
  149.5 11.0 %all_to_all.40.part_ref = f32[4,24,128]{2,1,0:T(8,128)S(1)} all-to-all(f32[4,24,128]{2,1,0:T(8,128)S(1)} %shard_map.66), channel_id=1, replica_groups={{0,8,16,24},{1,9,17,25},{2,10,18,26},{3,11,19,27},{4,12,20,28},{5,13,21..., dimensions={0} | all-to-all | bytes 98304 | tf_op jit(solution)/shard_map/all_to_all | solution.py:49
  160.5 0.7 shard_map.67
  (1 shorter events, 0.0 us)
Async XLA Ops:
  0.0 0.7 copy-start.3
  1.4 26.0 %all-to-all-start = ((bf16[8,16,192]{2,1,0:T(8,128)(2,1)}), bf16[8,16,192]{2,1,0:T(8,128)(2,1)S(1)}, u32[]{:S(2)}, u32[]{:S(2)}) async-start(bf16[8,16,192]{2,1,0:T(8,128)(2,1)} %shard_map.55), calls=%async_computation | async-start | bytes 131072 | tf_op jit(solution)/shard_map/all_to_all | solution.py:49
  28.4 24.3 %all-to-all-start.1 = ((bf16[8,32,384]{2,1,0:T(8,128)(2,1)}), bf16[8,32,384]{2,1,0:T(8,128)(2,1)S(1)}, u32[]{:S(2)}, u32[]{:S(2)}) async-start(bf16[8,32,384]{2,1,0:T(8,128)(2,1)} %bitcast.4), calls=%async_computation.1 | async-start | bytes 393216 | tf_op jit(solution)/shard_map/all_to_all | solution.py:49
  37.6 27.1 %collective-permute-start = (bf16[256,128]{1,0:T(8,128)(2,1)}, bf16[256,128]{1,0:T(8,128)(2,1)S(1)}, u32[]{:S(2)}, u32[]{:S(2)}) collective-permute-start(bf16[256,128]{1,0:T(8,128)(2,1)} %bitcast.30), channel_id=1, source_target_pairs={{0,32},{1,33},{2,34},{3,35},{4,36},{5,37},{6,38},{7,39},{8,40},{9,... | collective-permute-start | bytes 196616 | tf_op jit(solution)/shard_map/ppermute | solution.py:45
  50.8 1.4 copy-start.4
  64.6 1.3 copy-start
  65.9 7.6 %collective-permute-start.1 = (bf16[256,512]{1,0:T(8,128)(2,1)}, bf16[256,512]{1,0:T(8,128)(2,1)S(1)}, u32[]{:S(2)}, u32[]{:S(2)}) collective-permute-start(bf16[256,512]{1,0:T(8,128)(2,1)} %shard_map.60), channel_id=1, source_target_pairs={{0,64},{1,65},{2,66},{3,67},{4,68},{5,69},{6,70},{7,71},{8,72},{9,... | collective-permute-start | bytes 786440 | tf_op jit(solution)/shard_map/ppermute | solution.py:45
  68.2 1.1 copy-start.1
  70.0 32.5 %copy-start.2 = (bf16[1,256,128]{2,1,0:T(8,128)(2,1)S(1)}, bf16[1,256,128]{2,1,0:T(8,128)(2,1)}, u32[]{:S(2)}) copy-start(bf16[1,256,128]{2,1,0:T(8,128)(2,1)} %param.9) | copy-start | bytes 196612
  102.6 9.1 %collective-permute-start.2 = (bf16[256,512]{1,0:T(8,128)(2,1)S(1)}, bf16[256,512]{1,0:T(8,128)(2,1)S(1)}, u32[]{:S(2)}, u32[]{:S(2)}) collective-permute-start(bf16[256,512]{1,0:T(8,128)(2,1)S(1)} %shard_map.62.grad_ref), channel_id=1, source_target_pairs={{0,64},{1,65},{2,66},{3,67},{4,68},{5,69},{6,70},{7,71},{8,72},{9,... | collective-permute-start | bytes 786440 | tf_op jit(solution)/shard_map/ppermute | solution.py:45

commit v8 on v7

--- a/solution.py
+++ b/solution.py
@@ -205,11 +205,10 @@
     slot_index = flat_routes * capacity + jnp.sum(before * named, axis=1)
     slot_index = slot_index.reshape(n_tok, 2).T
 
+    raw, gate, up, hidden = lax.optimization_barrier((raw, gate, up, hidden_grad[0]))
     outgoing = call(dispatch_kernel, shape((slot_total, wide), BF16), [], [slot_index, raw])
     arrived = over("expert", outgoing)
-    hidden = hidden_grad[0]
     hidden_far = swapped(hidden, ZH_BIT)
-    arrived, gate, up = lax.optimization_barrier((arrived, gate, up))
     rows = lax.all_gather(arrived, "tp", axis_index_groups=X_GROUPS, axis=0, tiled=False)
     rows, hidden_far = lax.optimization_barrier((rows, hidden_far))
 

time: 162 us -> 159 us (0.981)
  waiting for transfers between devices: 17.5 us -> 12.2 us
  blocking collectives: 88.4 us -> 90.3 us
    all_gather x1, blocking collectives: 28.8 us -> 32.7 us  [body(): lax.all_gather(send, 'tp', axis_index_groups=ZH_GROUPS, axis=0, tiled=False)]
    all_to_all x2, waiting for transfers between devices: 7.49 us -> 4.12 us  [over(): lax.all_to_all(shard, axis, split_axis=0, concat_axis=0, axis_index_group...]
    all_to_all x3, blocking collectives: 47.6 us -> 45.6 us  [over(): lax.all_to_all(shard, axis, split_axis=0, concat_axis=0, axis_index_group...]
    ppermute x3, waiting for transfers between devices: 10 us -> 8.07 us  [swapped(): lax.ppermute(shard, 'tp', [(i, i ^ bit) for i in range(lax.axis_size('tp'...]
    unnamed x13 -> x15, local copies, waits for them, and re-layouts: 5.86 us -> 6.42 us
  transfers between devices with their start and end apart: 5 -> 5, of which waited for: 3 -> 3; matrix products, arithmetic and copies ran while one was open for 3% -> 2% of each run, Pallas kernels for 1% -> 1%
where the time goes in v8:
time: 159 us; the launch traced here: 158 us
  blocking collectives  90.3 us (57%)
  starting transfers between devices  41.2 us (26%)
  waiting for transfers between devices  12.2 us (8%)
  local copies, waits for them, and re-layouts  6.77 us (4%)
  Pallas kernels  6.55 us (4%)
    all_to_all x3, blocking collectives, over(): lax.all_to_all(shard, axis, split_axis=0, concat_axis=0, axis_index_group...  45.6 us
    all_gather x1, blocking collectives, body(): lax.all_gather(send, 'tp', axis_index_groups=ZH_GROUPS, axis=0, tiled=False)  32.7 us
    all_to_all x2, starting transfers between devices, over(): lax.all_to_all(shard, axis, split_axis=0, concat_axis=0, axis_index_group...  25.4 us
    ppermute x3, starting transfers between devices, swapped(): lax.ppermute(shard, 'tp', [(i, i ^ bit) for i in range(lax.axis_size('tp'...  15.8 us
    all_gather x1, blocking collectives, body(): lax.all_gather(arrived, 'tp', axis_index_groups=X_GROUPS, axis=0, tiled=F...  12 us
    ppermute x3, waiting for transfers between devices, swapped(): lax.ppermute(shard, 'tp', [(i, i ^ bit) for i in range(lax.axis_size('tp'...  8.07 us
    pallas_call x13, Pallas kernels, call(): pl.pallas_call(kernel, out_shape=outs, in_specs=[SMEM] * len(scalars) + [...  6.55 us
    unnamed x15, local copies, waits for them, and re-layouts  6.42 us
  transfers between devices with their start and end apart: 5, of which 3 were waited for; matrix products, arithmetic and copies ran while one was open for 2% of the time, Pallas kernels for 1%

profile of v8, /device:TPU:1, one launch (start us, length us, event | category | flops | bytes accessed | tf_op | source)
XLA Modules:
  0.0 157.6 jit_solution(6783053549382183119)
XLA Ops:
  0.0 0.0 copy-start.3
  0.0 0.7 copy-done.3
  0.7 0.7 shard_map.55
  1.4 16.3 %all-to-all-start = ((bf16[8,16,192]{2,1,0:T(8,128)(2,1)}), bf16[8,16,192]{2,1,0:T(8,128)(2,1)S(1)}, u32[]{:S(2)}, u32[]{:S(2)}) async-start(bf16[8,16,192]{2,1,0:T(8,128)(2,1)} %shard_map.55), calls=%async_computation | async-start | bytes 131072 | tf_op jit(solution)/shard_map/all_to_all | solution.py:49
  17.7 0.8 copy.10
  18.4 0.1 eq.15
  18.6 0.1 fusion
  18.7 0.2 reduce_window_sum.11
  18.8 0.2 select_reduce_fusion
  19.0 0.1 reduce_sum.12
  19.2 0.1 copy.11
  19.2 1.7 %copy.17 = bf16[192,8,4,128]{3,1,2,0:T(8,128)(2,1)S(1)} copy(bf16[192,8,4,128]{3,2,1,0:T(4,128)(2,1)} %bitcast.30) | data formatting | bytes 3145728
  20.9 0.0 copy-start.4
  20.9 0.1 shard_map.56.gate_ref
  21.1 1.3 copy-done.4
  22.3 0.3 copy.16
  22.6 0.0 copy-start.5
  22.6 0.0 copy-start.2
  22.6 0.1 shard_map.57.up_ref
  22.8 0.5 copy-done.5
  23.3 4.1 %all-to-all-done.raw_ref = bf16[8,16,192]{2,1,0:T(8,128)(2,1)S(1)} async-done(((bf16[8,16,192]{2,1,0:T(8,128)(2,1)}), bf16[8,16,192]{2,1,0:T(8,128)(2,1)S(1)}, u32[]{:S(2)}, u32[]{:S(2)}) %all-to-all-start) | async-done | bytes 49184 | tf_op jit(solution)/shard_map/all_to_all | solution.py:49
  27.4 1.0 shard_map.58
  28.4 9.2 %all-to-all-start.1 = ((bf16[8,32,384]{2,1,0:T(8,128)(2,1)}), bf16[8,32,384]{2,1,0:T(8,128)(2,1)S(1)}, u32[]{:S(2)}, u32[]{:S(2)}) async-start(bf16[8,32,384]{2,1,0:T(8,128)(2,1)} %bitcast.5), calls=%async_computation.1 | async-start | bytes 393216 | tf_op jit(solution)/shard_map/all_to_all | solution.py:49
  37.6 0.0 copy-done.2
  37.6 11.6 %collective-permute-start = (bf16[256,128]{1,0:T(8,128)(2,1)S(1)}, bf16[256,128]{1,0:T(8,128)(2,1)S(1)}, u32[]{:S(2)}, u32[]{:S(2)}) collective-permute-start(bf16[256,128]{1,0:T(8,128)(2,1)S(1)} %bitcast.27), channel_id=1, source_target_pairs={{0,32},{1,33},{2,34},{3,35},{4,36},{5,37},{6,38},{7,39},{8,40},{9,... | collective-permute-start | bytes 196616 | tf_op jit(solution)/shard_map/ppermute | solution.py:45
  49.2 0.0 all-to-all-done.1
  49.2 12.0 %all_gather.13.rows_ref = bf16[4,256,384]{2,1,0:T(8,128)(2,1)S(1)} all-gather(bf16[1,256,384]{2,1,0:T(8,128)(2,1)S(1)} %bitcast.32), channel_id=1, replica_groups={{0,1,2,3},{4,5,6,7},{8,9,10,11},{12,13,14,15},{16,17,18,19},{20,21,22,2..., dimensions={0}, use_global_device_ids=true | all-gather | bytes 983040 | tf_op jit(solution)/shard_map/all_gather | solution.py:212
  61.2 0.0 copy-start
  61.2 0.0 collective-permute-done.far_ref
  61.2 1.3 shard_map.60
  62.4 0.0 copy-done
  62.4 2.3 %collective-permute-start.1 = (bf16[256,512]{1,0:T(8,128)(2,1)}, bf16[256,512]{1,0:T(8,128)(2,1)S(1)}, u32[]{:S(2)}, u32[]{:S(2)}) collective-permute-start(bf16[256,512]{1,0:T(8,128)(2,1)} %shard_map.60), channel_id=1, source_target_pairs={{0,64},{1,65},{2,66},{3,67},{4,68},{5,69},{6,70},{7,71},{8,72},{9,... | collective-permute-start | bytes 786440 | tf_op jit(solution)/shard_map/ppermute | solution.py:45
  64.7 0.0 copy-start.1
  64.8 1.1 copy-done.1
  65.9 0.6 shard_map.59.keep_ref
  66.5 3.6 %collective-permute-done.1.near_ref = bf16[256,512]{1,0:T(8,128)(2,1)S(1)} collective-permute-done((bf16[256,512]{1,0:T(8,128)(2,1)}, bf16[256,512]{1,0:T(8,128)(2,1)S(1)}, u32[]{:S(2)}, u32[]{:S(2)}) %collective-permute-start.1) | collective-permute-done | bytes 262176 | tf_op jit(solution)/shard_map/ppermute | solution.py:45
  70.1 32.7 %all-gather = bf16[512,512]{1,0:T(8,128)(2,1)S(1)} all-gather(bf16[256,512]{1,0:T(8,128)(2,1)S(1)} %shard_map.61), channel_id=2, replica_groups={{0,32},{1,33},{2,34},{3,35},{4,36},{5,37},{6,38},{7,39},{8,40},{9,41},{..., dimensions={0}, use_global_device_ids=true | all-gather | bytes 786432 | tf_op jit(solution)/shard_map/all_gather | solution.py:235
  102.8 0.2 shard_map.62.grad_ref
  103.0 1.9 %collective-permute-start.2 = (bf16[256,512]{1,0:T(8,128)(2,1)S(1)}, bf16[256,512]{1,0:T(8,128)(2,1)S(1)}, u32[]{:S(2)}, u32[]{:S(2)}) collective-permute-start(bf16[256,512]{1,0:T(8,128)(2,1)S(1)} %shard_map.62.grad_ref), channel_id=1, source_target_pairs={{0,64},{1,65},{2,66},{3,67},{4,68},{5,69},{6,70},{7,71},{8,72},{9,... | collective-permute-start | bytes 786440 | tf_op jit(solution)/shard_map/ppermute | solution.py:45
  104.9 0.7 shard_map.63.held_ref
  105.6 4.5 %collective-permute-done.2.grad_ref = bf16[256,512]{1,0:T(8,128)(2,1)S(1)} collective-permute-done((bf16[256,512]{1,0:T(8,128)(2,1)S(1)}, bf16[256,512]{1,0:T(8,128)(2,1)S(1)}, u32[]{:S(2)}, u32[]{:S(2)}) %collective-permute-start.2) | collective-permute-done | bytes 262176 | tf_op jit(solution)/shard_map/ppermute | solution.py:45
  110.1 0.8 shard_map.64
  110.9 16.4 %all_to_all.35.pieces_ref = bf16[8,128,384]{2,1,0:T(8,128)(2,1)S(1)} all-to-all(bf16[8,128,384]{2,1,0:T(8,128)(2,1)S(1)} %shard_map.64), channel_id=1, replica_groups={{0,1,2,3,4,5,6,7},{8,9,10,11,12,13,14,15},{16,17,18,19,20,21,22,23},{24..., dimensions={0} | all-to-all | bytes 1572864 | tf_op jit(solution)/shard_map/all_to_all | solution.py:49
  127.3 0.1 shard_map.65
  127.4 17.7 %all_to_all.36 = bf16[8,16,384]{2,1,0:T(8,128)(2,1)S(1)} all-to-all(bf16[8,16,384]{2,1,0:T(8,128)(2,1)S(1)} %bitcast.26), channel_id=1, replica_groups=mesh['expert'=8,'tp'=128] {'expert'}, dimensions={0} | all-to-all | bytes 196608 | tf_op jit(solution)/shard_map/all_to_all | solution.py:49
  145.0 0.3 shard_map.66
  145.3 11.6 %all_to_all.37.part_ref = f32[4,24,128]{2,1,0:T(8,128)S(1)} all-to-all(f32[4,24,128]{2,1,0:T(8,128)S(1)} %shard_map.66), channel_id=1, replica_groups={{0,8,16,24},{1,9,17,25},{2,10,18,26},{3,11,19,27},{4,12,20,28},{5,13,21..., dimensions={0} | all-to-all | bytes 98304 | tf_op jit(solution)/shard_map/all_to_all | solution.py:49
  156.9 0.7 shard_map.67
  (2 shorter events, 0.1 us)
Async XLA Ops:
  0.0 0.7 copy-start.3
  1.4 26.0 %all-to-all-start = ((bf16[8,16,192]{2,1,0:T(8,128)(2,1)}), bf16[8,16,192]{2,1,0:T(8,128)(2,1)S(1)}, u32[]{:S(2)}, u32[]{:S(2)}) async-start(bf16[8,16,192]{2,1,0:T(8,128)(2,1)} %shard_map.55), calls=%async_computation | async-start | bytes 131072 | tf_op jit(solution)/shard_map/all_to_all | solution.py:49
  20.9 1.4 copy-start.4
  22.6 0.7 copy-start.5
  22.6 14.9 %copy-start.2 = (bf16[1,256,128]{2,1,0:T(8,128)(2,1)S(1)}, bf16[1,256,128]{2,1,0:T(8,128)(2,1)}, u32[]{:S(2)}) copy-start(bf16[1,256,128]{2,1,0:T(8,128)(2,1)} %param.9) | copy-start | bytes 196612
  28.4 20.8 %all-to-all-start.1 = ((bf16[8,32,384]{2,1,0:T(8,128)(2,1)}), bf16[8,32,384]{2,1,0:T(8,128)(2,1)S(1)}, u32[]{:S(2)}, u32[]{:S(2)}) async-start(bf16[8,32,384]{2,1,0:T(8,128)(2,1)} %bitcast.5), calls=%async_computation.1 | async-start | bytes 393216 | tf_op jit(solution)/shard_map/all_to_all | solution.py:49
  37.6 23.6 %collective-permute-start = (bf16[256,128]{1,0:T(8,128)(2,1)S(1)}, bf16[256,128]{1,0:T(8,128)(2,1)S(1)}, u32[]{:S(2)}, u32[]{:S(2)}) collective-permute-start(bf16[256,128]{1,0:T(8,128)(2,1)S(1)} %bitcast.27), channel_id=1, source_target_pairs={{0,32},{1,33},{2,34},{3,35},{4,36},{5,37},{6,38},{7,39},{8,40},{9,... | collective-permute-start | bytes 196616 | tf_op jit(solution)/shard_map/ppermute | solution.py:45
  61.2 1.3 copy-start
  62.4 7.6 %collective-permute-start.1 = (bf16[256,512]{1,0:T(8,128)(2,1)}, bf16[256,512]{1,0:T(8,128)(2,1)S(1)}, u32[]{:S(2)}, u32[]{:S(2)}) collective-permute-start(bf16[256,512]{1,0:T(8,128)(2,1)} %shard_map.60), channel_id=1, source_target_pairs={{0,64},{1,65},{2,66},{3,67},{4,68},{5,69},{6,70},{7,71},{8,72},{9,... | collective-permute-start | bytes 786440 | tf_op jit(solution)/shard_map/ppermute | solution.py:45
  64.7 1.1 copy-start.1
  103.0 7.1 %collective-permute-start.2 = (bf16[256,512]{1,0:T(8,128)(2,1)S(1)}, bf16[256,512]{1,0:T(8,128)(2,1)S(1)}, u32[]{:S(2)}, u32[]{:S(2)}) collective-permute-start(bf16[256,512]{1,0:T(8,128)(2,1)S(1)} %shard_map.62.grad_ref), channel_id=1, source_target_pairs={{0,64},{1,65},{2,66},{3,67},{4,68},{5,69},{6,70},{7,71},{8,72},{9,... | collective-permute-start | bytes 786440 | tf_op jit(solution)/shard_map/ppermute | solution.py:45

commit v9 on v8

--- a/solution.py
+++ b/solution.py
@@ -5,22 +5,14 @@
 from jax import lax
 from jax.experimental import pallas as pl
 from jax.experimental.pallas import tpu as pltpu
+from jax.sharding import Mesh
 from jax.sharding import PartitionSpec as P
 
 NX, NZL, NK = 4, 8, 4
 ORDER = [2 * k + z0 for z0 in range(2) for k in range(NK)]
 FEW, TILE = 16, 128
 
-
-def groups(bits, count=128):
-    mask = sum(1 << b for b in bits)
-    spread = [sum(((k >> i) & 1) << b for i, b in enumerate(bits)) for k in range(1 << len(bits))]
-    return [[base | v for v in spread] for base in range(count) if not base & mask]
-
-
-X_GROUPS, ZL_GROUPS, ZH_GROUPS = groups((0, 1)), groups((2, 3, 4)), groups((5,))
-M_GROUPS, K_GROUPS = groups((0, 1, 2)), groups((3, 4))
-Y_BIT, ZH_BIT = 64, 32
+AXES = ("expert", "y", "zh", "k", "z0", "x")
 F32, BF16 = jnp.float32, jnp.bfloat16
 NT = (((1,), (1,)), ((), ()))
 TN = (((0,), (0,)), ((), ()))
@@ -41,14 +33,16 @@
     )(*scalars, *arrays)
 
 
-def swapped(shard, bit):
-    return lax.ppermute(shard, "tp", [(i, i ^ bit) for i in range(lax.axis_size("tp"))])
-
-
-def over(axis, shard, groups=None):
-    return lax.all_to_all(
-        shard, axis, split_axis=0, concat_axis=0, axis_index_groups=groups, tiled=True
-    )
+def swapped(shard, axis):
+    return lax.ppermute(shard, axis, [(0, 1), (1, 0)])
+
+
+def over(axes, shard):
+    return lax.all_to_all(shard, axes, split_axis=0, concat_axis=0, tiled=True)
+
+
+def gathered(axis, shard):
+    return lax.all_gather(shard, axis, axis=0, tiled=False)
 
 
 def dot(a, b, dims=(((1,), (0,)), ((), ()))):
@@ -148,9 +142,16 @@
 
 def sum_kernel(pieces_ref, out_ref):
     total = pieces_ref[0].astype(F32)
-    for x in range(1, pieces_ref.shape[0]):
-        total = total + pieces_ref[x].astype(F32)
-    out_ref[...] = total.astype(BF16)
+    for m in range(1, pieces_ref.shape[0]):
+        total = total + pieces_ref[m].astype(F32)
+    total = total.astype(BF16)
+    wide = total.shape[1] // 2
+    feat = wide // NK
+    for k in range(NK):
+        part = [total[:, h * wide + k * feat : h * wide + (k + 1) * feat] for h in range(2)]
+        part = jnp.concatenate(part, axis=1)
+        for e in range(TILE // FEW):
+            out_ref[e * NK + k] = part[e * FEW : (e + 1) * FEW]
 
 
 def returned_rows(slot_ref, half):
@@ -158,29 +159,22 @@
     return jnp.right_shift(row, 4) * (2 * FEW) + half * FEW + jnp.bitwise_and(row, FEW - 1)
 
 
-def combine_kernel(slot_ref, back_ref, out_ref):
-    wide = back_ref.shape[1] // 2
-    back = back_ref[...]
-    part = [dot(back, one_hot(slot_ref, returned_rows(slot_ref, h)), TN) for h in range(2)]
-    part = part[0][:wide] + part[1][wide:]
-    rows = out_ref.shape[1]
-    for k in range(out_ref.shape[0]):
-        low = part[2 * k * rows : (2 * k + 1) * rows]
-        out_ref[k] = jnp.concatenate([low, part[(2 * k + 1) * rows : (2 * k + 2) * rows]], axis=1)
-
-
-def finish_kernel(part_ref, out_ref):
-    total = part_ref[0]
-    for z in range(1, part_ref.shape[0]):
-        total = total + part_ref[z]
-    n_tok = out_ref.shape[1]
-    out_ref[...] = jnp.concatenate([total[:, :n_tok], total[:, n_tok:]], axis=0).astype(BF16)
+def finish_kernel(slot_ref, back_ref, out_ref):
+    feat = out_ref.shape[0]
+    slots = []
+    for e in range(TILE // FEW):
+        total = back_ref[e * NK].astype(F32)
+        for k in range(1, NK):
+            total = total + back_ref[e * NK + k].astype(F32)
+        slots.append(total.astype(BF16))
+    slots = jnp.concatenate(slots, axis=0)
+    part = [dot(slots, one_hot(slot_ref, returned_rows(slot_ref, h)), TN) for h in range(2)]
+    out_ref[...] = (part[0][:feat] + part[1][feat:]).astype(BF16)
 
 
 def body(tokens, routes, w_gate, w_up, hidden_grad):
-    position = lax.axis_index("tp")
-    y_at = jnp.bitwise_and(jnp.right_shift(position, 6), 1).reshape(1)
-    zh_at = jnp.bitwise_and(jnp.right_shift(position, 5), 1).reshape(1)
+    y_at = lax.axis_index("y").astype(jnp.int32).reshape(1)
+    zh_at = lax.axis_index("zh").astype(jnp.int32).reshape(1)
     n_groups = lax.axis_size("expert")
     slot_total = hidden_grad.shape[1]
     capacity = slot_total // n_groups
@@ -197,7 +191,7 @@
     ]
 
     packed = call(pack_kernel, shape((NZL, feat // 3, 3 * n_tok), BF16), [], [tokens.T])
-    raw = over("tp", packed, ZL_GROUPS)
+    raw = over(("k", "z0"), packed)
 
     flat_routes = routes.reshape(n_tok * 2)
     named = (flat_routes[:, None] == jnp.arange(n_groups, dtype=jnp.int32)[None, :]).astype(jnp.int32)
@@ -208,8 +202,8 @@
     raw, gate, up, hidden = lax.optimization_barrier((raw, gate, up, hidden_grad[0]))
     outgoing = call(dispatch_kernel, shape((slot_total, wide), BF16), [], [slot_index, raw])
     arrived = over("expert", outgoing)
-    hidden_far = swapped(hidden, ZH_BIT)
-    rows = lax.all_gather(arrived, "tp", axis_index_groups=X_GROUPS, axis=0, tiled=False)
+    hidden_far = swapped(hidden, "zh")
+    rows = gathered("x", arrived)
     rows, hidden_far = lax.optimization_barrier((rows, hidden_far))
 
     n_flops = 2 * slot_total * block_rows * half
@@ -230,9 +224,9 @@
         n_flops,
         16,
     )
-    near = swapped(send, Y_BIT)
+    near = swapped(send, "y")
     send = call(near_kernel, shape((slot_total, half), BF16), [], [keep, near])
-    both = lax.all_gather(send, "tp", axis_index_groups=ZH_GROUPS, axis=0, tiled=False)
+    both = gathered("zh", send)
 
     grads = call(
         grad_kernel,
@@ -240,7 +234,7 @@
         [zh_at],
         [keep, near, both, hidden, hidden_far],
     )
-    other = swapped(grads, Y_BIT)
+    other = swapped(grads, "y")
     held = call(
         backward_own_kernel,
         shape((NX, slot_total, wide), F32),
@@ -257,24 +251,21 @@
         n_flops,
         16,
     )
-    pieces = over("tp", pieces, M_GROUPS)
-    summed = call(sum_kernel, shape((TILE, wide), BF16), [], [pieces])
-    returned = over("expert", summed)
-
-    part = call(combine_kernel, shape((NK, feat // 2, 2 * n_tok), F32), [], [slot_index, returned])
-    part = over("tp", part, K_GROUPS)
-    total = call(finish_kernel, shape((feat, n_tok), BF16), [], [part])
+    pieces = over(("z0", "x"), pieces)
+    parts = call(sum_kernel, shape((n_groups * NK, FEW, 2 * feat), BF16), [], [pieces])
+    parts = over(("expert", "k"), parts)
+    total = call(finish_kernel, shape((feat, n_tok), BF16), [], [slot_index, parts])
     return total.T
 
 
 def solution(mesh):
+    tp = AXES[1:]
+    cut = Mesh(mesh.devices.reshape(-1, 2, 2, NK, 2, NX), AXES)
     placed = (
-        P("expert", "tp"),
+        P("expert", tp),
         P("expert", None),
-        P("expert", "tp", None, None, None),
-        P("expert", "tp", None, None, None),
-        P("expert", None, "tp"),
-    )
-    return jax.shard_map(
-        body, mesh=mesh, in_specs=placed, out_specs=P("expert", "tp"), check_vma=False
-    )
+        P("expert", tp, None, None, None),
+        P("expert", tp, None, None, None),
+        P("expert", None, tp),
+    )
+    return jax.shard_map(body, mesh=cut, in_specs=placed, out_specs=P("expert", tp), check_vma=False)

time: 159 us -> 158 us (level)
    all_to_all x3 -> x2, blocking collectives: 45.6 us -> 45 us  [over(): return lax.all_to_all(shard, axes, split_axis=0, concat_axis=0, tiled=True)]
    pallas_call x13 -> x12, Pallas kernels: 6.55 us -> 6.46 us  [call(): pl.pallas_call(kernel, out_shape=outs, in_specs=[SMEM] * len(scalars) + [...]
where the time goes in v9:
time: 158 us; the launch traced here: 157 us
  blocking collectives  89.6 us (57%)
  starting transfers between devices  41.2 us (26%)
  waiting for transfers between devices  12.2 us (8%)
  local copies, waits for them, and re-layouts  6.77 us (4%)
  Pallas kernels  6.46 us (4%)
    all_to_all x2, blocking collectives, over(): return lax.all_to_all(shard, axes, split_axis=0, concat_axis=0, tiled=True)  45 us
    all_gather x2, blocking collectives, gathered(): return lax.all_gather(shard, axis, axis=0, tiled=False)  44.6 us
    all_to_all x2, starting transfers between devices, over(): return lax.all_to_all(shard, axes, split_axis=0, concat_axis=0, tiled=True)  25.4 us
    ppermute x3, starting transfers between devices, swapped(): return lax.ppermute(shard, axis, [(0, 1), (1, 0)])  15.8 us
    ppermute x3, waiting for transfers between devices, swapped(): return lax.ppermute(shard, axis, [(0, 1), (1, 0)])  8.07 us
    pallas_call x12, Pallas kernels, call(): pl.pallas_call(kernel, out_shape=outs, in_specs=[SMEM] * len(scalars) + [...  6.46 us
    unnamed x15, local copies, waits for them, and re-layouts  6.42 us
    all_to_all x2, waiting for transfers between devices, over(): return lax.all_to_all(shard, axes, split_axis=0, concat_axis=0, tiled=True)  4.12 us
  transfers between devices with their start and end apart: 5, of which 3 were waited for; matrix products, arithmetic and copies ran while one was open for 2% of the time, Pallas kernels for 1%

profile of v9, /device:TPU:1, one launch (start us, length us, event | category | flops | bytes accessed | tf_op | source)
XLA Modules:
  0.0 156.9 jit_solution(2899081529614759933)
XLA Ops:
  0.0 0.0 copy-start.3
  0.0 0.7 copy-done.3
  0.7 0.7 shard_map.55
  1.4 16.3 %all-to-all-start = ((bf16[8,16,192]{2,1,0:T(8,128)(2,1)}), bf16[8,16,192]{2,1,0:T(8,128)(2,1)S(1)}, u32[]{:S(2)}, u32[]{:S(2)}) async-start(bf16[8,16,192]{2,1,0:T(8,128)(2,1)} %shard_map.55), calls=%async_computation | async-start | bytes 131072 | tf_op jit(solution)/shard_map/all_to_all | solution.py:41
  17.7 0.8 copy.10
  18.4 0.1 eq.15
  18.6 0.1 fusion
  18.7 0.2 reduce_window_sum.11
  18.8 0.2 select_reduce_fusion
  19.0 0.1 reduce_sum.12
  19.2 0.1 copy.11
  19.2 1.7 %copy.17 = bf16[192,8,4,128]{3,1,2,0:T(8,128)(2,1)S(1)} copy(bf16[192,8,4,128]{3,2,1,0:T(4,128)(2,1)} %bitcast.26) | data formatting | bytes 3145728
  20.9 0.0 copy-start.4
  20.9 0.1 shard_map.56.gate_ref
  21.1 1.3 copy-done.4
  22.3 0.3 copy.16
  22.6 0.0 copy-start.5
  22.6 0.0 copy-start.2
  22.6 0.1 shard_map.57.up_ref
  22.8 0.5 copy-done.5
  23.3 4.1 %all-to-all-done.raw_ref = bf16[8,16,192]{2,1,0:T(8,128)(2,1)S(1)} async-done(((bf16[8,16,192]{2,1,0:T(8,128)(2,1)}), bf16[8,16,192]{2,1,0:T(8,128)(2,1)S(1)}, u32[]{:S(2)}, u32[]{:S(2)}) %all-to-all-start) | async-done | bytes 49184 | tf_op jit(solution)/shard_map/all_to_all | solution.py:41
  27.4 1.0 shard_map.58
  28.4 9.2 %all-to-all-start.1 = ((bf16[8,32,384]{2,1,0:T(8,128)(2,1)}), bf16[8,32,384]{2,1,0:T(8,128)(2,1)S(1)}, u32[]{:S(2)}, u32[]{:S(2)}) async-start(bf16[8,32,384]{2,1,0:T(8,128)(2,1)} %bitcast.5), calls=%async_computation.1 | async-start | bytes 393216 | tf_op jit(solution)/shard_map/all_to_all | solution.py:41
  37.6 0.0 copy-done.2
  37.6 11.6 %collective-permute-start = (bf16[256,128]{1,0:T(8,128)(2,1)S(1)}, bf16[256,128]{1,0:T(8,128)(2,1)S(1)}, u32[]{:S(2)}, u32[]{:S(2)}) collective-permute-start(bf16[256,128]{1,0:T(8,128)(2,1)S(1)} %bitcast.23), channel_id=1, source_target_pairs={{0,32},{32,0},{1,33},{33,1},{2,34},{34,2},{3,35},{35,3},{4,36},{36... | collective-permute-start | bytes 196616 | tf_op jit(solution)/shard_map/ppermute | solution.py:37
  49.2 0.0 all-to-all-done.1
  49.2 12.0 %all_gather.13.rows_ref = bf16[4,256,384]{2,1,0:T(8,128)(2,1)S(1)} all-gather(bf16[1,256,384]{2,1,0:T(8,128)(2,1)S(1)} %bitcast.28), channel_id=1, replica_groups=mesh['expert'=8,'y'=2,'zh'=2,'k'=4,'z0'=2,'x'=4] {'x'}, dimensions={0}, use_global_device_ids=true | all-gather | bytes 983040 | tf_op jit(solution)/shard_map/all_gather | solution.py:45
  61.2 0.0 copy-start
  61.2 0.0 collective-permute-done.far_ref
  61.2 1.3 shard_map.60
  62.4 0.0 copy-done
  62.4 2.3 %collective-permute-start.1 = (bf16[256,512]{1,0:T(8,128)(2,1)}, bf16[256,512]{1,0:T(8,128)(2,1)S(1)}, u32[]{:S(2)}, u32[]{:S(2)}) collective-permute-start(bf16[256,512]{1,0:T(8,128)(2,1)} %shard_map.60), channel_id=1, source_target_pairs={{0,64},{64,0},{1,65},{65,1},{2,66},{66,2},{3,67},{67,3},{4,68},{68... | collective-permute-start | bytes 786440 | tf_op jit(solution)/shard_map/ppermute | solution.py:37
  64.7 0.0 copy-start.1
  64.8 1.1 copy-done.1
  65.9 0.6 shard_map.59.keep_ref
  66.5 3.6 %collective-permute-done.1.near_ref = bf16[256,512]{1,0:T(8,128)(2,1)S(1)} collective-permute-done((bf16[256,512]{1,0:T(8,128)(2,1)}, bf16[256,512]{1,0:T(8,128)(2,1)S(1)}, u32[]{:S(2)}, u32[]{:S(2)}) %collective-permute-start.1) | collective-permute-done | bytes 262176 | tf_op jit(solution)/shard_map/ppermute | solution.py:37
  70.1 32.7 %all-gather = bf16[512,512]{1,0:T(8,128)(2,1)S(1)} all-gather(bf16[256,512]{1,0:T(8,128)(2,1)S(1)} %shard_map.61), channel_id=2, replica_groups=mesh['expert'=8,'y'=2,'zh'=2,'k'=4,'z0'=2,'x'=4] {'zh'}, dimensions={0}, use_global_device_ids=true | all-gather | bytes 786432 | tf_op jit(solution)/shard_map/all_gather | solution.py:45
  102.8 0.2 shard_map.62.grad_ref
  103.0 1.9 %collective-permute-start.2 = (bf16[256,512]{1,0:T(8,128)(2,1)S(1)}, bf16[256,512]{1,0:T(8,128)(2,1)S(1)}, u32[]{:S(2)}, u32[]{:S(2)}) collective-permute-start(bf16[256,512]{1,0:T(8,128)(2,1)S(1)} %shard_map.62.grad_ref), channel_id=1, source_target_pairs={{0,64},{64,0},{1,65},{65,1},{2,66},{66,2},{3,67},{67,3},{4,68},{68... | collective-permute-start | bytes 786440 | tf_op jit(solution)/shard_map/ppermute | solution.py:37
  104.9 0.7 shard_map.63.held_ref
  105.6 4.5 %collective-permute-done.2.grad_ref = bf16[256,512]{1,0:T(8,128)(2,1)S(1)} collective-permute-done((bf16[256,512]{1,0:T(8,128)(2,1)S(1)}, bf16[256,512]{1,0:T(8,128)(2,1)S(1)}, u32[]{:S(2)}, u32[]{:S(2)}) %collective-permute-start.2) | collective-permute-done | bytes 262176 | tf_op jit(solution)/shard_map/ppermute | solution.py:37
  110.1 0.8 shard_map.64
  110.9 16.4 %all_to_all.24.pieces_ref = bf16[8,128,384]{2,1,0:T(8,128)(2,1)S(1)} all-to-all(bf16[8,128,384]{2,1,0:T(8,128)(2,1)S(1)} %shard_map.64), channel_id=1, replica_groups=mesh['expert'=8,'y'=2,'zh'=2,'k'=4,'z0'=2,'x'=4] {'z0','x'}, dimensions={0} | all-to-all | bytes 1572864 | tf_op jit(solution)/shard_map/all_to_all | solution.py:41
  127.3 0.2 shard_map.65
  127.5 28.6 %all_to_all.25.back_ref = bf16[32,16,96]{2,1,0:T(8,128)(2,1)S(1)} all-to-all(bf16[32,16,96]{2,1,0:T(8,128)(2,1)S(1)} %shard_map.65), channel_id=1, replica_groups=mesh['expert'=8,'y'=2,'zh'=2,'k'=4,'z0'=2,'x'=4] {'expert','k'}, dimensions={0} | all-to-all | bytes 196608 | tf_op jit(solution)/shard_map/all_to_all | solution.py:41
  156.1 0.8 shard_map.66
  (2 shorter events, 0.1 us)
Async XLA Ops:
  0.0 0.7 copy-start.3
  1.4 26.0 %all-to-all-start = ((bf16[8,16,192]{2,1,0:T(8,128)(2,1)}), bf16[8,16,192]{2,1,0:T(8,128)(2,1)S(1)}, u32[]{:S(2)}, u32[]{:S(2)}) async-start(bf16[8,16,192]{2,1,0:T(8,128)(2,1)} %shard_map.55), calls=%async_computation | async-start | bytes 131072 | tf_op jit(solution)/shard_map/all_to_all | solution.py:41
  20.9 1.4 copy-start.4
  22.6 0.7 copy-start.5
  22.6 14.9 %copy-start.2 = (bf16[1,256,128]{2,1,0:T(8,128)(2,1)S(1)}, bf16[1,256,128]{2,1,0:T(8,128)(2,1)}, u32[]{:S(2)}) copy-start(bf16[1,256,128]{2,1,0:T(8,128)(2,1)} %param.9) | copy-start | bytes 196612
  28.4 20.8 %all-to-all-start.1 = ((bf16[8,32,384]{2,1,0:T(8,128)(2,1)}), bf16[8,32,384]{2,1,0:T(8,128)(2,1)S(1)}, u32[]{:S(2)}, u32[]{:S(2)}) async-start(bf16[8,32,384]{2,1,0:T(8,128)(2,1)} %bitcast.5), calls=%async_computation.1 | async-start | bytes 393216 | tf_op jit(solution)/shard_map/all_to_all | solution.py:41
  37.6 23.6 %collective-permute-start = (bf16[256,128]{1,0:T(8,128)(2,1)S(1)}, bf16[256,128]{1,0:T(8,128)(2,1)S(1)}, u32[]{:S(2)}, u32[]{:S(2)}) collective-permute-start(bf16[256,128]{1,0:T(8,128)(2,1)S(1)} %bitcast.23), channel_id=1, source_target_pairs={{0,32},{32,0},{1,33},{33,1},{2,34},{34,2},{3,35},{35,3},{4,36},{36... | collective-permute-start | bytes 196616 | tf_op jit(solution)/shard_map/ppermute | solution.py:37
  61.2 1.3 copy-start
  62.4 7.6 %collective-permute-start.1 = (bf16[256,512]{1,0:T(8,128)(2,1)}, bf16[256,512]{1,0:T(8,128)(2,1)S(1)}, u32[]{:S(2)}, u32[]{:S(2)}) collective-permute-start(bf16[256,512]{1,0:T(8,128)(2,1)} %shard_map.60), channel_id=1, source_target_pairs={{0,64},{64,0},{1,65},{65,1},{2,66},{66,2},{3,67},{67,3},{4,68},{68... | collective-permute-start | bytes 786440 | tf_op jit(solution)/shard_map/ppermute | solution.py:37
  64.7 1.1 copy-start.1
  103.0 7.1 %collective-permute-start.2 = (bf16[256,512]{1,0:T(8,128)(2,1)S(1)}, bf16[256,512]{1,0:T(8,128)(2,1)S(1)}, u32[]{:S(2)}, u32[]{:S(2)}) collective-permute-start(bf16[256,512]{1,0:T(8,128)(2,1)S(1)} %shard_map.62.grad_ref), channel_id=1, source_target_pairs={{0,64},{64,0},{1,65},{65,1},{2,66},{66,2},{3,67},{67,3},{4,68},{68... | collective-permute-start | bytes 786440 | tf_op jit(solution)/shard_map/ppermute | solution.py:37

commit v10 on v9

--- a/solution.py
+++ b/solution.py
@@ -57,27 +57,43 @@
         out_ref[z] = packed
 
 
-def arrange_kernel(in_ref, out_ref):
-    feat = in_ref.shape[0] // (NX * NZL)
+def arrange_kernel(gate_ref, up_ref, gate_out_ref, up_out_ref):
+    feat = gate_ref.shape[0] // (NX * NZL)
     for x in range(NX):
         for at, z in enumerate(ORDER):
             src, dst = (z * NX + x) * feat, (x * NZL + at) * feat
-            out_ref[dst : dst + feat] = in_ref[src : src + feat]
-
-
-def one_hot(slot_ref, slots):
-    hit = (slots == slot_ref[0:1, :]) | (slots == slot_ref[1:2, :])
-    return jnp.where(hit, 1.0, 0.0).astype(BF16)
-
-
-def dispatch_kernel(slot_ref, raw_ref, out_ref):
-    n_tok = slot_ref.shape[1]
+            gate_out_ref[dst : dst + feat] = gate_ref[src : src + feat]
+            up_out_ref[dst : dst + feat] = up_ref[src : src + feat]
+
+
+def slots_of(routes_ref):
+    named = routes_ref[...].astype(F32)
+    shape = (named.shape[1], named.shape[1])
+    before, now = (lax.broadcasted_iota(jnp.int32, shape, axis) for axis in range(2))
+    turned = [
+        jnp.sum(jnp.where(before == now, named[j : j + 1], 0.0), axis=1, keepdims=True) for j in range(2)
+    ]
+    slots = []
+    for k in range(2):
+        own = named[k : k + 1]
+        same = jnp.where(turned[0] == own, 1.0, 0.0) + jnp.where(turned[1] == own, 1.0, 0.0)
+        place = jnp.sum(jnp.where(before < now, same, 0.0), axis=0, keepdims=True)
+        slots.append((own * (2.0 * FEW) + place).astype(jnp.int32))
+    return slots
+
+
+def one_hot(taken, slots):
+    return jnp.where((slots == taken[0]) | (slots == taken[1]), 1.0, 0.0).astype(BF16)
+
+
+def dispatch_kernel(routes_ref, raw_ref, out_ref):
+    n_tok = routes_ref.shape[1]
     pieces = [
         raw_ref[z, :, j * n_tok : (j + 1) * n_tok] for z in ORDER for j in range(3)
     ]
     raw = jnp.concatenate(pieces, axis=0)
     slots = lax.broadcasted_iota(jnp.int32, (out_ref.shape[0], n_tok), 0)
-    out_ref[...] = dot(one_hot(slot_ref, slots), raw, NT).astype(BF16)
+    out_ref[...] = dot(one_hot(slots_of(routes_ref), slots), raw, NT).astype(BF16)
 
 
 def halves(y_ref, width):
@@ -154,13 +170,14 @@
             out_ref[e * NK + k] = part[e * FEW : (e + 1) * FEW]
 
 
-def returned_rows(slot_ref, half):
-    row = lax.broadcasted_iota(jnp.int32, (TILE, slot_ref.shape[1]), 0)
+def returned_rows(n_tok, half):
+    row = lax.broadcasted_iota(jnp.int32, (TILE, n_tok), 0)
     return jnp.right_shift(row, 4) * (2 * FEW) + half * FEW + jnp.bitwise_and(row, FEW - 1)
 
 
-def finish_kernel(slot_ref, back_ref, out_ref):
-    feat = out_ref.shape[0]
+def finish_kernel(routes_ref, back_ref, out_ref):
+    feat, n_tok = out_ref.shape
+    taken = slots_of(routes_ref)
     slots = []
     for e in range(TILE // FEW):
         total = back_ref[e * NK].astype(F32)
@@ -168,7 +185,7 @@
             total = total + back_ref[e * NK + k].astype(F32)
         slots.append(total.astype(BF16))
     slots = jnp.concatenate(slots, axis=0)
-    part = [dot(slots, one_hot(slot_ref, returned_rows(slot_ref, h)), TN) for h in range(2)]
+    part = [dot(slots, one_hot(taken, returned_rows(n_tok, h)), TN) for h in range(2)]
     out_ref[...] = (part[0][:feat] + part[1][feat:]).astype(BF16)
 
 
@@ -177,7 +194,6 @@
     zh_at = lax.axis_index("zh").astype(jnp.int32).reshape(1)
     n_groups = lax.axis_size("expert")
     slot_total = hidden_grad.shape[1]
-    capacity = slot_total // n_groups
     n_tok, feat = tokens.shape
     block_rows = w_gate.shape[2]
     hid = w_gate.shape[4]
@@ -185,22 +201,14 @@
     shape = jax.ShapeDtypeStruct
 
     half = 4 * hid
-    gate, up = [
-        call(arrange_kernel, shape((block_rows, half), BF16), [], [w[0, 0].reshape(block_rows, half)])
-        for w in (w_gate, w_up)
-    ]
+    flat = [w[0, 0].reshape(block_rows, half) for w in (w_gate, w_up)]
+    gate, up = call(arrange_kernel, [shape((block_rows, half), BF16)] * 2, [], flat, mib=16)
 
     packed = call(pack_kernel, shape((NZL, feat // 3, 3 * n_tok), BF16), [], [tokens.T])
     raw = over(("k", "z0"), packed)
 
-    flat_routes = routes.reshape(n_tok * 2)
-    named = (flat_routes[:, None] == jnp.arange(n_groups, dtype=jnp.int32)[None, :]).astype(jnp.int32)
-    before = jnp.cumsum(named, axis=0) - named
-    slot_index = flat_routes * capacity + jnp.sum(before * named, axis=1)
-    slot_index = slot_index.reshape(n_tok, 2).T
-
     raw, gate, up, hidden = lax.optimization_barrier((raw, gate, up, hidden_grad[0]))
-    outgoing = call(dispatch_kernel, shape((slot_total, wide), BF16), [], [slot_index, raw])
+    outgoing = call(dispatch_kernel, shape((slot_total, wide), BF16), [], [routes.T, raw])
     arrived = over("expert", outgoing)
     hidden_far = swapped(hidden, "zh")
     rows = gathered("x", arrived)
@@ -254,7 +262,7 @@
     pieces = over(("z0", "x"), pieces)
     parts = call(sum_kernel, shape((n_groups * NK, FEW, 2 * feat), BF16), [], [pieces])
     parts = over(("expert", "k"), parts)
-    total = call(finish_kernel, shape((feat, n_tok), BF16), [], [slot_index, parts])
+    total = call(finish_kernel, shape((feat, n_tok), BF16), [], [routes.T, parts])
     return total.T
 
 

time: 158 us -> 156 us (0.987)
  waiting for transfers between devices: 12.2 us -> 17 us
  blocking collectives: 89.6 us -> 86.7 us
  local copies, waits for them, and re-layouts: 6.77 us -> 4.25 us
    unnamed x15 -> x10, local copies, waits for them, and re-layouts: 6.42 us -> 1.85 us
    all_gather x2, blocking collectives: 44.6 us -> 41.5 us  [gathered(): return lax.all_gather(shard, axis, axis=0, tiled=False)]
    all_to_all x2, waiting for transfers between devices: 4.12 us -> 7.12 us  [over(): return lax.all_to_all(shard, axes, split_axis=0, concat_axis=0, tiled=True)]
    another operation x0 -> x1, local copies, waits for them, and re-layouts: none -> 2.41 us  [body(): flat = [w[0, 0].reshape(block_rows, half) for w in (w_gate, w_up)]]
    ppermute x3, waiting for transfers between devices: 8.07 us -> 9.86 us  [swapped(): return lax.ppermute(shard, axis, [(0, 1), (1, 0)])]
    pallas_call x12 -> x11, Pallas kernels: 6.46 us -> 6.61 us  [call(): pl.pallas_call(kernel, out_shape=outs, in_specs=[SMEM] * len(scalars) + [...]
where the time goes in v10:
time: 156 us
  blocking collectives  86.7 us (56%)
  starting transfers between devices  41.2 us (26%)
  waiting for transfers between devices  17 us (11%)
  Pallas kernels  6.61 us (4%)
  local copies, waits for them, and re-layouts  4.25 us (3%)
    all_to_all x2, blocking collectives, over(): return lax.all_to_all(shard, axes, split_axis=0, concat_axis=0, tiled=True)  45.2 us
    all_gather x2, blocking collectives, gathered(): return lax.all_gather(shard, axis, axis=0, tiled=False)  41.5 us
    all_to_all x2, starting transfers between devices, over(): return lax.all_to_all(shard, axes, split_axis=0, concat_axis=0, tiled=True)  25.4 us
    ppermute x3, starting transfers between devices, swapped(): return lax.ppermute(shard, axis, [(0, 1), (1, 0)])  15.8 us
    ppermute x3, waiting for transfers between devices, swapped(): return lax.ppermute(shard, axis, [(0, 1), (1, 0)])  9.86 us
    all_to_all x2, waiting for transfers between devices, over(): return lax.all_to_all(shard, axes, split_axis=0, concat_axis=0, tiled=True)  7.12 us
    pallas_call x11, Pallas kernels, call(): pl.pallas_call(kernel, out_shape=outs, in_specs=[SMEM] * len(scalars) + [...  6.61 us
  transfers between devices with their start and end apart: 5, of which 3 were waited for; matrix products, arithmetic and copies ran while one was open for 2% of the time, Pallas kernels for 1%

profile of v10, /device:TPU:1, one launch (start us, length us, event | category | flops | bytes accessed | tf_op | source)
XLA Modules:
  0.0 155.9 jit_solution(12778827939070372685)
XLA Ops:
  0.0 0.0 copy-start.3
  0.0 0.7 copy-done.3
  0.7 0.7 shard_map.55
  1.4 16.3 %all-to-all-start = ((bf16[8,16,192]{2,1,0:T(8,128)(2,1)}), bf16[8,16,192]{2,1,0:T(8,128)(2,1)S(1)}, u32[]{:S(2)}, u32[]{:S(2)}) async-start(bf16[8,16,192]{2,1,0:T(8,128)(2,1)} %shard_map.55), calls=%async_computation | async-start | bytes 131072 | tf_op jit(solution)/shard_map/all_to_all | solution.py:41
  17.7 2.4 %copy_bitcast_fusion = (bf16[1536,512]{1,0:T(8,128)(2,1)S(1)}, bf16[1536,512]{1,0:T(8,128)(2,1)S(1)}) fusion(bf16[192,8,4,128]{3,2,1,0:T(4,128)(2,1)} %bitcast.23, bf16[192,8,4,128]{3,2,1,0:T(4,128)(2,1)} %bitcast.24), kind=kLoop, calls=%fused_computation | loop fusion | bytes 6291456 | tf_op jit(solution)/shard_map/reshape;squeeze | solution.py:204
  20.1 0.0 copy-start.4
  20.1 0.0 copy-start.2
  20.1 0.2 shard_map.56
  20.3 7.1 %all-to-all-done.raw_ref = bf16[8,16,192]{2,1,0:T(8,128)(2,1)S(1)} async-done(((bf16[8,16,192]{2,1,0:T(8,128)(2,1)}), bf16[8,16,192]{2,1,0:T(8,128)(2,1)S(1)}, u32[]{:S(2)}, u32[]{:S(2)}) %all-to-all-start) | async-done | bytes 49184 | tf_op jit(solution)/shard_map/all_to_all | solution.py:41
  27.4 0.0 copy-done.4
  27.4 1.0 shard_map.57
  28.4 9.2 %all-to-all-start.1 = ((bf16[8,32,384]{2,1,0:T(8,128)(2,1)}), bf16[8,32,384]{2,1,0:T(8,128)(2,1)S(1)}, u32[]{:S(2)}, u32[]{:S(2)}) async-start(bf16[8,32,384]{2,1,0:T(8,128)(2,1)} %bitcast.5), calls=%async_computation.1 | async-start | bytes 393216 | tf_op jit(solution)/shard_map/all_to_all | solution.py:41
  37.6 0.0 copy-done.2
  37.6 11.6 %collective-permute-start = (bf16[256,128]{1,0:T(8,128)(2,1)S(1)}, bf16[256,128]{1,0:T(8,128)(2,1)S(1)}, u32[]{:S(2)}, u32[]{:S(2)}) collective-permute-start(bf16[256,128]{1,0:T(8,128)(2,1)S(1)} %bitcast.18), channel_id=1, source_target_pairs={{0,32},{32,0},{1,33},{33,1},{2,34},{34,2},{3,35},{35,3},{4,36},{36... | collective-permute-start | bytes 196616 | tf_op jit(solution)/shard_map/ppermute | solution.py:37
  49.2 0.0 all-to-all-done.1
  49.2 12.0 %all_gather.13.rows_ref = bf16[4,256,384]{2,1,0:T(8,128)(2,1)S(1)} all-gather(bf16[1,256,384]{2,1,0:T(8,128)(2,1)S(1)} %bitcast.25), channel_id=1, replica_groups=mesh['expert'=8,'y'=2,'zh'=2,'k'=4,'z0'=2,'x'=4] {'x'}, dimensions={0}, use_global_device_ids=true | all-gather | bytes 983040 | tf_op jit(solution)/shard_map/all_gather | solution.py:45
  61.2 0.0 copy-start
  61.2 0.0 collective-permute-done.far_ref
  61.2 1.3 shard_map.59
  62.5 0.0 copy-done
  62.5 2.3 %collective-permute-start.1 = (bf16[256,512]{1,0:T(8,128)(2,1)}, bf16[256,512]{1,0:T(8,128)(2,1)S(1)}, u32[]{:S(2)}, u32[]{:S(2)}) collective-permute-start(bf16[256,512]{1,0:T(8,128)(2,1)} %shard_map.59), channel_id=1, source_target_pairs={{0,64},{64,0},{1,65},{65,1},{2,66},{66,2},{3,67},{67,3},{4,68},{68... | collective-permute-start | bytes 786440 | tf_op jit(solution)/shard_map/ppermute | solution.py:37
  64.8 0.0 copy-start.1
  64.8 1.1 copy-done.1
  66.0 0.6 shard_map.58.keep_ref
  66.5 3.6 %collective-permute-done.1.near_ref = bf16[256,512]{1,0:T(8,128)(2,1)S(1)} collective-permute-done((bf16[256,512]{1,0:T(8,128)(2,1)}, bf16[256,512]{1,0:T(8,128)(2,1)S(1)}, u32[]{:S(2)}, u32[]{:S(2)}) %collective-permute-start.1) | collective-permute-done | bytes 262176 | tf_op jit(solution)/shard_map/ppermute | solution.py:37
  70.2 29.6 %all-gather = bf16[512,512]{1,0:T(8,128)(2,1)S(1)} all-gather(bf16[256,512]{1,0:T(8,128)(2,1)S(1)} %shard_map.60), channel_id=2, replica_groups=mesh['expert'=8,'y'=2,'zh'=2,'k'=4,'z0'=2,'x'=4] {'zh'}, dimensions={0}, use_global_device_ids=true | all-gather | bytes 786432 | tf_op jit(solution)/shard_map/all_gather | solution.py:45
  99.7 0.2 shard_map.61.grad_ref
  99.9 1.9 %collective-permute-start.2 = (bf16[256,512]{1,0:T(8,128)(2,1)S(1)}, bf16[256,512]{1,0:T(8,128)(2,1)S(1)}, u32[]{:S(2)}, u32[]{:S(2)}) collective-permute-start(bf16[256,512]{1,0:T(8,128)(2,1)S(1)} %shard_map.61.grad_ref), channel_id=1, source_target_pairs={{0,64},{64,0},{1,65},{65,1},{2,66},{66,2},{3,67},{67,3},{4,68},{68... | collective-permute-start | bytes 786440 | tf_op jit(solution)/shard_map/ppermute | solution.py:37
  101.9 0.7 shard_map.62.held_ref
  102.6 6.3 %collective-permute-done.2.grad_ref = bf16[256,512]{1,0:T(8,128)(2,1)S(1)} collective-permute-done((bf16[256,512]{1,0:T(8,128)(2,1)S(1)}, bf16[256,512]{1,0:T(8,128)(2,1)S(1)}, u32[]{:S(2)}, u32[]{:S(2)}) %collective-permute-start.2) | collective-permute-done | bytes 262176 | tf_op jit(solution)/shard_map/ppermute | solution.py:37
  108.9 0.8 shard_map.63
  109.7 18.5 %all_to_all.24.pieces_ref = bf16[8,128,384]{2,1,0:T(8,128)(2,1)S(1)} all-to-all(bf16[8,128,384]{2,1,0:T(8,128)(2,1)S(1)} %shard_map.63), channel_id=1, replica_groups=mesh['expert'=8,'y'=2,'zh'=2,'k'=4,'z0'=2,'x'=4] {'z0','x'}, dimensions={0} | all-to-all | bytes 1572864 | tf_op jit(solution)/shard_map/all_to_all | solution.py:41
  128.1 0.2 shard_map.64
  128.3 26.7 %all_to_all.25.back_ref = bf16[32,16,96]{2,1,0:T(8,128)(2,1)S(1)} all-to-all(bf16[32,16,96]{2,1,0:T(8,128)(2,1)S(1)} %shard_map.64), channel_id=1, replica_groups=mesh['expert'=8,'y'=2,'zh'=2,'k'=4,'z0'=2,'x'=4] {'expert','k'}, dimensions={0} | all-to-all | bytes 196608 | tf_op jit(solution)/shard_map/all_to_all | solution.py:41
  155.0 0.9 shard_map.65
  (1 shorter events, 0.0 us)
Async XLA Ops:
  0.0 0.7 copy-start.3
  1.4 26.0 %all-to-all-start = ((bf16[8,16,192]{2,1,0:T(8,128)(2,1)}), bf16[8,16,192]{2,1,0:T(8,128)(2,1)S(1)}, u32[]{:S(2)}, u32[]{:S(2)}) async-start(bf16[8,16,192]{2,1,0:T(8,128)(2,1)} %shard_map.55), calls=%async_computation | async-start | bytes 131072 | tf_op jit(solution)/shard_map/all_to_all | solution.py:41
  20.1 7.4 %copy-start.4 = (s32[64,2]{0,1:T(2,128)S(1)}, s32[64,2]{0,1:T(2,128)}, u32[]{:S(2)}) copy-start(s32[64,2]{0,1:T(2,128)} %param.6) | copy-start | bytes 1540
  20.1 17.5 %copy-start.2 = (bf16[1,256,128]{2,1,0:T(8,128)(2,1)S(1)}, bf16[1,256,128]{2,1,0:T(8,128)(2,1)}, u32[]{:S(2)}) copy-start(bf16[1,256,128]{2,1,0:T(8,128)(2,1)} %param.9) | copy-start | bytes 196612
  28.4 20.8 %all-to-all-start.1 = ((bf16[8,32,384]{2,1,0:T(8,128)(2,1)}), bf16[8,32,384]{2,1,0:T(8,128)(2,1)S(1)}, u32[]{:S(2)}, u32[]{:S(2)}) async-start(bf16[8,32,384]{2,1,0:T(8,128)(2,1)} %bitcast.5), calls=%async_computation.1 | async-start | bytes 393216 | tf_op jit(solution)/shard_map/all_to_all | solution.py:41
  37.6 23.6 %collective-permute-start = (bf16[256,128]{1,0:T(8,128)(2,1)S(1)}, bf16[256,128]{1,0:T(8,128)(2,1)S(1)}, u32[]{:S(2)}, u32[]{:S(2)}) collective-permute-start(bf16[256,128]{1,0:T(8,128)(2,1)S(1)} %bitcast.18), channel_id=1, source_target_pairs={{0,32},{32,0},{1,33},{33,1},{2,34},{34,2},{3,35},{35,3},{4,36},{36... | collective-permute-start | bytes 196616 | tf_op jit(solution)/shard_map/ppermute | solution.py:37
  61.2 1.3 copy-start
  62.5 7.6 %collective-permute-start.1 = (bf16[256,512]{1,0:T(8,128)(2,1)}, bf16[256,512]{1,0:T(8,128)(2,1)S(1)}, u32[]{:S(2)}, u32[]{:S(2)}) collective-permute-start(bf16[256,512]{1,0:T(8,128)(2,1)} %shard_map.59), channel_id=1, source_target_pairs={{0,64},{64,0},{1,65},{65,1},{2,66},{66,2},{3,67},{67,3},{4,68},{68... | collective-permute-start | bytes 786440 | tf_op jit(solution)/shard_map/ppermute | solution.py:37
  64.8 1.1 copy-start.1
  99.9 8.9 %collective-permute-start.2 = (bf16[256,512]{1,0:T(8,128)(2,1)S(1)}, bf16[256,512]{1,0:T(8,128)(2,1)S(1)}, u32[]{:S(2)}, u32[]{:S(2)}) collective-permute-start(bf16[256,512]{1,0:T(8,128)(2,1)S(1)} %shard_map.61.grad_ref), channel_id=1, source_target_pairs={{0,64},{64,0},{1,65},{65,1},{2,66},{66,2},{3,67},{67,3},{4,68},{68... | collective-permute-start | bytes 786440 | tf_op jit(solution)/shard_map/ppermute | solution.py:37

commit v11 on v10

--- a/solution.py
+++ b/solution.py
@@ -47,14 +47,6 @@
 
 def dot(a, b, dims=(((1,), (0,)), ((), ()))):
     return lax.dot_general(a, b, dims, preferred_element_type=F32)
-
-
-def pack_kernel(tok_ref, out_ref):
-    turned = tok_ref[...]
-    third = turned.shape[0] // 3
-    packed = jnp.concatenate([turned[j * third : (j + 1) * third] for j in range(3)], axis=1)
-    for z in range(out_ref.shape[0]):
-        out_ref[z] = packed
 
 
 def arrange_kernel(gate_ref, up_ref, gate_out_ref, up_out_ref):
@@ -86,14 +78,30 @@
     return jnp.where((slots == taken[0]) | (slots == taken[1]), 1.0, 0.0).astype(BF16)
 
 
-def dispatch_kernel(routes_ref, raw_ref, out_ref):
-    n_tok = routes_ref.shape[1]
-    pieces = [
-        raw_ref[z, :, j * n_tok : (j + 1) * n_tok] for z in ORDER for j in range(3)
+def packed_rows(n_tok, half):
+    row = lax.broadcasted_iota(jnp.int32, (TILE, n_tok), 0)
+    return jnp.right_shift(row, 4) * (2 * FEW) + half * FEW + jnp.bitwise_and(row, FEW - 1)
+
+
+def dispatch_kernel(routes_ref, tok_ref, out_ref):
+    taken = slots_of(routes_ref)
+    tokens = tok_ref[...]
+    part = [dot(one_hot(taken, packed_rows(tokens.shape[1], h)), tokens, NT) for h in range(2)]
+    part = jnp.concatenate(part, axis=1).astype(BF16)
+    for e in range(TILE // FEW):
+        for k in range(NK):
+            out_ref[e * NK + k] = part[e * FEW : (e + 1) * FEW]
+
+
+def copies_kernel(in_ref, out_ref):
+    feat = in_ref.shape[2] // 2
+    blocks = [
+        jnp.concatenate([in_ref[e * NK + k] for e in range(TILE // FEW)], axis=0) for k in range(NK)
     ]
-    raw = jnp.concatenate(pieces, axis=0)
-    slots = lax.broadcasted_iota(jnp.int32, (out_ref.shape[0], n_tok), 0)
-    out_ref[...] = dot(one_hot(slots_of(routes_ref), slots), raw, NT).astype(BF16)
+    lanes = [block[:, h * feat : (h + 1) * feat] for h in range(2) for block in blocks]
+    rows = jnp.concatenate(lanes, axis=1)
+    for m in range(out_ref.shape[0]):
+        out_ref[m] = rows
 
 
 def halves(y_ref, width):
@@ -105,20 +113,31 @@
 def forward_kernel(y_ref, rows_ref, gate_ref, up_ref, out_ref, *, mine):
     width = gate_ref.shape[1] // 2
     at = halves(y_ref, width)[0 if mine else 1]
-    rows = jnp.concatenate([rows_ref[x] for x in range(rows_ref.shape[0])], axis=1)
+    wide = rows_ref.shape[2] // 2
+    members = [z0 * NX + x for x in range(NX) for z0 in range(2)]
+    rows = [
+        jnp.concatenate([rows_ref[m, :, h * wide : (h + 1) * wide] for m in members], axis=1)
+        for h in range(2)
+    ]
+    rows = jnp.concatenate(rows, axis=0)
     for m, w_ref in enumerate((gate_ref, up_ref)):
         out_ref[:, m * width : (m + 1) * width] = dot(rows, w_ref[:, at]).astype(out_ref.dtype)
 
 
 def near_kernel(keep_ref, near_ref, send_ref):
     send_ref[...] = (keep_ref[...] + near_ref[...].astype(F32)).astype(BF16)
+
+
+def slot_order(ref):
+    starts = [(2 * source + h) * FEW for h in range(2) for source in range(TILE // FEW)]
+    return jnp.concatenate([ref[v : v + FEW] for v in starts], axis=0).astype(F32)
 
 
 def grad_kernel(zh_ref, keep_ref, near_ref, both_ref, hid_ref, far_ref, out_ref):
     width = keep_ref.shape[1]
     hid = width // 4
     total = keep_ref[...] + near_ref[...].astype(F32) + both_ref[1 - zh_ref[0]].astype(F32)
-    own, far = hid_ref[...].astype(F32), far_ref[...].astype(F32)
+    own, far = slot_order(hid_ref), slot_order(far_ref)
     for j in range(2):
         upstream = jnp.where(zh_ref[0] == j, own, far)
         gate_pre = total[:, j * hid : (j + 1) * hid]
@@ -147,10 +166,7 @@
     for x in range(NX):
         total = held_ref[x] + backward(y_ref, grad_ref, gate_ref, up_ref, x, False)
         total = total.astype(BF16)
-        part = []
-        for h in range(2):
-            starts = [(2 * e + h) * FEW for e in range(TILE // FEW)]
-            part.append(jnp.concatenate([total[v : v + FEW] for v in starts], axis=0))
+        part = [total[h * TILE : (h + 1) * TILE] for h in range(2)]
         for z0 in range(2):
             at = slice(z0 * wide, (z0 + 1) * wide)
             out_ref[z0 * NX + x] = jnp.concatenate([part[0][:, at], part[1][:, at]], axis=1)
@@ -170,11 +186,6 @@
             out_ref[e * NK + k] = part[e * FEW : (e + 1) * FEW]
 
 
-def returned_rows(n_tok, half):
-    row = lax.broadcasted_iota(jnp.int32, (TILE, n_tok), 0)
-    return jnp.right_shift(row, 4) * (2 * FEW) + half * FEW + jnp.bitwise_and(row, FEW - 1)
-
-
 def finish_kernel(routes_ref, back_ref, out_ref):
     feat, n_tok = out_ref.shape
     taken = slots_of(routes_ref)
@@ -185,7 +196,7 @@
             total = total + back_ref[e * NK + k].astype(F32)
         slots.append(total.astype(BF16))
     slots = jnp.concatenate(slots, axis=0)
-    part = [dot(slots, one_hot(taken, returned_rows(n_tok, h)), TN) for h in range(2)]
+    part = [dot(slots, one_hot(taken, packed_rows(n_tok, h)), TN) for h in range(2)]
     out_ref[...] = (part[0][:feat] + part[1][feat:]).astype(BF16)
 
 
@@ -197,22 +208,22 @@
     n_tok, feat = tokens.shape
     block_rows = w_gate.shape[2]
     hid = w_gate.shape[4]
-    wide = NZL * feat
+    wide = 2 * NK * feat
     shape = jax.ShapeDtypeStruct
 
     half = 4 * hid
     flat = [w[0, 0].reshape(block_rows, half) for w in (w_gate, w_up)]
     gate, up = call(arrange_kernel, [shape((block_rows, half), BF16)] * 2, [], flat, mib=16)
 
-    packed = call(pack_kernel, shape((NZL, feat // 3, 3 * n_tok), BF16), [], [tokens.T])
-    raw = over(("k", "z0"), packed)
-
-    raw, gate, up, hidden = lax.optimization_barrier((raw, gate, up, hidden_grad[0]))
-    outgoing = call(dispatch_kernel, shape((slot_total, wide), BF16), [], [routes.T, raw])
-    arrived = over("expert", outgoing)
+    sent = call(
+        dispatch_kernel, shape((n_groups * NK, FEW, 2 * feat), BF16), [], [routes.T, tokens.T]
+    )
+    gate, up, hidden = lax.optimization_barrier((gate, up, hidden_grad[0]))
+    arrived = over(("expert", "k"), sent)
     hidden_far = swapped(hidden, "zh")
-    rows = gathered("x", arrived)
-    rows, hidden_far = lax.optimization_barrier((rows, hidden_far))
+    arrived, gate, up, hidden_far = lax.optimization_barrier((arrived, gate, up, hidden_far))
+    copies = call(copies_kernel, shape((2 * NX, TILE, wide), BF16), [], [arrived])
+    rows = over(("z0", "x"), copies)
 
     n_flops = 2 * slot_total * block_rows * half
     given = [rows, gate, up]

time: 156 us -> 166 us (1.064)
  waiting for transfers between devices: 17 us -> 19.3 us
  starting transfers between devices: 41.2 us -> 43.4 us
  blocking collectives: 86.7 us -> 88.8 us
  Pallas kernels: 6.61 us -> 8.41 us
    all_to_all x2, blocking collectives: 45.2 us -> 74.2 us  [over(): return lax.all_to_all(shard, axes, split_axis=0, concat_axis=0, tiled=True)]
    all_gather x2 -> x1, blocking collectives: 41.5 us -> 14.6 us  [gathered(): return lax.all_gather(shard, axis, axis=0, tiled=False)]
    all_to_all x2, waiting for transfers between devices: 7.12 us -> 9.66 us  [over(): return lax.all_to_all(shard, axes, split_axis=0, concat_axis=0, tiled=True)]
    pallas_call x11, Pallas kernels: 6.61 us -> 8.41 us  [call(): pl.pallas_call(kernel, out_shape=outs, in_specs=[SMEM] * len(scalars) + [...]
  transfers between devices with their start and end apart: 5 -> 5, of which waited for: 3 -> 4; matrix products, arithmetic and copies ran while one was open for 2% -> 1% of each run, Pallas kernels for 1% -> 2%
where the time goes in v11:
time: 166 us; the launch traced here: 165 us
  blocking collectives  88.8 us (53%)
  starting transfers between devices  43.4 us (26%)
  waiting for transfers between devices  19.3 us (12%)
  Pallas kernels  8.41 us (5%)
  local copies, waits for them, and re-layouts  5.33 us (3%)
    all_to_all x2, blocking collectives, over(): return lax.all_to_all(shard, axes, split_axis=0, concat_axis=0, tiled=True)  74.2 us
    all_to_all x2, starting transfers between devices, over(): return lax.all_to_all(shard, axes, split_axis=0, concat_axis=0, tiled=True)  26.3 us
    ppermute x3, starting transfers between devices, swapped(): return lax.ppermute(shard, axis, [(0, 1), (1, 0)])  17 us
    all_gather x1, blocking collectives, gathered(): return lax.all_gather(shard, axis, axis=0, tiled=False)  14.6 us
    ppermute x3, waiting for transfers between devices, swapped(): return lax.ppermute(shard, axis, [(0, 1), (1, 0)])  9.67 us
    all_to_all x2, waiting for transfers between devices, over(): return lax.all_to_all(shard, axes, split_axis=0, concat_axis=0, tiled=True)  9.66 us
    pallas_call x11, Pallas kernels, call(): pl.pallas_call(kernel, out_shape=outs, in_specs=[SMEM] * len(scalars) + [...  8.41 us
  transfers between devices with their start and end apart: 5, of which 4 were waited for; matrix products, arithmetic and copies ran while one was open for 1% of the time, Pallas kernels for 2%

profile of v11, /device:TPU:1, one launch (start us, length us, event | category | flops | bytes accessed | tf_op | source)
XLA Modules:
  0.0 165.4 jit_solution(17170425081612257827)
XLA Ops:
  0.0 0.0 copy-start.2
  0.0 0.7 copy-done.2
  0.7 0.0 copy-start.3
  0.7 0.7 copy-done.3
  1.4 1.0 shard_map.55
  2.4 20.8 %all-to-all-start = ((bf16[32,16,96]{2,1,0:T(8,128)(2,1)}), bf16[32,16,96]{2,1,0:T(8,128)(2,1)S(1)}, u32[]{:S(2)}, u32[]{:S(2)}) async-start(bf16[32,16,96]{2,1,0:T(8,128)(2,1)} %shard_map.55), calls=%async_computation | async-start | bytes 262144 | tf_op jit(solution)/shard_map/all_to_all | solution.py:41
  23.2 2.4 %copy_bitcast_fusion = (bf16[1536,512]{1,0:T(8,128)(2,1)S(1)}, bf16[1536,512]{1,0:T(8,128)(2,1)S(1)}) fusion(bf16[192,8,4,128]{3,2,1,0:T(4,128)(2,1)} %bitcast.21, bf16[192,8,4,128]{3,2,1,0:T(4,128)(2,1)} %bitcast.22), kind=kLoop, calls=%fused_computation | loop fusion | bytes 6291456 | tf_op jit(solution)/shard_map/reshape;squeeze | solution.py:215
  25.6 0.0 copy-start.1
  25.6 0.2 shard_map.56
  25.8 0.6 copy-done.1
  26.5 12.5 %collective-permute-start = (bf16[256,128]{1,0:T(8,128)(2,1)S(1)}, bf16[256,128]{1,0:T(8,128)(2,1)S(1)}, u32[]{:S(2)}, u32[]{:S(2)}) collective-permute-start(bf16[256,128]{1,0:T(8,128)(2,1)S(1)} %bitcast.16), channel_id=1, source_target_pairs={{0,32},{32,0},{1,33},{33,1},{2,34},{34,2},{3,35},{35,3},{4,36},{36... | collective-permute-start | bytes 196616 | tf_op jit(solution)/shard_map/ppermute | solution.py:37
  38.9 2.3 %collective-permute-done.far_ref = bf16[256,128]{1,0:T(8,128)(2,1)S(1)} collective-permute-done((bf16[256,128]{1,0:T(8,128)(2,1)S(1)}, bf16[256,128]{1,0:T(8,128)(2,1)S(1)}, u32[]{:S(2)}, u32[]{:S(2)}) %collective-permute-start) | collective-permute-done | bytes 65568 | tf_op jit(solution)/shard_map/ppermute | solution.py:37
  41.2 0.0 all-to-all-done.in_ref
  41.2 0.2 shard_map.57
  41.4 0.0 copy-start
  41.4 0.9 copy-done
  42.3 5.5 %all-to-all-start.1 = ((bf16[8,128,384]{2,1,0:T(8,128)(2,1)}), bf16[8,128,384]{2,1,0:T(8,128)(2,1)}, u32[]{:S(2)}, u32[]{:S(2)}) async-start(bf16[8,128,384]{2,1,0:T(8,128)(2,1)} %copy-done), calls=%async_computation.1 | async-start | bytes 1572864 | tf_op jit(solution)/shard_map/all_to_all | solution.py:41
  47.9 9.7 %all-to-all-done.1.rows_ref = bf16[8,128,384]{2,1,0:T(8,128)(2,1)} async-done(((bf16[8,128,384]{2,1,0:T(8,128)(2,1)}), bf16[8,128,384]{2,1,0:T(8,128)(2,1)}, u32[]{:S(2)}, u32[]{:S(2)}) %all-to-all-start.1) | async-done | bytes 786464 | tf_op jit(solution)/shard_map/all_to_all | solution.py:41
  57.5 2.5 %shard_map.59 = bf16[256,512]{1,0:T(8,128)(2,1)} custom-call(s32[1]{0:T(128)} %bitcast.1.y_ref, bf16[8,128,384]{2,1,0:T(8,128)(2,1)} %all-to-all-done.1.rows_ref, bf16[1536,512]{1,0:T(8,128)(2,1)S(1)} %get-tuple-element.20.gate_ref, bf16[1536,512]{1,0:T(8,128)(2,1)S(1)} %get-tuple-element.21.up_ref), custom_call_target="tpu_custom_call" | custom-call | flops 402653184 | bytes 4194304 | tf_op jit(solution)/shard_map/pallas_call | solution.py:26
  60.0 2.3 %collective-permute-start.1 = (bf16[256,512]{1,0:T(8,128)(2,1)}, bf16[256,512]{1,0:T(8,128)(2,1)S(1)}, u32[]{:S(2)}, u32[]{:S(2)}) collective-permute-start(bf16[256,512]{1,0:T(8,128)(2,1)} %shard_map.59), channel_id=1, source_target_pairs={{0,64},{64,0},{1,65},{65,1},{2,66},{66,2},{3,67},{67,3},{4,68},{68... | collective-permute-start | bytes 786440 | tf_op jit(solution)/shard_map/ppermute | solution.py:37
  62.3 1.7 %shard_map.58.keep_ref = f32[256,512]{1,0:T(8,128)S(1)} custom-call(s32[1]{0:T(128)} %bitcast.1.y_ref, bf16[8,128,384]{2,1,0:T(8,128)(2,1)} %all-to-all-done.1.rows_ref, bf16[1536,512]{1,0:T(8,128)(2,1)S(1)} %get-tuple-element.20.gate_ref, bf16[1536,512]{1,0:T(8,128)(2,1)S(1)} %get-tuple-element.21.up_ref), custom_call_target="tpu_custom_call" | custom-call | flops 402653184 | bytes 4456448 | tf_op jit(solution)/shard_map/pallas_call | solution.py:26
  64.0 3.3 %collective-permute-done.1.near_ref = bf16[256,512]{1,0:T(8,128)(2,1)S(1)} collective-permute-done((bf16[256,512]{1,0:T(8,128)(2,1)}, bf16[256,512]{1,0:T(8,128)(2,1)S(1)}, u32[]{:S(2)}, u32[]{:S(2)}) %collective-permute-start.1) | collective-permute-done | bytes 262176 | tf_op jit(solution)/shard_map/ppermute | solution.py:37
  67.4 14.6 %all-gather = bf16[512,512]{1,0:T(8,128)(2,1)S(1)} all-gather(bf16[256,512]{1,0:T(8,128)(2,1)S(1)} %shard_map.60), channel_id=2, replica_groups=mesh['expert'=8,'y'=2,'zh'=2,'k'=4,'z0'=2,'x'=4] {'zh'}, dimensions={0}, use_global_device_ids=true | all-gather | bytes 786432 | tf_op jit(solution)/shard_map/all_gather | solution.py:45
  82.0 0.2 shard_map.61.grad_ref
  82.2 2.3 %collective-permute-start.2 = (bf16[256,512]{1,0:T(8,128)(2,1)S(1)}, bf16[256,512]{1,0:T(8,128)(2,1)S(1)}, u32[]{:S(2)}, u32[]{:S(2)}) collective-permute-start(bf16[256,512]{1,0:T(8,128)(2,1)S(1)} %shard_map.61.grad_ref), channel_id=1, source_target_pairs={{0,64},{64,0},{1,65},{65,1},{2,66},{66,2},{3,67},{67,3},{4,68},{68... | collective-permute-start | bytes 786440 | tf_op jit(solution)/shard_map/ppermute | solution.py:37
  84.5 0.7 shard_map.62.held_ref
  85.2 4.1 %collective-permute-done.2.grad_ref = bf16[256,512]{1,0:T(8,128)(2,1)S(1)} collective-permute-done((bf16[256,512]{1,0:T(8,128)(2,1)S(1)}, bf16[256,512]{1,0:T(8,128)(2,1)S(1)}, u32[]{:S(2)}, u32[]{:S(2)}) %collective-permute-start.2) | collective-permute-done | bytes 262176 | tf_op jit(solution)/shard_map/ppermute | solution.py:37
  89.3 0.8 shard_map.63
  90.1 0.0 copy-start.4
  90.1 23.6 %all_to_all.20.pieces_ref = bf16[8,128,384]{2,1,0:T(8,128)(2,1)S(1)} all-to-all(bf16[8,128,384]{2,1,0:T(8,128)(2,1)S(1)} %shard_map.63), channel_id=1, replica_groups=mesh['expert'=8,'y'=2,'zh'=2,'k'=4,'z0'=2,'x'=4] {'z0','x'}, dimensions={0} | all-to-all | bytes 1572864 | tf_op jit(solution)/shard_map/all_to_all | solution.py:41
  113.7 0.2 shard_map.64
  113.9 50.7 %all_to_all.21.back_ref = bf16[32,16,96]{2,1,0:T(8,128)(2,1)S(1)} all-to-all(bf16[32,16,96]{2,1,0:T(8,128)(2,1)S(1)} %shard_map.64), channel_id=1, replica_groups=mesh['expert'=8,'y'=2,'zh'=2,'k'=4,'z0'=2,'x'=4] {'expert','k'}, dimensions={0} | all-to-all | bytes 196608 | tf_op jit(solution)/shard_map/all_to_all | solution.py:41
  164.6 0.0 copy-done.4
  164.6 0.9 shard_map.65
  (1 shorter events, 0.0 us)
Async XLA Ops:
  0.0 0.7 copy-start.2
  0.7 0.7 copy-start.3
  2.4 38.9 %all-to-all-start = ((bf16[32,16,96]{2,1,0:T(8,128)(2,1)}), bf16[32,16,96]{2,1,0:T(8,128)(2,1)S(1)}, u32[]{:S(2)}, u32[]{:S(2)}) async-start(bf16[32,16,96]{2,1,0:T(8,128)(2,1)} %shard_map.55), calls=%async_computation | async-start | bytes 262144 | tf_op jit(solution)/shard_map/all_to_all | solution.py:41
  25.6 0.8 copy-start.1
  26.5 14.8 %collective-permute-start = (bf16[256,128]{1,0:T(8,128)(2,1)S(1)}, bf16[256,128]{1,0:T(8,128)(2,1)S(1)}, u32[]{:S(2)}, u32[]{:S(2)}) collective-permute-start(bf16[256,128]{1,0:T(8,128)(2,1)S(1)} %bitcast.16), channel_id=1, source_target_pairs={{0,32},{32,0},{1,33},{33,1},{2,34},{34,2},{3,35},{35,3},{4,36},{36... | collective-permute-start | bytes 196616 | tf_op jit(solution)/shard_map/ppermute | solution.py:37
  41.4 0.9 copy-start
  42.3 15.2 %all-to-all-start.1 = ((bf16[8,128,384]{2,1,0:T(8,128)(2,1)}), bf16[8,128,384]{2,1,0:T(8,128)(2,1)}, u32[]{:S(2)}, u32[]{:S(2)}) async-start(bf16[8,128,384]{2,1,0:T(8,128)(2,1)} %copy-done), calls=%async_computation.1 | async-start | bytes 1572864 | tf_op jit(solution)/shard_map/all_to_all | solution.py:41
  60.0 7.3 %collective-permute-start.1 = (bf16[256,512]{1,0:T(8,128)(2,1)}, bf16[256,512]{1,0:T(8,128)(2,1)S(1)}, u32[]{:S(2)}, u32[]{:S(2)}) collective-permute-start(bf16[256,512]{1,0:T(8,128)(2,1)} %shard_map.59), channel_id=1, source_target_pairs={{0,64},{64,0},{1,65},{65,1},{2,66},{66,2},{3,67},{67,3},{4,68},{68... | collective-permute-start | bytes 786440 | tf_op jit(solution)/shard_map/ppermute | solution.py:37
  82.2 7.1 %collective-permute-start.2 = (bf16[256,512]{1,0:T(8,128)(2,1)S(1)}, bf16[256,512]{1,0:T(8,128)(2,1)S(1)}, u32[]{:S(2)}, u32[]{:S(2)}) collective-permute-start(bf16[256,512]{1,0:T(8,128)(2,1)S(1)} %shard_map.61.grad_ref), channel_id=1, source_target_pairs={{0,64},{64,0},{1,65},{65,1},{2,66},{66,2},{3,67},{67,3},{4,68},{68... | collective-permute-start | bytes 786440 | tf_op jit(solution)/shard_map/ppermute | solution.py:37
  90.1 74.5 %copy-start.4 = (s32[64,2]{0,1:T(2,128)S(1)}, s32[64,2]{0,1:T(2,128)}, u32[]{:S(2)}) copy-start(s32[64,2]{0,1:T(2,128)} %param.6) | copy-start | bytes 1540

commit v12 on v10

--- a/solution.py
+++ b/solution.py
@@ -183,9 +183,14 @@
         total = back_ref[e * NK].astype(F32)
         for k in range(1, NK):
             total = total + back_ref[e * NK + k].astype(F32)
-        slots.append(total.astype(BF16))
+        slots.append(total)
     slots = jnp.concatenate(slots, axis=0)
-    part = [dot(slots, one_hot(taken, returned_rows(n_tok, h)), TN) for h in range(2)]
+    high = slots.astype(BF16)
+    low = (slots - high.astype(F32)).astype(BF16)
+    part = []
+    for h in range(2):
+        placing = one_hot(taken, returned_rows(n_tok, h))
+        part.append(dot(high, placing, TN) + dot(low, placing, TN))
     out_ref[...] = (part[0][:feat] + part[1][feat:]).astype(BF16)
 
 

time: 156 us -> 156 us (level)
  no operation moved by 1% of the time
where the time goes in v12:
time: 156 us
  blocking collectives  86.7 us (56%)
  starting transfers between devices  41.2 us (26%)
  waiting for transfers between devices  17 us (11%)
  Pallas kernels  6.64 us (4%)
  local copies, waits for them, and re-layouts  4.25 us (3%)
    all_to_all x2, blocking collectives, over(): return lax.all_to_all(shard, axes, split_axis=0, concat_axis=0, tiled=True)  45.2 us
    all_gather x2, blocking collectives, gathered(): return lax.all_gather(shard, axis, axis=0, tiled=False)  41.5 us
    all_to_all x2, starting transfers between devices, over(): return lax.all_to_all(shard, axes, split_axis=0, concat_axis=0, tiled=True)  25.4 us
    ppermute x3, starting transfers between devices, swapped(): return lax.ppermute(shard, axis, [(0, 1), (1, 0)])  15.8 us
    ppermute x3, waiting for transfers between devices, swapped(): return lax.ppermute(shard, axis, [(0, 1), (1, 0)])  9.86 us
    all_to_all x2, waiting for transfers between devices, over(): return lax.all_to_all(shard, axes, split_axis=0, concat_axis=0, tiled=True)  7.12 us
    pallas_call x11, Pallas kernels, call(): pl.pallas_call(kernel, out_shape=outs, in_specs=[SMEM] * len(scalars) + [...  6.64 us
  transfers between devices with their start and end apart: 5, of which 3 were waited for; matrix products, arithmetic and copies ran while one was open for 2% of the time, Pallas kernels for 1%

profile of v12, /device:TPU:1, one launch (start us, length us, event | category | flops | bytes accessed | tf_op | source)
XLA Modules:
  0.0 155.9 jit_solution(11129942226570338150)
XLA Ops:
  0.0 0.0 copy-start.3
  0.0 0.7 copy-done.3
  0.7 0.7 shard_map.55
  1.4 16.3 %all-to-all-start = ((bf16[8,16,192]{2,1,0:T(8,128)(2,1)}), bf16[8,16,192]{2,1,0:T(8,128)(2,1)S(1)}, u32[]{:S(2)}, u32[]{:S(2)}) async-start(bf16[8,16,192]{2,1,0:T(8,128)(2,1)} %shard_map.55), calls=%async_computation | async-start | bytes 131072 | tf_op jit(solution)/shard_map/all_to_all | solution.py:41
  17.7 2.4 %copy_bitcast_fusion = (bf16[1536,512]{1,0:T(8,128)(2,1)S(1)}, bf16[1536,512]{1,0:T(8,128)(2,1)S(1)}) fusion(bf16[192,8,4,128]{3,2,1,0:T(4,128)(2,1)} %bitcast.23, bf16[192,8,4,128]{3,2,1,0:T(4,128)(2,1)} %bitcast.24), kind=kLoop, calls=%fused_computation | loop fusion | bytes 6291456 | tf_op jit(solution)/shard_map/reshape;squeeze | solution.py:209
  20.1 0.0 copy-start.4
  20.1 0.0 copy-start.2
  20.1 0.2 shard_map.56
  20.3 7.1 %all-to-all-done.raw_ref = bf16[8,16,192]{2,1,0:T(8,128)(2,1)S(1)} async-done(((bf16[8,16,192]{2,1,0:T(8,128)(2,1)}), bf16[8,16,192]{2,1,0:T(8,128)(2,1)S(1)}, u32[]{:S(2)}, u32[]{:S(2)}) %all-to-all-start) | async-done | bytes 49184 | tf_op jit(solution)/shard_map/all_to_all | solution.py:41
  27.4 0.0 copy-done.4
  27.4 1.0 shard_map.57
  28.4 9.2 %all-to-all-start.1 = ((bf16[8,32,384]{2,1,0:T(8,128)(2,1)}), bf16[8,32,384]{2,1,0:T(8,128)(2,1)S(1)}, u32[]{:S(2)}, u32[]{:S(2)}) async-start(bf16[8,32,384]{2,1,0:T(8,128)(2,1)} %bitcast.5), calls=%async_computation.1 | async-start | bytes 393216 | tf_op jit(solution)/shard_map/all_to_all | solution.py:41
  37.6 0.0 copy-done.2
  37.6 11.6 %collective-permute-start = (bf16[256,128]{1,0:T(8,128)(2,1)S(1)}, bf16[256,128]{1,0:T(8,128)(2,1)S(1)}, u32[]{:S(2)}, u32[]{:S(2)}) collective-permute-start(bf16[256,128]{1,0:T(8,128)(2,1)S(1)} %bitcast.18), channel_id=1, source_target_pairs={{0,32},{32,0},{1,33},{33,1},{2,34},{34,2},{3,35},{35,3},{4,36},{36... | collective-permute-start | bytes 196616 | tf_op jit(solution)/shard_map/ppermute | solution.py:37
  49.2 0.0 all-to-all-done.1
  49.2 12.0 %all_gather.13.rows_ref = bf16[4,256,384]{2,1,0:T(8,128)(2,1)S(1)} all-gather(bf16[1,256,384]{2,1,0:T(8,128)(2,1)S(1)} %bitcast.25), channel_id=1, replica_groups=mesh['expert'=8,'y'=2,'zh'=2,'k'=4,'z0'=2,'x'=4] {'x'}, dimensions={0}, use_global_device_ids=true | all-gather | bytes 983040 | tf_op jit(solution)/shard_map/all_gather | solution.py:45
  61.2 0.0 copy-start
  61.2 0.0 collective-permute-done.far_ref
  61.2 1.3 shard_map.59
  62.5 0.0 copy-done
  62.5 2.3 %collective-permute-start.1 = (bf16[256,512]{1,0:T(8,128)(2,1)}, bf16[256,512]{1,0:T(8,128)(2,1)S(1)}, u32[]{:S(2)}, u32[]{:S(2)}) collective-permute-start(bf16[256,512]{1,0:T(8,128)(2,1)} %shard_map.59), channel_id=1, source_target_pairs={{0,64},{64,0},{1,65},{65,1},{2,66},{66,2},{3,67},{67,3},{4,68},{68... | collective-permute-start | bytes 786440 | tf_op jit(solution)/shard_map/ppermute | solution.py:37
  64.8 0.0 copy-start.1
  64.8 1.1 copy-done.1
  66.0 0.6 shard_map.58.keep_ref
  66.5 3.6 %collective-permute-done.1.near_ref = bf16[256,512]{1,0:T(8,128)(2,1)S(1)} collective-permute-done((bf16[256,512]{1,0:T(8,128)(2,1)}, bf16[256,512]{1,0:T(8,128)(2,1)S(1)}, u32[]{:S(2)}, u32[]{:S(2)}) %collective-permute-start.1) | collective-permute-done | bytes 262176 | tf_op jit(solution)/shard_map/ppermute | solution.py:37
  70.2 29.6 %all-gather = bf16[512,512]{1,0:T(8,128)(2,1)S(1)} all-gather(bf16[256,512]{1,0:T(8,128)(2,1)S(1)} %shard_map.60), channel_id=2, replica_groups=mesh['expert'=8,'y'=2,'zh'=2,'k'=4,'z0'=2,'x'=4] {'zh'}, dimensions={0}, use_global_device_ids=true | all-gather | bytes 786432 | tf_op jit(solution)/shard_map/all_gather | solution.py:45
  99.7 0.2 shard_map.61.grad_ref
  99.9 1.9 %collective-permute-start.2 = (bf16[256,512]{1,0:T(8,128)(2,1)S(1)}, bf16[256,512]{1,0:T(8,128)(2,1)S(1)}, u32[]{:S(2)}, u32[]{:S(2)}) collective-permute-start(bf16[256,512]{1,0:T(8,128)(2,1)S(1)} %shard_map.61.grad_ref), channel_id=1, source_target_pairs={{0,64},{64,0},{1,65},{65,1},{2,66},{66,2},{3,67},{67,3},{4,68},{68... | collective-permute-start | bytes 786440 | tf_op jit(solution)/shard_map/ppermute | solution.py:37
  101.9 0.7 shard_map.62.held_ref
  102.6 6.3 %collective-permute-done.2.grad_ref = bf16[256,512]{1,0:T(8,128)(2,1)S(1)} collective-permute-done((bf16[256,512]{1,0:T(8,128)(2,1)S(1)}, bf16[256,512]{1,0:T(8,128)(2,1)S(1)}, u32[]{:S(2)}, u32[]{:S(2)}) %collective-permute-start.2) | collective-permute-done | bytes 262176 | tf_op jit(solution)/shard_map/ppermute | solution.py:37
  108.9 0.8 shard_map.63
  109.7 18.5 %all_to_all.24.pieces_ref = bf16[8,128,384]{2,1,0:T(8,128)(2,1)S(1)} all-to-all(bf16[8,128,384]{2,1,0:T(8,128)(2,1)S(1)} %shard_map.63), channel_id=1, replica_groups=mesh['expert'=8,'y'=2,'zh'=2,'k'=4,'z0'=2,'x'=4] {'z0','x'}, dimensions={0} | all-to-all | bytes 1572864 | tf_op jit(solution)/shard_map/all_to_all | solution.py:41
  128.1 0.2 shard_map.64
  128.3 26.7 %all_to_all.25.back_ref = bf16[32,16,96]{2,1,0:T(8,128)(2,1)S(1)} all-to-all(bf16[32,16,96]{2,1,0:T(8,128)(2,1)S(1)} %shard_map.64), channel_id=1, replica_groups=mesh['expert'=8,'y'=2,'zh'=2,'k'=4,'z0'=2,'x'=4] {'expert','k'}, dimensions={0} | all-to-all | bytes 196608 | tf_op jit(solution)/shard_map/all_to_all | solution.py:41
  155.0 0.9 shard_map.65
  (1 shorter events, 0.0 us)
Async XLA Ops:
  0.0 0.7 copy-start.3
  1.4 26.0 %all-to-all-start = ((bf16[8,16,192]{2,1,0:T(8,128)(2,1)}), bf16[8,16,192]{2,1,0:T(8,128)(2,1)S(1)}, u32[]{:S(2)}, u32[]{:S(2)}) async-start(bf16[8,16,192]{2,1,0:T(8,128)(2,1)} %shard_map.55), calls=%async_computation | async-start | bytes 131072 | tf_op jit(solution)/shard_map/all_to_all | solution.py:41
  20.1 7.4 %copy-start.4 = (s32[64,2]{0,1:T(2,128)S(1)}, s32[64,2]{0,1:T(2,128)}, u32[]{:S(2)}) copy-start(s32[64,2]{0,1:T(2,128)} %param.6) | copy-start | bytes 1540
  20.1 17.5 %copy-start.2 = (bf16[1,256,128]{2,1,0:T(8,128)(2,1)S(1)}, bf16[1,256,128]{2,1,0:T(8,128)(2,1)}, u32[]{:S(2)}) copy-start(bf16[1,256,128]{2,1,0:T(8,128)(2,1)} %param.9) | copy-start | bytes 196612
  28.4 20.8 %all-to-all-start.1 = ((bf16[8,32,384]{2,1,0:T(8,128)(2,1)}), bf16[8,32,384]{2,1,0:T(8,128)(2,1)S(1)}, u32[]{:S(2)}, u32[]{:S(2)}) async-start(bf16[8,32,384]{2,1,0:T(8,128)(2,1)} %bitcast.5), calls=%async_computation.1 | async-start | bytes 393216 | tf_op jit(solution)/shard_map/all_to_all | solution.py:41
  37.6 23.6 %collective-permute-start = (bf16[256,128]{1,0:T(8,128)(2,1)S(1)}, bf16[256,128]{1,0:T(8,128)(2,1)S(1)}, u32[]{:S(2)}, u32[]{:S(2)}) collective-permute-start(bf16[256,128]{1,0:T(8,128)(2,1)S(1)} %bitcast.18), channel_id=1, source_target_pairs={{0,32},{32,0},{1,33},{33,1},{2,34},{34,2},{3,35},{35,3},{4,36},{36... | collective-permute-start | bytes 196616 | tf_op jit(solution)/shard_map/ppermute | solution.py:37
  61.2 1.3 copy-start
  62.5 7.6 %collective-permute-start.1 = (bf16[256,512]{1,0:T(8,128)(2,1)}, bf16[256,512]{1,0:T(8,128)(2,1)S(1)}, u32[]{:S(2)}, u32[]{:S(2)}) collective-permute-start(bf16[256,512]{1,0:T(8,128)(2,1)} %shard_map.59), channel_id=1, source_target_pairs={{0,64},{64,0},{1,65},{65,1},{2,66},{66,2},{3,67},{67,3},{4,68},{68... | collective-permute-start | bytes 786440 | tf_op jit(solution)/shard_map/ppermute | solution.py:37
  64.8 1.1 copy-start.1
  99.9 8.9 %collective-permute-start.2 = (bf16[256,512]{1,0:T(8,128)(2,1)S(1)}, bf16[256,512]{1,0:T(8,128)(2,1)S(1)}, u32[]{:S(2)}, u32[]{:S(2)}) collective-permute-start(bf16[256,512]{1,0:T(8,128)(2,1)S(1)} %shard_map.61.grad_ref), channel_id=1, source_target_pairs={{0,64},{64,0},{1,65},{65,1},{2,66},{66,2},{3,67},{67,3},{4,68},{68... | collective-permute-start | bytes 786440 | tf_op jit(solution)/shard_map/ppermute | solution.py:37

commit v13 on v12

--- a/solution.py
+++ b/solution.py
@@ -49,8 +49,11 @@
     return lax.dot_general(a, b, dims, preferred_element_type=F32)
 
 
-def pack_kernel(tok_ref, out_ref):
-    turned = tok_ref[...]
+def pack_kernel(tok_ref, out_ref, held_ref, done):
+    fetch = pltpu.make_async_copy(tok_ref, held_ref, done)
+    fetch.start()
+    fetch.wait()
+    turned = held_ref[...]
     third = turned.shape[0] // 3
     packed = jnp.concatenate([turned[j * third : (j + 1) * third] for j in range(3)], axis=1)
     for z in range(out_ref.shape[0]):
@@ -209,7 +212,14 @@
     flat = [w[0, 0].reshape(block_rows, half) for w in (w_gate, w_up)]
     gate, up = call(arrange_kernel, [shape((block_rows, half), BF16)] * 2, [], flat, mib=16)
 
-    packed = call(pack_kernel, shape((NZL, feat // 3, 3 * n_tok), BF16), [], [tokens.T])
+    packed = pl.pallas_call(
+        pack_kernel,
+        out_shape=shape((NZL, feat // 3, 3 * n_tok), BF16),
+        in_specs=[pl.BlockSpec(memory_space=pl.ANY)],
+        out_specs=VMEM,
+        scratch_shapes=[pltpu.VMEM((feat, n_tok), BF16), pltpu.SemaphoreType.DMA],
+        compiler_params=pltpu.CompilerParams(vmem_limit_bytes=56 * 1024 * 1024),
+    )(tokens.T)
     raw = over(("k", "z0"), packed)
 
     raw, gate, up, hidden = lax.optimization_barrier((raw, gate, up, hidden_grad[0]))

time: 156 us -> 157 us (level)
  starting transfers between devices: 41.2 us -> 44.1 us
  blocking collectives: 86.7 us -> 85 us
    ppermute x3, starting transfers between devices: 15.8 us -> 18.6 us  [swapped(): return lax.ppermute(shard, axis, [(0, 1), (1, 0)])]
    all_to_all x2, blocking collectives: 45.2 us -> 43.5 us  [over(): return lax.all_to_all(shard, axes, split_axis=0, concat_axis=0, tiled=True)]
    pallas_call x11 -> x10, Pallas kernels: 6.64 us -> 5.95 us  [call(): pl.pallas_call(kernel, out_shape=outs, in_specs=[SMEM] * len(scalars) + [...]
where the time goes in v13:
time: 157 us; the launch traced here: 156 us
  blocking collectives  85 us (54%)
  starting transfers between devices  44.1 us (28%)
  waiting for transfers between devices  15.8 us (10%)
  Pallas kernels  7.37 us (5%)
  local copies, waits for them, and re-layouts  3.55 us (2%)
    all_to_all x2, blocking collectives, over(): return lax.all_to_all(shard, axes, split_axis=0, concat_axis=0, tiled=True)  43.5 us
    all_gather x2, blocking collectives, gathered(): return lax.all_gather(shard, axis, axis=0, tiled=False)  41.5 us
    all_to_all x2, starting transfers between devices, over(): return lax.all_to_all(shard, axes, split_axis=0, concat_axis=0, tiled=True)  25.5 us
    ppermute x3, starting transfers between devices, swapped(): return lax.ppermute(shard, axis, [(0, 1), (1, 0)])  18.6 us
    ppermute x3, waiting for transfers between devices, swapped(): return lax.ppermute(shard, axis, [(0, 1), (1, 0)])  8.68 us
    all_to_all x2, waiting for transfers between devices, over(): return lax.all_to_all(shard, axes, split_axis=0, concat_axis=0, tiled=True)  7.12 us
    pallas_call x10, Pallas kernels, call(): pl.pallas_call(kernel, out_shape=outs, in_specs=[SMEM] * len(scalars) + [...  5.95 us
  transfers between devices with their start and end apart: 5, of which 3 were waited for; matrix products, arithmetic and copies ran while one was open for 2% of the time, Pallas kernels for 1%

profile of v13, /device:TPU:1, one launch (start us, length us, event | category | flops | bytes accessed | tf_op | source)
XLA Modules:
  0.0 156.0 jit_solution(18297834500657395995)
XLA Ops:
  0.0 1.4 shard_map.55
  1.4 16.3 %all-to-all-start = ((bf16[8,16,192]{2,1,0:T(8,128)(2,1)}), bf16[8,16,192]{2,1,0:T(8,128)(2,1)S(1)}, u32[]{:S(2)}, u32[]{:S(2)}) async-start(bf16[8,16,192]{2,1,0:T(8,128)(2,1)} %shard_map.55), calls=%async_computation | async-start | bytes 131072 | tf_op jit(solution)/shard_map/all_to_all | solution.py:41
  17.7 2.4 %copy_bitcast_fusion = (bf16[1536,512]{1,0:T(8,128)(2,1)S(1)}, bf16[1536,512]{1,0:T(8,128)(2,1)S(1)}) fusion(bf16[192,8,4,128]{3,2,1,0:T(4,128)(2,1)} %bitcast.22, bf16[192,8,4,128]{3,2,1,0:T(4,128)(2,1)} %bitcast.23), kind=kLoop, calls=%fused_computation | loop fusion | bytes 6291456 | tf_op jit(solution)/shard_map/reshape;squeeze | solution.py:212
  20.1 0.0 copy-start.3
  20.1 0.0 copy-start.2
  20.1 0.2 shard_map.56
  20.3 7.1 %all-to-all-done.raw_ref = bf16[8,16,192]{2,1,0:T(8,128)(2,1)S(1)} async-done(((bf16[8,16,192]{2,1,0:T(8,128)(2,1)}), bf16[8,16,192]{2,1,0:T(8,128)(2,1)S(1)}, u32[]{:S(2)}, u32[]{:S(2)}) %all-to-all-start) | async-done | bytes 49184 | tf_op jit(solution)/shard_map/all_to_all | solution.py:41
  27.5 0.0 copy-done.3
  27.5 1.0 shard_map.57
  28.5 9.2 %all-to-all-start.1 = ((bf16[8,32,384]{2,1,0:T(8,128)(2,1)}), bf16[8,32,384]{2,1,0:T(8,128)(2,1)S(1)}, u32[]{:S(2)}, u32[]{:S(2)}) async-start(bf16[8,32,384]{2,1,0:T(8,128)(2,1)} %bitcast.5), calls=%async_computation.1 | async-start | bytes 393216 | tf_op jit(solution)/shard_map/all_to_all | solution.py:41
  37.7 0.0 copy-done.2
  37.7 11.6 %collective-permute-start = (bf16[256,128]{1,0:T(8,128)(2,1)S(1)}, bf16[256,128]{1,0:T(8,128)(2,1)S(1)}, u32[]{:S(2)}, u32[]{:S(2)}) collective-permute-start(bf16[256,128]{1,0:T(8,128)(2,1)S(1)} %bitcast.18), channel_id=1, source_target_pairs={{0,32},{32,0},{1,33},{33,1},{2,34},{34,2},{3,35},{35,3},{4,36},{36... | collective-permute-start | bytes 196616 | tf_op jit(solution)/shard_map/ppermute | solution.py:37
  49.2 0.0 all-to-all-done.1
  49.2 12.0 %all_gather.13.rows_ref = bf16[4,256,384]{2,1,0:T(8,128)(2,1)S(1)} all-gather(bf16[1,256,384]{2,1,0:T(8,128)(2,1)S(1)} %bitcast.24), channel_id=1, replica_groups=mesh['expert'=8,'y'=2,'zh'=2,'k'=4,'z0'=2,'x'=4] {'x'}, dimensions={0}, use_global_device_ids=true | all-gather | bytes 983040 | tf_op jit(solution)/shard_map/all_gather | solution.py:45
  61.2 0.0 copy-start
  61.2 0.0 collective-permute-done.far_ref
  61.2 1.3 shard_map.59
  62.5 0.0 copy-done
  62.5 2.3 %collective-permute-start.1 = (bf16[256,512]{1,0:T(8,128)(2,1)}, bf16[256,512]{1,0:T(8,128)(2,1)S(1)}, u32[]{:S(2)}, u32[]{:S(2)}) collective-permute-start(bf16[256,512]{1,0:T(8,128)(2,1)} %shard_map.59), channel_id=1, source_target_pairs={{0,64},{64,0},{1,65},{65,1},{2,66},{66,2},{3,67},{67,3},{4,68},{68... | collective-permute-start | bytes 786440 | tf_op jit(solution)/shard_map/ppermute | solution.py:37
  64.8 0.0 copy-start.1
  64.9 1.1 copy-done.1
  66.0 0.6 shard_map.58.keep_ref
  66.6 3.6 %collective-permute-done.1.near_ref = bf16[256,512]{1,0:T(8,128)(2,1)S(1)} collective-permute-done((bf16[256,512]{1,0:T(8,128)(2,1)}, bf16[256,512]{1,0:T(8,128)(2,1)S(1)}, u32[]{:S(2)}, u32[]{:S(2)}) %collective-permute-start.1) | collective-permute-done | bytes 262176 | tf_op jit(solution)/shard_map/ppermute | solution.py:37
  70.2 29.6 %all-gather = bf16[512,512]{1,0:T(8,128)(2,1)S(1)} all-gather(bf16[256,512]{1,0:T(8,128)(2,1)S(1)} %shard_map.60), channel_id=2, replica_groups=mesh['expert'=8,'y'=2,'zh'=2,'k'=4,'z0'=2,'x'=4] {'zh'}, dimensions={0}, use_global_device_ids=true | all-gather | bytes 786432 | tf_op jit(solution)/shard_map/all_gather | solution.py:45
  99.8 0.2 shard_map.61.grad_ref
  100.0 4.8 %collective-permute-start.2 = (bf16[256,512]{1,0:T(8,128)(2,1)S(1)}, bf16[256,512]{1,0:T(8,128)(2,1)S(1)}, u32[]{:S(2)}, u32[]{:S(2)}) collective-permute-start(bf16[256,512]{1,0:T(8,128)(2,1)S(1)} %shard_map.61.grad_ref), channel_id=1, source_target_pairs={{0,64},{64,0},{1,65},{65,1},{2,66},{66,2},{3,67},{67,3},{4,68},{68... | collective-permute-start | bytes 786440 | tf_op jit(solution)/shard_map/ppermute | solution.py:37
  104.8 0.7 shard_map.62.held_ref
  105.5 5.1 %collective-permute-done.2.grad_ref = bf16[256,512]{1,0:T(8,128)(2,1)S(1)} collective-permute-done((bf16[256,512]{1,0:T(8,128)(2,1)S(1)}, bf16[256,512]{1,0:T(8,128)(2,1)S(1)}, u32[]{:S(2)}, u32[]{:S(2)}) %collective-permute-start.2) | collective-permute-done | bytes 262176 | tf_op jit(solution)/shard_map/ppermute | solution.py:37
  110.6 0.8 shard_map.63
  111.4 16.8 %all_to_all.24.pieces_ref = bf16[8,128,384]{2,1,0:T(8,128)(2,1)S(1)} all-to-all(bf16[8,128,384]{2,1,0:T(8,128)(2,1)S(1)} %shard_map.63), channel_id=1, replica_groups=mesh['expert'=8,'y'=2,'zh'=2,'k'=4,'z0'=2,'x'=4] {'z0','x'}, dimensions={0} | all-to-all | bytes 1572864 | tf_op jit(solution)/shard_map/all_to_all | solution.py:41
  128.2 0.2 shard_map.64
  128.4 26.7 %all_to_all.25.back_ref = bf16[32,16,96]{2,1,0:T(8,128)(2,1)S(1)} all-to-all(bf16[32,16,96]{2,1,0:T(8,128)(2,1)S(1)} %shard_map.64), channel_id=1, replica_groups=mesh['expert'=8,'y'=2,'zh'=2,'k'=4,'z0'=2,'x'=4] {'expert','k'}, dimensions={0} | all-to-all | bytes 196608 | tf_op jit(solution)/shard_map/all_to_all | solution.py:41
  155.1 0.9 shard_map.65
  (1 shorter events, 0.0 us)
Async XLA Ops:
  1.4 26.0 %all-to-all-start = ((bf16[8,16,192]{2,1,0:T(8,128)(2,1)}), bf16[8,16,192]{2,1,0:T(8,128)(2,1)S(1)}, u32[]{:S(2)}, u32[]{:S(2)}) async-start(bf16[8,16,192]{2,1,0:T(8,128)(2,1)} %shard_map.55), calls=%async_computation | async-start | bytes 131072 | tf_op jit(solution)/shard_map/all_to_all | solution.py:41
  20.1 7.4 %copy-start.3 = (s32[64,2]{0,1:T(2,128)S(1)}, s32[64,2]{0,1:T(2,128)}, u32[]{:S(2)}) copy-start(s32[64,2]{0,1:T(2,128)} %param.6) | copy-start | bytes 1540
  20.1 17.5 %copy-start.2 = (bf16[1,256,128]{2,1,0:T(8,128)(2,1)S(1)}, bf16[1,256,128]{2,1,0:T(8,128)(2,1)}, u32[]{:S(2)}) copy-start(bf16[1,256,128]{2,1,0:T(8,128)(2,1)} %param.9) | copy-start | bytes 196612
  28.5 20.8 %all-to-all-start.1 = ((bf16[8,32,384]{2,1,0:T(8,128)(2,1)}), bf16[8,32,384]{2,1,0:T(8,128)(2,1)S(1)}, u32[]{:S(2)}, u32[]{:S(2)}) async-start(bf16[8,32,384]{2,1,0:T(8,128)(2,1)} %bitcast.5), calls=%async_computation.1 | async-start | bytes 393216 | tf_op jit(solution)/shard_map/all_to_all | solution.py:41
  37.7 23.6 %collective-permute-start = (bf16[256,128]{1,0:T(8,128)(2,1)S(1)}, bf16[256,128]{1,0:T(8,128)(2,1)S(1)}, u32[]{:S(2)}, u32[]{:S(2)}) collective-permute-start(bf16[256,128]{1,0:T(8,128)(2,1)S(1)} %bitcast.18), channel_id=1, source_target_pairs={{0,32},{32,0},{1,33},{33,1},{2,34},{34,2},{3,35},{35,3},{4,36},{36... | collective-permute-start | bytes 196616 | tf_op jit(solution)/shard_map/ppermute | solution.py:37
  61.2 1.3 copy-start
  62.5 7.6 %collective-permute-start.1 = (bf16[256,512]{1,0:T(8,128)(2,1)}, bf16[256,512]{1,0:T(8,128)(2,1)S(1)}, u32[]{:S(2)}, u32[]{:S(2)}) collective-permute-start(bf16[256,512]{1,0:T(8,128)(2,1)} %shard_map.59), channel_id=1, source_target_pairs={{0,64},{64,0},{1,65},{65,1},{2,66},{66,2},{3,67},{67,3},{4,68},{68... | collective-permute-start | bytes 786440 | tf_op jit(solution)/shard_map/ppermute | solution.py:37
  64.8 1.1 copy-start.1
  100.0 10.6 %collective-permute-start.2 = (bf16[256,512]{1,0:T(8,128)(2,1)S(1)}, bf16[256,512]{1,0:T(8,128)(2,1)S(1)}, u32[]{:S(2)}, u32[]{:S(2)}) collective-permute-start(bf16[256,512]{1,0:T(8,128)(2,1)S(1)} %shard_map.61.grad_ref), channel_id=1, source_target_pairs={{0,64},{64,0},{1,65},{65,1},{2,66},{66,2},{3,67},{67,3},{4,68},{68... | collective-permute-start | bytes 786440 | tf_op jit(solution)/shard_map/ppermute | solution.py:37
